TPU v7x, 256 devices: a whole 4x4x8 slice. The times are simulated.
256 devices in a mesh: basis: 8 (over z_lo, core), orb: 16 (over y, x), rep: 2 (over z_hi).
Axes of the slice: x: 4, y: 4, z: 8 (z_hi: 2, z_lo: 4; z = z_hi * 4 + z_lo), core: 2. Of those that a mesh axis runs over, the one named last changes fastest.
Arguments:
- coefficients: float32 [16, 8192, 512], P('orb', ('basis', 'rep')), may hold values from -6 to 6
- basis_metric: bfloat16 [65536, 128], P('orb'), as said below
- pattern: int32 [1024], P('orb'), may hold values 0 or 1
- starts: int32 [128], P('orb'), may hold values from 0 to 928, as said below
Outputs:
- coefficients_out: float32 [16, 8192, 512], P('orb', ('basis', 'rep'))
Inputs may be any that keep to these rules, and one draw needn't show every extreme that they name: Orbital block j lies in group g = floor(j * 64 / 512); starts[j] is the smaller of 928 and a block between g * 64 and g * 64 + 2 * 64 - 96. `basis_metric`: the first 64 columns of each block's rows form a symmetric block with unit diagonal.
All inputs are finite; a program needn't handle non-finite values. No bound on the sum of `pattern` on one device may be relied on, other than what follows from the above.
Results may differ from a plain program's by a relative error of at most 0.0003.
Values may be sent and summed in bfloat16 or wider, within the bound.
A program may use at most 64 MiB of HBM per device.

v0:
```python
import jax
import jax.numpy as jnp
from jax import lax
from jax.sharding import PartitionSpec as P

BLK = 64
GROUP_BLOCKS = 64
SUPPORT = 96
ITERS = 2


HIGH = lax.Precision.HIGHEST


def passed_along(block, axis, distance):
    devices = range(lax.axis_size(axis))
    route = [(i - distance, i) for i in devices if i - distance in devices]
    return lax.ppermute(block, axis, route)


def extended(block, sides, width):
    for axis, dim in sides:
        count = lax.axis_size(axis)
        forward = [(i, i + 1) for i in range(count - 1)]
        backward = [(target, source) for source, target in forward]
        low = lax.ppermute(
            lax.slice_in_dim(block, block.shape[dim] - width, None, axis=dim), axis, forward
        )
        high = lax.ppermute(lax.slice_in_dim(block, 0, width, axis=dim), axis, backward)
        block = jnp.concatenate([low, block, high], axis=dim)
    return block


def from_partner(value, axis, apart):
    mask = 2**apart
    pairs = [(source, source ^ mask) for source in range(lax.axis_size(axis))]
    return lax.ppermute(value, axis, pairs)


def per_device(coefficients, basis_metric, pattern, starts):
    tile_rows = coefficients.shape[1]
    orb_cols = coefficients.shape[2]
    place_count = lax.axis_size(("basis", "rep"))
    position = lax.axis_index(("basis", "rep"))
    group_index = lax.axis_index("orb")
    group_count = lax.axis_size("orb")
    total_blocks = GROUP_BLOCKS * group_count
    low_half = position < place_count // 2
    top_bit = lax.axis_size("basis").bit_length() - 2
    block_ids = group_index * GROUP_BLOCKS + jnp.arange(GROUP_BLOCKS, dtype=jnp.int32)
    keep_flag = (pattern * (block_ids < total_blocks - 1).astype(jnp.int32)).astype(jnp.bfloat16)
    effective = jnp.concatenate(
        [basis_metric[:, :BLK], basis_metric[:, BLK:] * jnp.repeat(keep_flag, BLK)[:, None]], axis=1
    )
    following = passed_along(effective, "orb", -1)
    window = jnp.concatenate(
        [jnp.zeros((BLK, 2 * BLK), jnp.bfloat16), effective, following], axis=0
    )
    my_rows = lax.dynamic_slice_in_dim(window, position * tile_rows, tile_rows + BLK, 0)
    my_rows = my_rows.astype(jnp.float32).reshape(tile_rows // BLK + 1, BLK, 2 * BLK)
    diag_blocks = my_rows[1:, :, :BLK]
    up_blocks = my_rows[1:, :, BLK:]
    prev_blocks = my_rows[:-1, :, BLK:]
    row_blocks = (
        group_index * GROUP_BLOCKS
        + (position * tile_rows + jnp.arange(tile_rows, dtype=jnp.int32)) // BLK
    )
    column_starts = jnp.repeat(starts, BLK)
    inside = (row_blocks[:, None] >= column_starts[None, :]) & (
        row_blocks[:, None] < column_starts[None, :] + SUPPORT
    )
    mask_live = inside.astype(jnp.float32)
    norm_scale = 1.0 / (SUPPORT * BLK)
    identity = jnp.eye(orb_cols, dtype=jnp.float32)
    zero_block = jnp.zeros((orb_cols, orb_cols), jnp.float32)
    coeff_now = coefficients[0] * mask_live
    for sweep_index in range(ITERS):
        padded = extended(coeff_now, ((("basis", "rep"), 0),), BLK)
        shaped = padded.reshape(tile_rows // BLK + 2, BLK, orb_cols)
        applied = jnp.einsum("wij,wjo->wio", diag_blocks, shaped[1:-1], precision=HIGH)
        applied = applied + jnp.einsum("wij,wjo->wio", up_blocks, shaped[2:], precision=HIGH)
        applied = applied + jnp.einsum("wji,wjo->wio", prev_blocks, shaped[:-2], precision=HIGH)
        applied = applied.reshape(tile_rows, orb_cols)
        payload = jnp.stack([coeff_now, applied])
        partner = from_partner(payload, "basis", top_bit)
        beside = extended(partner[:, None], (("orb", 1),), 1)
        gathered = jnp.where(low_half, beside[:, 0], beside[:, 2])
        neighbour = gathered[0]
        self_part = jnp.einsum("ro,rp->op", coeff_now, applied, precision=HIGH)
        neighbour_image = gathered[1]
        side_part = lax.cond(
            low_half,
            lambda: jnp.einsum("ro,rp->op", coeff_now, neighbour_image, precision=HIGH),
            lambda: jnp.einsum("ro,rp->op", applied, neighbour, precision=HIGH),
        )
        low_part = jnp.where(low_half, side_part, zero_block)
        high_part = jnp.where(low_half, zero_block, side_part)
        gram_self, gram_low, gram_high = lax.psum(
            (self_part, low_part, high_part), ("basis", "rep")
        )
        side_gram = jnp.where(low_half, gram_low, gram_high) * norm_scale
        self_step = (3.0 * identity - gram_self * norm_scale) * 0.5
        cross_step = -0.5 * side_gram.T
        updated = jnp.dot(coeff_now, self_step, precision=HIGH) + jnp.dot(
            neighbour, cross_step, precision=HIGH
        )
        coeff_now = updated * mask_live
    return coeff_now[None]


def solution(mesh):
    in_specs = (P("orb", ("basis", "rep"), None), P("orb", None), P("orb"), P("orb"))
    out_specs = P("orb", ("basis", "rep"), None)
    return jax.shard_map(
        per_device, mesh=mesh, in_specs=in_specs, out_specs=out_specs, check_vma=False
    )
```

profile of v0, /device:TPU:25, one launch (start us, length us, event | category | flops | bytes accessed | tf_op | source)
XLA Modules:
  0.0 627.1 jit_solution(6744699506872997897)
XLA Ops:
  6.5 0.7 fusion.59
  7.4 2.5 fusion.73
  9.9 0.9 copy-done.5
  10.8 1.6 pad_maximum_fusion.6
  12.4 4.6 collective-permute-start
  17.4 9.7 %collective-permute-start.1 = (f32[64,512]{1,0:T(8,128)S(1)}, f32[64,512]{1,0:T(8,128)S(1)}, u32[]{:S(2)}, u32[]{:S(2)}) collective-permute-start(f32[64,512]{1,0:T(8,128)S(1)} %get-tuple-element.61), channel_id=1, source_target_pairs={{1,0},{32,1},{33,32},{64,33},{65,64},{96,65},{97,96},{128,97},{129... | collective-permute-start | bytes 393224 | tf_op jit(solution)/shard_map/ppermute | solution.py:29
  27.1 1.9 collective-permute-start.2
  29.4 9.3 %collective-permute-done.2 = f32[64,512]{1,0:T(8,128)} collective-permute-done((f32[64,512]{1,0:T(8,128)S(1)}, f32[64,512]{1,0:T(8,128)}, u32[]{:S(2)}, u32[]{:S(2)}) %collective-permute-start.2) | collective-permute-done | bytes 131104 | tf_op jit(solution)/shard_map/ppermute | solution.py:26
  38.7 1.1 pad_maximum_fusion.5
  39.9 0.5 fusion.41
  40.4 0.7 fusion.46
  41.1 0.8 fusion.19
  41.9 0.8 convolution_add_fusion.3
  43.0 3.1 collective-permute-start.3
  46.1 89.7 %collective-permute-done.3 = f32[2,512,512]{2,1,0:T(8,128)} collective-permute-done((f32[2,512,512]{2,1,0:T(8,128)S(1)}, f32[2,512,512]{2,1,0:T(8,128)}, u32[]{:S(2)}, u32[]{:S(2)}) %collective-permute-start.3) | collective-permute-done | bytes 2097184 | tf_op jit(solution)/shard_map/ppermute | solution.py:37
  135.8 2.7 collective-permute-start.4
  138.5 5.5 collective-permute-start.5
  144.0 4.0 fusion.11
  148.0 38.3 %collective-permute-done.4 = f32[2,1,512,512]{3,2,0,1:T(8,128)} collective-permute-done((f32[2,1,512,512]{3,2,0,1:T(8,128)}, f32[2,1,512,512]{3,2,0,1:T(8,128)}, u32[]{:S(2)}, u32[]{:S(2)}) %collective-permute-start.4) | collective-permute-done | bytes 2097184 | tf_op jit(solution)/shard_map/ppermute | solution.py:26
  186.3 0.9 collective-permute-done.5
  187.2 2.1 broadcast_select_fusion.1
  189.4 1.3 copy-done.2
  190.7 1.9 conditional.2
  190.7 1.9 fusion
  192.5 1.6 broadcast_select_fusion.4
  194.3 123.7 %all-reduce.7.cloned.1.call-done = (f32[512,512]{1,0:T(8,128)}, f32[512,512]{1,0:T(8,128)}, f32[512,512]{1,0:T(8,128)}) async-done(((f32[512,512]{1,0:T(8,128)}, f32[512,512]{1,0:T(8,128)}, f32[512,512]{1,0:T(8,128)}), (f32[512,512]{1,0:T(8,128)}, f32[512,512]{1,0:T(8,128)}, f32[512,512]{1,0:T(8,128)})) %all-reduce.7.cloned.1.call-update) | async-done | bytes 3145744 | tf_op jit(solution)/shard_map/psum | solution.py:98
  317.9 3.3 fusion.6
  321.2 2.0 fusion.4
  323.3 7.2 %collective-permute-start.6 = (f32[64,512]{1,0:T(8,128)S(1)}, f32[64,512]{1,0:T(8,128)S(1)}, u32[]{:S(2)}, u32[]{:S(2)}) collective-permute-start(f32[64,512]{1,0:T(8,128)S(1)} %get-tuple-element.55), channel_id=1, source_target_pairs={{1,0},{32,1},{33,32},{64,33},{65,64},{96,65},{97,96},{128,97},{129... | collective-permute-start | bytes 393224 | tf_op jit(solution)/shard_map/ppermute | solution.py:29
  330.5 2.0 collective-permute-start.7
  332.5 0.6 fusion.48
  333.1 5.4 collective-permute-done.6
  338.5 3.4 collective-permute-done.7
  342.2 0.7 fusion.44
  342.9 0.8 convolution_add_fusion.1
  344.0 91.6 %collective-permute-done.8 = f32[2,512,512]{2,1,0:T(8,128)S(1)} collective-permute-done((f32[2,512,512]{2,1,0:T(8,128)S(1)}, f32[2,512,512]{2,1,0:T(8,128)S(1)}, u32[]{:S(2)}, u32[]{:S(2)}) %collective-permute-start.8) | collective-permute-done | bytes 2097184 | tf_op jit(solution)/shard_map/ppermute | solution.py:37
  435.6 4.6 collective-permute-start.10
  440.2 1.9 collective-permute-start.9
  442.1 2.8 fusion.76
  444.9 40.4 %collective-permute-done.10 = f32[2,1,512,512]{3,2,0,1:T(8,128)S(1)} collective-permute-done((f32[2,1,512,512]{3,2,0,1:T(8,128)S(1)}, f32[2,1,512,512]{3,2,0,1:T(8,128)S(1)}, u32[]{:S(2)}, u32[]{:S(2)}) %collective-permute-start.10) | collective-permute-done | bytes 2097184 | tf_op jit(solution)/shard_map/ppermute | solution.py:29
  485.3 6.5 %collective-permute-done.9 = f32[2,1,512,512]{3,2,0,1:T(8,128)S(1)} collective-permute-done((f32[2,1,512,512]{3,2,0,1:T(8,128)S(1)}, f32[2,1,512,512]{3,2,0,1:T(8,128)S(1)}, u32[]{:S(2)}, u32[]{:S(2)}) %collective-permute-start.9) | collective-permute-done | bytes 2097184 | tf_op jit(solution)/shard_map/ppermute | solution.py:26
  492.4 1.3 copy-done
  493.7 1.9 conditional.3
  493.7 1.9 fusion.1
  495.5 1.6 broadcast_select_fusion.2
  497.2 116.8 %all-reduce.5.cloned.1.call-done = (f32[512,512]{1,0:T(8,128)}, f32[512,512]{1,0:T(8,128)}, f32[512,512]{1,0:T(8,128)}) async-done(((f32[512,512]{1,0:T(8,128)}, f32[512,512]{1,0:T(8,128)}, f32[512,512]{1,0:T(8,128)}), (f32[512,512]{1,0:T(8,128)}, f32[512,512]{1,0:T(8,128)}, f32[512,512]{1,0:T(8,128)})) %all-reduce.5.cloned.1.call-update) | async-done | bytes 3145744 | tf_op jit(solution)/shard_map/psum | solution.py:98
  614.0 3.3 fusion.9
  617.3 3.0 fusion.3
  (56 shorter events, 2.3 us)
Async XLA Ops:
  6.5 311.4 %all-reduce.7.cloned.1.call-start = ((), (), s32[]{:S(2)}) async-start(), calls=%async_computation.1 | async-start | bytes 6291456 | tf_op jit(solution)/shard_map/psum | solution.py:98
  9.9 1.0 copy-start.5
  9.9 7.1 %copy-start.16 = (s32[8]{0:T(128)S(1)}, s32[8]{0:T(128)}, u32[]{:S(2)}) copy-start(s32[8]{0:T(128)} %param.11) | copy-start | bytes 100
  9.9 7.3 %copy-start.4 = (f32[1,512,512]{2,1,0:T(8,128)S(1)}, f32[1,512,512]{2,1,0:T(8,128)}, u32[]{:S(2)}) copy-start(f32[1,512,512]{2,1,0:T(8,128)} %param.8) | copy-start | bytes 3145732
  12.4 27.5 %collective-permute-start = (bf16[4096,128]{1,0:T(8,128)(2,1)}, bf16[4096,128]{1,0:T(8,128)(2,1)}, u32[]{:S(2)}, u32[]{:S(2)}) collective-permute-start(bf16[4096,128]{1,0:T(8,128)(2,1)} %pad_maximum_fusion.6), channel_id=1, source_target_pairs={{2,0},{4,2},{6,4},{8,6},{10,8},{12,10},{14,12},{16,14},{18,16},{20... | collective-permute-start | bytes 3145736 | tf_op jit(solution)/shard_map/ppermute | solution.py:18
  17.1 12.1 %copy-start.10 = (s32[512]{0:T(512)}, s32[512]{0:T(512)S(1)}, u32[]{:S(2)}) copy-start(s32[512]{0:T(512)S(1)} %ge.37) | copy-start | bytes 6148
  17.1 12.1 %copy-start.12 = (s32[512]{0:T(512)}, s32[512]{0:T(512)S(1)}, u32[]{:S(2)}) copy-start(s32[512]{0:T(512)S(1)} %get-tuple-element.66) | copy-start | bytes 6148
  17.1 12.1 %copy-start.14 = (s32[512]{0:T(512)}, s32[512]{0:T(512)S(1)}, u32[]{:S(2)}) copy-start(s32[512]{0:T(512)S(1)} %get-tuple-element.65) | copy-start | bytes 6148
  17.4 12.0 %collective-permute-start.1 = (f32[64,512]{1,0:T(8,128)S(1)}, f32[64,512]{1,0:T(8,128)S(1)}, u32[]{:S(2)}, u32[]{:S(2)}) collective-permute-start(f32[64,512]{1,0:T(8,128)S(1)} %get-tuple-element.61), channel_id=1, source_target_pairs={{1,0},{32,1},{33,32},{64,33},{65,64},{96,65},{97,96},{128,97},{129... | collective-permute-start | bytes 393224 | tf_op jit(solution)/shard_map/ppermute | solution.py:29
  27.1 11.6 %collective-permute-start.2 = (f32[64,512]{1,0:T(8,128)S(1)}, f32[64,512]{1,0:T(8,128)}, u32[]{:S(2)}, u32[]{:S(2)}) collective-permute-start(f32[64,512]{1,0:T(8,128)S(1)} %get-tuple-element.62), channel_id=1, source_target_pairs={{0,1},{1,32},{32,33},{33,64},{64,65},{65,96},{96,97},{97,128},{128... | collective-permute-start | bytes 393224 | tf_op jit(solution)/shard_map/ppermute | solution.py:26
  29.2 13.5 %copy-start.7 = (f32[1,512,512]{2,1,0:T(8,128)}, f32[1,512,512]{2,1,0:T(8,128)S(1)}, u32[]{:S(2)}) copy-start(f32[1,512,512]{2,1,0:T(8,128)S(1)} %and_select_fusion) | copy-start | bytes 3145732
  29.3 10.6 %copy-start.6 = (bf16[4096,64]{1,0:T(8,128)(2,1)S(1)}, bf16[4096,64]{1,0:T(8,128)(2,1)}, u32[]{:S(2)}) copy-start(bf16[4096,64]{1,0:T(8,128)(2,1)} %copy-done.5) | copy-start | bytes 1572868
  39.9 1.2 copy-start.11
  39.9 1.2 copy-start.13
  43.0 92.9 %collective-permute-start.3 = (f32[2,512,512]{2,1,0:T(8,128)S(1)}, f32[2,512,512]{2,1,0:T(8,128)}, u32[]{:S(2)}, u32[]{:S(2)}) collective-permute-start(f32[2,512,512]{2,1,0:T(8,128)S(1)} %pad_maximum_fusion), channel_id=1, source_target_pairs={{0,128},{32,160},{64,192},{96,224},{128,0},{160,32},{192,64},{224,... | collective-permute-start | bytes 6291464 | tf_op jit(solution)/shard_map/ppermute | solution.py:37
  135.8 50.5 %collective-permute-start.4 = (f32[2,1,512,512]{3,2,0,1:T(8,128)}, f32[2,1,512,512]{3,2,0,1:T(8,128)}, u32[]{:S(2)}, u32[]{:S(2)}) collective-permute-start(f32[2,1,512,512]{3,2,0,1:T(8,128)} %bitcast.12), channel_id=1, source_target_pairs={{0,2},{2,4},{4,6},{6,8},{8,10},{10,12},{12,14},{14,16},{16,18},{18... | collective-permute-start | bytes 6291464 | tf_op jit(solution)/shard_map/ppermute | solution.py:26
  138.5 48.8 %collective-permute-start.5 = (f32[2,1,512,512]{3,2,0,1:T(8,128)}, f32[2,1,512,512]{3,2,0,1:T(8,128)}, u32[]{:S(2)}, u32[]{:S(2)}) collective-permute-start(f32[2,1,512,512]{3,2,0,1:T(8,128)} %bitcast.12), channel_id=1, source_target_pairs={{2,0},{4,2},{6,4},{8,6},{10,8},{12,10},{14,12},{16,14},{18,16},{20... | collective-permute-start | bytes 6291464 | tf_op jit(solution)/shard_map/ppermute | solution.py:29
  189.3 1.3 copy-start.2
  194.2 127.0 %copy-start.3 = (f32[2,1,512,512]{3,2,0,1:T(8,128)S(1)}, f32[2,1,512,512]{3,2,0,1:T(8,128)}, u32[]{:S(2)}) copy-start(f32[2,1,512,512]{3,2,0,1:T(8,128)} %copy-done.2) | copy-start | bytes 6291460
  194.2 127.0 %copy-start.15 = (s32[512]{0:T(512)S(1)}, s32[512]{0:T(512)}, u32[]{:S(2)}) copy-start(s32[512]{0:T(512)} %copy-done.14) | copy-start | bytes 6148
  194.2 419.8 %all-reduce.5.cloned.1.call-start = ((), (), s32[]{:S(2)}) async-start(), calls=%async_computation | async-start | bytes 6291456 | tf_op jit(solution)/shard_map/psum | solution.py:98
  317.9 3.3 copy-start.9
  323.3 15.3 %collective-permute-start.6 = (f32[64,512]{1,0:T(8,128)S(1)}, f32[64,512]{1,0:T(8,128)S(1)}, u32[]{:S(2)}, u32[]{:S(2)}) collective-permute-start(f32[64,512]{1,0:T(8,128)S(1)} %get-tuple-element.55), channel_id=1, source_target_pairs={{1,0},{32,1},{33,32},{64,33},{65,64},{96,65},{97,96},{128,97},{129... | collective-permute-start | bytes 393224 | tf_op jit(solution)/shard_map/ppermute | solution.py:29
  330.5 11.4 %collective-permute-start.7 = (f32[64,512]{1,0:T(8,128)S(1)}, f32[64,512]{1,0:T(8,128)S(1)}, u32[]{:S(2)}, u32[]{:S(2)}) collective-permute-start(f32[64,512]{1,0:T(8,128)S(1)} %get-tuple-element.56), channel_id=1, source_target_pairs={{0,1},{1,32},{32,33},{33,64},{64,65},{65,96},{96,97},{97,128},{128... | collective-permute-start | bytes 393224 | tf_op jit(solution)/shard_map/ppermute | solution.py:26
  343.9 91.7 %collective-permute-start.8 = (f32[2,512,512]{2,1,0:T(8,128)S(1)}, f32[2,512,512]{2,1,0:T(8,128)S(1)}, u32[]{:S(2)}, u32[]{:S(2)}) collective-permute-start(f32[2,512,512]{2,1,0:T(8,128)S(1)} %pad_maximum_fusion.1), channel_id=1, source_target_pairs={{0,128},{32,160},{64,192},{96,224},{128,0},{160,32},{192,64},{224,... | collective-permute-start | bytes 6291464 | tf_op jit(solution)/shard_map/ppermute | solution.py:37
  435.6 49.7 %collective-permute-start.10 = (f32[2,1,512,512]{3,2,0,1:T(8,128)S(1)}, f32[2,1,512,512]{3,2,0,1:T(8,128)S(1)}, u32[]{:S(2)}, u32[]{:S(2)}) collective-permute-start(f32[2,1,512,512]{3,2,0,1:T(8,128)S(1)} %bitcast.72), channel_id=1, source_target_pairs={{2,0},{4,2},{6,4},{8,6},{10,8},{12,10},{14,12},{16,14},{18,16},{20... | collective-permute-start | bytes 6291464 | tf_op jit(solution)/shard_map/ppermute | solution.py:29
  440.2 51.6 %collective-permute-start.9 = (f32[2,1,512,512]{3,2,0,1:T(8,128)S(1)}, f32[2,1,512,512]{3,2,0,1:T(8,128)S(1)}, u32[]{:S(2)}, u32[]{:S(2)}) collective-permute-start(f32[2,1,512,512]{3,2,0,1:T(8,128)S(1)} %bitcast.73), channel_id=1, source_target_pairs={{0,2},{2,4},{4,6},{6,8},{8,10},{10,12},{12,14},{14,16},{16,18},{18... | collective-permute-start | bytes 6291464 | tf_op jit(solution)/shard_map/ppermute | solution.py:26
  492.3 1.3 copy-start
  497.2 120.1 %copy-start.1 = (f32[2,1,512,512]{3,2,0,1:T(8,128)S(1)}, f32[2,1,512,512]{3,2,0,1:T(8,128)}, u32[]{:S(2)}) copy-start(f32[2,1,512,512]{3,2,0,1:T(8,128)} %copy-done) | copy-start | bytes 6291460
  614.0 3.3 copy-start.8
Sparse Core Ops, SparseCore 0:
  194.3 123.5 all-reduce.6
  497.3 116.6 all-reduce.4
where the time goes:
time: 629 us; the launch traced here: 627 us
  waiting for transfers between devices  526 us (84%)
  starting transfers between devices  43.3 us (7%)
  matrix products  26.6 us (4%)
  between operations  13.9 us (2%)
  other arithmetic  13.2 us (2%)
    psum x2, waiting for transfers between devices, per_device(): lax.psum((self_part, low_part, high_part), ('basis', 'rep'))  240 us
    ppermute x2, waiting for transfers between devices, from_partner(): return lax.ppermute(value, axis, pairs)  181 us
    ppermute x4, waiting for transfers between devices, extended(): lax.ppermute(lax.slice_in_dim(block, block.shape[dim] - width, None, axis...  57.5 us
    ppermute x4, waiting for transfers between devices, extended(): lax.ppermute(lax.slice_in_dim(block, 0, width, axis=dim), axis, backward)  46.7 us
    ppermute x4, starting transfers between devices, extended(): lax.ppermute(lax.slice_in_dim(block, 0, width, axis=dim), axis, backward)  26.9 us
  transfers between devices with their start and end apart: 13, of which 11 were waited for; matrix products, arithmetic and copies ran while one was open for 1% of the time, Pallas kernels for 0%

commit v1 on v0

v1 whole, which is shorter than its diff:
```python
import functools

import jax
import jax.numpy as jnp
from jax import lax
from jax.experimental import pallas as pl
from jax.experimental.pallas import tpu as pltpu
from jax.sharding import PartitionSpec as P

BLK = 64
GROUP_BLOCKS = 64
SUPPORT = 96
ITERS = 2
ROWS = 512
ORBS = 512
HALF = 256
GP = 32
HP = 64
TILE = 128
CMAX = 6.0
QMAX = 32767.0
BF = jnp.bfloat16
F32 = jnp.float32
I16 = jnp.int16

HALO_NEXT, HALO_PREV, GSIB, HSIB = 0, 1, 2, 3
RS, RSC, HRS, HRSC = 4, 12, 20, 24
EA, EAS, NA, NAS = 28, 36, 44, 52
HA, HAS, HL, HLS = 60, 64, 68, 72
FE, FES, FN, FNS, FH, FHS = 76, 77, 78, 79, 80, 81
NX, NXC, MET = 82, 83, 84
COUNT = 85


def split(x):
    hi = x.astype(BF)
    return hi, (x - hi.astype(F32)).astype(BF)


def dot(a, b, dims=((1,), (0,))):
    return lax.dot_general(a, b, (dims, ((), ())), preferred_element_type=F32)


def dot3(ah, al, bh, bl, dims=((1,), (0,))):
    return dot(ah, bh, dims) + (dot(ah, bl, dims) + dot(al, bh, dims))


def kernel(
    coef, metric, pattern, starts, out,
    c, chi, clo, nf, nhi, nlo, yhi, ylo, band, gp, hp,
    nq_out, nq_in, cs_own, cs_in, meff, mrecv, msel,
    gsib, hsib, qs, rs, qsc, rsc, hqs, hrs, hqsc, hrsc,
    ea, es, na, ns, ha, hs, ehi, elo, xhi, xlo, mhi, mlo,
    ss, rr, local_sem,
):
    b, o, r = lax.axis_index("basis"), lax.axis_index("orb"), lax.axis_index("rep")
    groups = lax.axis_size("orb")
    core, zl = b % 2, b // 2
    z = r * 4 + zl
    p = b * 2 + r
    q = p % 8
    low = zl < 2
    high = jnp.logical_not(low)
    side = jnp.where(low, o - 1, o + 1)
    away = jnp.where(low, o + 1, o - 1)
    has_side = jnp.logical_and(side >= 0, side < groups)
    has_away = jnp.logical_and(away >= 0, away < groups)
    j = r * 2 + zl - 2

    def dev(bb, oo, rep):
        return {"basis": bb, "orb": oo, "rep": rep}

    def zdev(zz, oo):
        return dev((zz % 4) * 2 + core, oo, zz // 4)

    sibling = dev(zl * 2 + 1 - core, o, r)

    barrier = pltpu.get_barrier_semaphore()

    def greet(device):
        pl.semaphore_signal(barrier, inc=1, device_id=device, device_id_type=pl.DeviceIdType.MESH)

    for k in range(1, 8):
        greet(zdev((z + k) % 8, o))
    greet(sibling)
    step_b = jnp.where(r == 1, b + 1, b - 1)
    has_step = jnp.logical_and(step_b >= 0, step_b < 8)

    @pl.when(has_step)
    def _():
        greet(dev(step_b, o, 1 - r))

    @pl.when(has_side)
    def _():
        for k in range(8):
            greet(zdev((z + k) % 8, side))

    @pl.when(has_away)
    def _():
        base = jnp.where(low, 0, 4)
        for m in range(4):
            greet(dev(base + (m % 2) * 2 + core, away, m // 2))

    load_main = pltpu.make_async_copy(metric.at[pl.ds(pl.multiple_of(q * 512, 64), 512)], meff.at[pl.ds(0, 512)], local_sem.at[0])
    load_prev = pltpu.make_async_copy(
        metric.at[pl.ds(pl.multiple_of((q * 512 + 4032) % 4096, 64), 64)], meff.at[pl.ds(512, 64)], local_sem.at[1]
    )
    load_main.start()
    load_prev.start()
    lane = lax.broadcasted_iota(jnp.int32, (8, ORBS), 1) // BLK
    cs = jnp.zeros((8, ORBS), F32)
    for i in range(8):
        cs = jnp.where(lane == i, starts[i].astype(F32), cs)
    cs_own[...] = cs
    first_block = (o * GROUP_BLOCKS + p * 8).astype(F32)

    def live(t, cs_ref):
        rows = lax.broadcasted_iota(jnp.int32, (TILE, ORBS), 0) // BLK
        block = rows.astype(F32) + (first_block + (t * (TILE // BLK)).astype(F32))
        at = cs_ref[0:1, :]
        return jnp.logical_and(block >= at, block < at + SUPPORT)

    def tiles(body):
        def step(t, carry):
            body(t, pl.ds(pl.multiple_of(t * TILE, TILE), TILE))
            return carry

        lax.fori_loop(0, ROWS // TILE, step, 0)

    def prepare(t, rows):
        x = jnp.where(live(t, cs_own), coef[rows, :], 0.0)
        c[rows, :] = x
        hi, lo = split(x)
        chi[0, rows, :] = hi
        clo[0, rows, :] = lo
        nq_out[rows, :] = jnp.round(jnp.clip(x, -CMAX, CMAX) * (QMAX / CMAX)).astype(I16)

    tiles(prepare)

    for it in range(ITERS):

        @pl.when(p == 0)
        def _():
            chi[it, 512:576, :] = jnp.zeros((64, ORBS), BF)

        @pl.when(p == 15)
        def _():
            chi[it, 576:640, :] = jnp.zeros((64, ORBS), BF)

    load_main.wait()
    load_prev.wait()
    right = lax.broadcasted_iota(jnp.int32, (BLK, 2 * BLK), 1) >= BLK
    for i in range(9):
        at = (q * 8 + i) % 64 if i < 8 else (q * 8 + 63) % 64
        keep = jnp.where(o * GROUP_BLOCKS + at < groups * GROUP_BLOCKS - 1, pattern[at], 0).astype(F32)
        block = meff[i * 64 : i * 64 + 64, :].astype(F32)
        meff[i * 64 : i * 64 + 64, :] = jnp.where(right, block * keep, block).astype(BF)

    waits = [jnp.int32(8), has_step.astype(jnp.int32), 8 * has_side.astype(jnp.int32), 4 * has_away.astype(jnp.int32)]
    pl.semaphore_wait(barrier, waits[0] + waits[1] + waits[2] + waits[3])

    sent = []

    def send(src, dst, it, index, device, cond=None):
        def start():
            pltpu.make_async_remote_copy(
                src_ref=src, dst_ref=dst, send_sem=ss.at[it, index], recv_sem=rr.at[it, index],
                device_id=device, device_id_type=pl.DeviceIdType.MESH,
            ).start()

        if cond is None:
            start()
        else:
            pl.when(cond)(start)
        sent.append((src, it, index, cond))

    def arrived(dst, it, index):
        pltpu.make_async_copy(dst, dst, rr.at[it, index]).wait()

    def send_halo(it):
        up_b = jnp.where(r == 0, b, b + 1)
        down_b = jnp.where(r == 1, b, b - 1)
        send(chi.at[it, pl.ds(0, 64)], chi.at[it, pl.ds(576, 64)], it, HALO_NEXT, dev(down_b, o, 1 - r), p > 0)
        send(chi.at[it, pl.ds(448, 64)], chi.at[it, pl.ds(512, 64)], it, HALO_PREV, dev(up_b, o, 1 - r), p < 15)

    def wait_halo(it):
        pl.when(p < 15)(lambda: arrived(chi.at[it, pl.ds(576, 64)], it, HALO_NEXT))
        pl.when(p > 0)(lambda: arrived(chi.at[it, pl.ds(512, 64)], it, HALO_PREV))

    gives_metric = jnp.logical_and(high, o > 0)
    send(meff, mrecv, 0, MET, dev(b, o - 1, r), gives_metric)
    send_halo(0)
    partner = dev(jnp.where(low, b + 4, b - 4), side, r)
    send(nq_out, nq_in, 0, NX, partner, has_side)
    send(cs_own, cs_in, 0, NXC, partner, has_side)

    @pl.when(low)
    def _():
        msel[...] = meff[...]

    @pl.when(jnp.logical_and(high, has_side))
    def _():
        arrived(mrecv, 0, MET)
        msel[...] = mrecv[...]

    @pl.when(jnp.logical_and(high, jnp.logical_not(has_side)))
    def _():
        msel[...] = jnp.zeros((576, 128), BF)

    @pl.when(p == 8)
    def _():
        msel[512:576, :] = meff[512:576, :]

    band[...] = jnp.zeros((ROWS, 640), BF)
    row_at = lax.broadcasted_iota(jnp.int32, (128, 128), 0)
    lane_at = lax.broadcasted_iota(jnp.int32, (128, 128), 1)
    top, left = row_at < 64, lane_at < 64
    bottom, rest = row_at >= 64, lane_at >= 64
    for t in range(4):
        m = msel[t * 128 : t * 128 + 128, :].astype(F32)
        rolled = pltpu.roll(m, 64, 1)
        corner = jnp.where(jnp.logical_and(top, rest), m, 0.0)
        diag = jnp.where(top, m, jnp.where(rest, rolled, 0.0)) + corner.T
        band[t * 128 : t * 128 + 128, t * 128 : t * 128 + 128] = diag.astype(BF)
        if t < 3:
            off = jnp.where(jnp.logical_and(bottom, left), rolled, 0.0)
            band[t * 128 : t * 128 + 128, t * 128 + 128 : t * 128 + 256] = off.astype(BF)
            band[t * 128 + 128 : t * 128 + 256, t * 128 : t * 128 + 128] = off.T.astype(BF)
        else:
            band[384:512, 512:640] = jnp.where(jnp.logical_and(bottom, rest), m, 0.0).astype(BF)
    before = pltpu.roll(msel[448:576, :].astype(F32), 64, 1).T
    shifted = pltpu.roll(before, 64, 1)
    band[0:128, 512:640] = jnp.where(jnp.logical_and(top, left), shifted, 0.0).astype(BF)

    def images(it):
        def body(t, rows):
            y = dot(band[rows, :], chi[it]) + dot(band[rows, 0:512], clo[it])
            yhi[rows, :], ylo[rows, :] = split(y)

        tiles(body)

    def gram(it):
        def body(t, cols):
            gp[it, cols, :] = dot3(chi[it, 0:512, cols], clo[it, :, cols], yhi[...], ylo[...], ((0,), (0,)))

        tiles(body)

    def cross(it):
        def body(t, cols):
            hp[it, cols, :] = dot3(yhi[:, cols], ylo[:, cols], nhi[...], nlo[...], ((0,), (0,)))

        tiles(body)

    own_half = pl.ds(pl.multiple_of(core * HALF, HALF), HALF)
    other_half = pl.ds(pl.multiple_of((1 - core) * HALF, HALF), HALF)

    def pair_and_pack(it, part, from_pair, packed, scale, size):
        count = HALF // size

        def add(i, top_value):
            rows = pl.ds(pl.multiple_of(core * HALF + i * size, size), size)
            x = part[it, rows, :] + from_pair[it, pl.ds(pl.multiple_of(i * size, size), size), :]
            part[it, rows, :] = x
            return jnp.maximum(top_value, jnp.abs(x))

        peak = jnp.max(lax.fori_loop(0, count, add, jnp.zeros((size, ORBS), F32)), axis=(0, 1), keepdims=True)
        peak = jnp.maximum(peak, 1e-30)
        scale[it] = jnp.broadcast_to(peak * (1.0 / QMAX), (8, 128))
        inv = QMAX / peak

        def pack(i, carry):
            rows = pl.ds(pl.multiple_of(core * HALF + i * size, size), size)
            packed[it, i] = jnp.round(part[it, rows, :] * inv).astype(I16)
            return carry

        lax.fori_loop(0, count, pack, 0)

    def quantized(x):
        peak = jnp.maximum(jnp.max(jnp.abs(x), axis=(0, 1), keepdims=True), 1e-30)
        return jnp.round(x * (QMAX / peak)).astype(I16), jnp.broadcast_to(peak * (1.0 / QMAX), (8, 128))

    def scatter_gram(it):
        arrived(gsib.at[it], it, GSIB)
        pair_and_pack(it, gp, gsib, qs, qsc, GP)
        for k in range(1, 8):
            to = (z + k) % 8
            send(qs.at[it, to], rs.at[it, k], it, RS + k, zdev(to, o))
            send(qsc.at[it], rsc.at[it, k], it, RSC + k, zdev(to, o))

    def scatter_cross(it):
        arrived(hsib.at[it], it, HSIB)
        pair_and_pack(it, hp, hsib, hqs, hqsc, HP)

    def high_peer(m):
        pz = zl if m % 2 == 0 else 5 - zl
        pr = r if m // 2 == 0 else 1 - r
        return pz, pr

    def send_cross(it):
        for m in range(1, 4):
            pz, pr = high_peer(m)
            device = dev(pz * 2 + core, o, pr)
            send(hqs.at[it, pr * 2 + pz - 2], hrs.at[it, m], it, HRS + m, device, high)
            send(hqsc.at[it], hrsc.at[it, m], it, HRSC + m, device, high)

    def own_gram(it, with_side):
        rows = pl.ds(pl.multiple_of(core * HALF + z * GP, GP), GP)
        total = gp[it, rows, :]
        for k in range(1, 8):
            arrived(rs.at[it, k], it, RS + k)
            arrived(rsc.at[it, k], it, RSC + k)
            total = total + rs[it, k].astype(jnp.int32).astype(F32) * rsc[it, k, 0:1, 0:1]
        here = lax.broadcasted_iota(jnp.int32, (GP, ORBS), 0) + (core * HALF + z * GP)
        same = here == lax.broadcasted_iota(jnp.int32, (GP, ORBS), 1)
        value, scale = quantized(total * (1.0 / (SUPPORT * BLK)) - same.astype(F32))
        ea[it, rows, :] = value
        at = core * 8 + z
        es[it, at] = scale
        for k in range(1, 8):
            device = zdev((z + k) % 8, o)
            send(ea.at[it, rows], ea.at[it, rows], it, EA + k, device)
            send(es.at[it, at], es.at[it, at], it, EAS + k, device)
        if with_side:
            for k in range(8):
                to = (z + k) % 8
                column = jnp.where(to % 4 < 2, o + 1, o - 1)
                there = jnp.logical_and(column >= 0, column < groups)
                send(ea.at[it, rows], na.at[rows], it, NA + k, zdev(to, column), there)
                send(es.at[it, at], ns.at[at], it, NAS + k, zdev(to, column), there)

    def own_cross(it):
        rows = pl.ds(pl.multiple_of(core * HALF + j * HP, HP), HP)
        at = core * 4 + j
        low_there = jnp.logical_and(high, o < groups - 1)

        @pl.when(high)
        def _():
            total = hp[it, rows, :]
            for m in range(1, 4):
                arrived(hrs.at[it, m], it, HRS + m)
                arrived(hrsc.at[it, m], it, HRSC + m)
                total = total + hrs[it, m].astype(jnp.int32).astype(F32) * hrsc[it, m, 0:1, 0:1]
            value, scale = quantized(total * (1.0 / (SUPPORT * BLK)))
            ha[it, rows, :] = value
            hs[it, at] = scale

        for m in range(4):
            pz, pr = high_peer(m)
            low_z = zl - 2 if m % 2 == 0 else 3 - zl
            send(ha.at[it, rows], ha.at[it, rows], it, HL + m, dev(low_z * 2 + core, o + 1, pr), low_there)
            send(hs.at[it, at], hs.at[it, at], it, HLS + m, dev(low_z * 2 + core, o + 1, pr), low_there)
            if m > 0:
                send(ha.at[it, rows], ha.at[it, rows], it, HA + m, dev(pz * 2 + core, o, pr), high)
                send(hs.at[it, at], hs.at[it, at], it, HAS + m, dev(pz * 2 + core, o, pr), high)

    def from_peer(full, scales, it, k, size, count, data, tag):
        return full, scales

    own_eight = pl.ds(pl.multiple_of(core * 8, 8), 8)
    other_eight = pl.ds(pl.multiple_of((1 - core) * 8, 8), 8)
    own_four = pl.ds(pl.multiple_of(core * 4, 4), 4)
    other_four = pl.ds(pl.multiple_of((1 - core) * 4, 4), 4)

    def piece(at, size):
        return pl.ds(pl.multiple_of(at * size, size), size)

    def pass_gram(it):
        for k in range(1, 8):
            at = core * 8 + (z + 8 - k) % 8
            arrived(ea.at[it, piece(at, GP)], it, EA + k)
            arrived(es.at[it, at], it, EAS + k)
        send(ea.at[it, own_half], ea.at[it, own_half], it, FE, sibling)
        send(es.at[it, own_eight], es.at[it, own_eight], it, FES, sibling)

    def pass_side(it):
        @pl.when(has_side)
        def _():
            for k in range(8):
                at = core * 8 + (z + 8 - k) % 8
                arrived(na.at[piece(at, GP)], it, NA + k)
                arrived(ns.at[at], it, NAS + k)

        send(na.at[own_half], na.at[own_half], it, FN, sibling, has_side)
        send(ns.at[own_eight], ns.at[own_eight], it, FNS, sibling, has_side)

    def pass_cross(it):
        @pl.when(high)
        def _():
            for m in range(1, 4):
                pz, pr = high_peer(m)
                at = core * 4 + pr * 2 + pz - 2
                arrived(ha.at[it, piece(at, HP)], it, HA + m)
                arrived(hs.at[it, at], it, HAS + m)

        @pl.when(jnp.logical_and(low, has_side))
        def _():
            for m in range(4):
                pz = zl if m % 2 == 0 else 1 - zl
                pr = r if m // 2 == 0 else 1 - r
                at = core * 4 + pr * 2 + pz
                arrived(ha.at[it, piece(at, HP)], it, HL + m)
                arrived(hs.at[it, at], it, HLS + m)

        cond = jnp.logical_or(high, has_side)
        send(ha.at[it, own_half], ha.at[it, own_half], it, FH, sibling, cond)
        send(hs.at[it, own_four], hs.at[it, own_four], it, FHS, sibling, cond)

    def unpack(value, scale):
        return value.astype(jnp.int32).astype(F32) * scale[0:1, 0:1]

    def take_gram(it):
        arrived(ea.at[it, other_half], it, FE)
        arrived(es.at[it, other_eight], it, FES)

        def body(i, carry):
            rows = piece(i, GP)
            ehi[rows, :], elo[rows, :] = split(unpack(ea[it, rows, :], es[it, i]))
            return carry

        lax.fori_loop(0, 16, body, 0)

    def take_side(it):
        @pl.when(has_side)
        def _():
            arrived(na.at[other_half], it, FN)
            arrived(ns.at[other_eight], it, FNS)

            def body(i, carry):
                rows = piece(i, GP)
                mhi[rows, :], mlo[rows, :] = split(unpack(na[rows, :], ns[i]))
                return carry

            lax.fori_loop(0, 16, body, 0)

        @pl.when(jnp.logical_not(has_side))
        def _():
            mhi[...] = jnp.zeros((ORBS, ORBS), BF)
            mlo[...] = jnp.zeros((ORBS, ORBS), BF)

    def take_cross(it):
        @pl.when(jnp.logical_or(high, has_side))
        def _():
            arrived(ha.at[it, other_half], it, FH)
            arrived(hs.at[it, other_four], it, FHS)

        def value(i):
            return jnp.concatenate(
                [unpack(ha[it, piece(2 * i, HP), :], hs[it, 2 * i]), unpack(ha[it, piece(2 * i + 1, HP), :], hs[it, 2 * i + 1])], axis=0
            )

        @pl.when(jnp.logical_and(low, has_side))
        def _():
            def body(i, carry):
                rows = piece(i, TILE)
                xhi[rows, :], xlo[rows, :] = split(value(i))
                return carry

            lax.fori_loop(0, 4, body, 0)

        @pl.when(jnp.logical_and(high, has_side))
        def _():
            def body(i, carry):
                cols = piece(i, TILE)
                xhi[:, cols], xlo[:, cols] = split(value(i).T)
                return carry

            lax.fori_loop(0, 4, body, 0)

        @pl.when(jnp.logical_not(has_side))
        def _():
            xhi[...] = jnp.zeros((ORBS, ORBS), BF)
            xlo[...] = jnp.zeros((ORBS, ORBS), BF)

    def updated(it, t, rows):
        change = dot3(chi[it, rows, :], clo[it, rows, :], ehi[...], elo[...])
        change = change + dot3(nhi[rows, :], nlo[rows, :], xhi[...], xlo[...])
        return jnp.where(live(t, cs_own), c[rows, :] - 0.5 * change, 0.0)

    wait_halo(0)
    images(0)
    gram(0)
    send(gp.at[0, other_half], gsib.at[0], 0, GSIB, sibling)
    scatter_gram(0)
    own_gram(0, True)

    @pl.when(has_side)
    def _():
        arrived(nq_in, 0, NX)
        arrived(cs_in, 0, NXC)

        def body(t, rows):
            x = nq_in[rows, :].astype(jnp.int32).astype(F32) * (CMAX / QMAX)
            nf[rows, :] = x
            nhi[rows, :], nlo[rows, :] = split(x)

        tiles(body)

    @pl.when(jnp.logical_not(has_side))
    def _():
        nf[...] = jnp.zeros((ROWS, ORBS), F32)
        nhi[...] = jnp.zeros((ROWS, ORBS), BF)
        nlo[...] = jnp.zeros((ROWS, ORBS), BF)
        cs_in[...] = jnp.zeros((8, ORBS), F32)

    def cross_round(it):
        pl.when(high)(lambda: cross(it))
        send(hp.at[it, other_half], hsib.at[it], it, HSIB, sibling, high)

    cross_round(0)
    pass_gram(0)
    pass_side(0)
    pl.when(high)(lambda: scatter_cross(0))
    send_cross(0)
    own_cross(0)
    take_gram(0)
    pass_cross(0)
    take_cross(0)

    def first(t, rows):
        x = updated(0, t, rows)
        c[rows, :] = x
        hi, lo = split(x)
        chi[1, rows, :] = hi
        clo[1, rows, :] = lo

    tiles(first)
    send_halo(1)
    take_side(0)

    def beside(t, rows):
        change = dot3(nhi[rows, :], nlo[rows, :], mhi[...], mlo[...])
        change = change + dot3(chi[0, rows, :], clo[0, rows, :], xhi[...], xlo[...], ((1,), (1,)))
        x = jnp.where(live(t, cs_in), nf[rows, :] - 0.5 * change, 0.0)
        nhi[rows, :], nlo[rows, :] = split(x)

    pl.when(has_side)(lambda: tiles(beside))

    wait_halo(1)
    images(1)
    gram(1)
    send(gp.at[1, other_half], gsib.at[1], 1, GSIB, sibling)
    cross_round(1)
    scatter_gram(1)
    pl.when(high)(lambda: scatter_cross(1))
    send_cross(1)
    own_gram(1, False)
    own_cross(1)
    pass_gram(1)
    pass_cross(1)
    take_gram(1)
    take_cross(1)

    def last(t, rows):
        out[rows, :] = updated(1, t, rows)

    tiles(last)

    for src, it, index, cond in sent:

        def wait(src=src, it=it, index=index):
            pltpu.make_async_copy(src, src, ss.at[it, index]).wait()

        if cond is None:
            wait()
        else:
            pl.when(cond)(wait)


def per_device(coefficients, basis_metric, pattern, starts):
    vm = pltpu.VMEM
    square = (ORBS, ORBS)
    scratch = [
        vm((ROWS, ORBS), F32), vm((2, 640, ORBS), BF), vm((2, ROWS, ORBS), BF),
        vm((ROWS, ORBS), F32), vm((ROWS, ORBS), BF), vm((ROWS, ORBS), BF),
        vm((ROWS, ORBS), BF), vm((ROWS, ORBS), BF), vm((ROWS, 640), BF),
        vm((2, ORBS, ORBS), F32), vm((2, ORBS, ORBS), F32),
        vm((ROWS, ORBS), I16), vm((ROWS, ORBS), I16), vm((8, ORBS), F32), vm((8, ORBS), F32),
        vm((576, 128), BF), vm((576, 128), BF), vm((576, 128), BF),
        vm((2, HALF, ORBS), F32), vm((2, HALF, ORBS), F32),
        vm((2, 8, GP, ORBS), I16), vm((2, 8, GP, ORBS), I16), vm((2, 8, 128), F32), vm((2, 8, 8, 128), F32),
        vm((2, 4, HP, ORBS), I16), vm((2, 4, HP, ORBS), I16), vm((2, 8, 128), F32), vm((2, 4, 8, 128), F32),
        vm((2, ORBS, ORBS), I16), vm((2, 16, 8, 128), F32), vm(square, I16), vm((16, 8, 128), F32),
        vm((2, ORBS, ORBS), I16), vm((2, 8, 8, 128), F32),
        vm(square, BF), vm(square, BF), vm(square, BF), vm(square, BF), vm(square, BF), vm(square, BF),
        pltpu.SemaphoreType.DMA((2, COUNT)), pltpu.SemaphoreType.DMA((2, COUNT)), pltpu.SemaphoreType.DMA((2,)),
    ]
    result = pl.pallas_call(
        kernel,
        out_shape=jax.ShapeDtypeStruct((ROWS, ORBS), F32),
        in_specs=[
            pl.BlockSpec(memory_space=pltpu.VMEM),
            pl.BlockSpec(memory_space=pl.ANY),
            pl.BlockSpec(memory_space=pltpu.SMEM),
            pl.BlockSpec(memory_space=pltpu.SMEM),
        ],
        out_specs=pl.BlockSpec(memory_space=pltpu.VMEM),
        scratch_shapes=scratch,
        compiler_params=pltpu.CompilerParams(
            collective_id=0, has_side_effects=True, vmem_limit_bytes=50 * 1024 * 1024
        ),
    )(coefficients[0], basis_metric, pattern, starts)
    return result[None]


def solution(mesh):
    in_specs = (P("orb", ("basis", "rep"), None), P("orb", None), P("orb"), P("orb"))
    out_specs = P("orb", ("basis", "rep"), None)
    return jax.shard_map(
        per_device, mesh=mesh, in_specs=in_specs, out_specs=out_specs, check_vma=False
    )
```

time: 629 us -> 136 us (0.22)
  waiting for transfers between devices: 526 us -> 0 us
  Pallas kernels: 0 us -> 131 us
  starting transfers between devices: 43.3 us -> 0 us
  matrix products: 26.6 us -> 0 us
  between operations: 13.9 us -> 0.01 us
  other arithmetic: 13.2 us -> 0 us
    ppermute x11 -> x0, waiting for transfers between devices: 286 us -> none  [the longest x2 181 us: from_partner(): return lax.ppermute(value, axis, pairs)]
    psum x2 -> x0, waiting for transfers between devices: 240 us -> none  [per_device(): lax.psum((self_part, low_part, high_part), ('basis', 'rep'))]
    pallas_call x0 -> x1, Pallas kernels: none -> 131 us  [per_device(): pl.pallas_call(kernel, out_shape=jax.ShapeDtypeStruct((ROWS, ORBS), F32),...]
    ppermute x11 -> x0, starting transfers between devices: 43.2 us -> none  [the longest x4 26.9 us: extended(): lax.ppermute(lax.slice_in_dim(block, 0, width, axis=dim), axis, backward)]
    dot_general x14 -> x0, matrix products: 26.6 us -> none  [the longest x2 6.89 us: per_device(): self_part = jnp.einsum('ro,rp->op', coeff_now, applied, precision=HIGH)]
  transfers between devices with their start and end apart: 13 -> 0, of which waited for: 11 -> 0; matrix products, arithmetic and copies ran while one was open for 1% -> 0% of each run, Pallas kernels for 0% -> 0%
where the time goes in v1:
time: 136 us; the launch traced here: 135 us
  Pallas kernels  131 us (96%)
  local copies, waits for them, and re-layouts  4.09 us (3%)
    pallas_call x1, Pallas kernels, per_device(): pl.pallas_call(kernel, out_shape=jax.ShapeDtypeStruct((ROWS, ORBS), F32),...  131 us
    unnamed x9, local copies, waits for them, and re-layouts  4.09 us

profile of v1, /device:TPU:25, one launch (start us, length us, event | category | flops | bytes accessed | tf_op | source)
XLA Modules:
  0.0 135.4 jit_solution(9423568597002410640)
XLA Ops:
  0.0 0.0 copy-start.3
  0.0 0.0 copy-start.2
  0.0 0.7 copy-done.3
  0.7 0.0 copy-done.2
  0.7 0.0 copy-start
  0.7 1.2 copy-done
  1.9 0.0 copy-start.1
  1.9 1.2 copy-done.1
  3.1 131.3 %shard_map.46 = f32[512,512]{1,0:T(8,128)S(1)} custom-call(f32[512,512]{1,0:T(8,128)S(1)} %bitcast.3, bf16[4096,128]{1,0:T(8,128)(2,1)S(1)} %copy-done.1, s32[64]{0:T(128)S(1)} %copy-done.2, s32[8]{0:T(128)S(1)} %copy-done.3), custom_call_target="tpu_custom_call" | custom-call | tf_op jit(solution)/shard_map/pallas_call | solution.py:587
  134.4 1.0 copy.6
Async XLA Ops:
  0.0 0.7 copy-start.3
  0.0 0.7 copy-start.2
  0.7 1.2 copy-start
  1.9 1.2 copy-start.1

commit v2 on v1

--- a/solution.py
+++ b/solution.py
@@ -14,7 +14,9 @@
 ROWS = 512
 ORBS = 512
 HALF = 256
-GP = 32
+GP = 80
+PACKED = 1280
+PHALF = 640
 HP = 64
 TILE = 128
 CMAX = 6.0
@@ -27,9 +29,11 @@
 RS, RSC, HRS, HRSC = 4, 12, 20, 24
 EA, EAS, NA, NAS = 28, 36, 44, 52
 HA, HAS, HL, HLS = 60, 64, 68, 72
-FE, FES, FN, FNS, FH, FHS = 76, 77, 78, 79, 80, 81
-NX, NXC, MET = 82, 83, 84
-COUNT = 85
+FE, FES, FN, FNS, FH, FHS = 76, 77, 78, 79, 80, 82
+NX, NXC, MET, HN, HNS = 84, 85, 86, 87, 88
+COUNT = 89
+
+KEPT = [(a, b) for a in range(4) for b in range(a, 4)]
 
 
 def split(x):
@@ -50,7 +54,7 @@
     c, chi, clo, nf, nhi, nlo, yhi, ylo, band, gp, hp,
     nq_out, nq_in, cs_own, cs_in, meff, mrecv, msel,
     gsib, hsib, qs, rs, qsc, rsc, hqs, hrs, hqsc, hrsc,
-    ea, es, na, ns, ha, hs, ehi, elo, xhi, xlo, mhi, mlo,
+    ea, es, na, ns, ha, hs, ehi, elo, xhi, xlo, thi, tlo, mhi, mlo, ef,
     ss, rr, local_sem,
 ):
     b, o, r = lax.axis_index("basis"), lax.axis_index("orb"), lax.axis_index("rep")
@@ -92,15 +96,20 @@
 
     @pl.when(has_side)
     def _():
-        for k in range(8):
-            greet(zdev((z + k) % 8, side))
+        base = jnp.where(low, 4, 0)
+        for m in range(4):
+            greet(dev(base + (m % 2) * 2 + core, side, m // 2))
+        greet(dev(b, side, r))
 
     @pl.when(has_away)
     def _():
-        base = jnp.where(low, 0, 4)
-        for m in range(4):
-            greet(dev(base + (m % 2) * 2 + core, away, m // 2))
-
+        greet(dev(b, away, r))
+
+    loads = [
+        pltpu.make_async_copy(coef.at[pl.ds(t * TILE, TILE)], c.at[pl.ds(t * TILE, TILE)], local_sem.at[2 + t]) for t in range(4)
+    ]
+    for load in loads:
+        load.start()
     load_main = pltpu.make_async_copy(metric.at[pl.ds(pl.multiple_of(q * 512, 64), 512)], meff.at[pl.ds(0, 512)], local_sem.at[0])
     load_prev = pltpu.make_async_copy(
         metric.at[pl.ds(pl.multiple_of((q * 512 + 4032) % 4096, 64), 64)], meff.at[pl.ds(512, 64)], local_sem.at[1]
@@ -128,14 +137,16 @@
         lax.fori_loop(0, ROWS // TILE, step, 0)
 
     def prepare(t, rows):
-        x = jnp.where(live(t, cs_own), coef[rows, :], 0.0)
+        x = jnp.where(live(t, cs_own), c[rows, :], 0.0)
         c[rows, :] = x
         hi, lo = split(x)
         chi[0, rows, :] = hi
         clo[0, rows, :] = lo
         nq_out[rows, :] = jnp.round(jnp.clip(x, -CMAX, CMAX) * (QMAX / CMAX)).astype(I16)
 
-    tiles(prepare)
+    for t in range(4):
+        loads[t].wait()
+        prepare(jnp.int32(t), pl.ds(t * TILE, TILE))
 
     for it in range(ITERS):
 
@@ -156,15 +167,17 @@
         block = meff[i * 64 : i * 64 + 64, :].astype(F32)
         meff[i * 64 : i * 64 + 64, :] = jnp.where(right, block * keep, block).astype(BF)
 
-    waits = [jnp.int32(8), has_step.astype(jnp.int32), 8 * has_side.astype(jnp.int32), 4 * has_away.astype(jnp.int32)]
+    waits = [jnp.int32(8), has_step.astype(jnp.int32), 5 * has_side.astype(jnp.int32), has_away.astype(jnp.int32)]
     pl.semaphore_wait(barrier, waits[0] + waits[1] + waits[2] + waits[3])
 
     sent = []
 
-    def send(src, dst, it, index, device, cond=None):
+    def send(src, dst, it, index, device, cond=None, land=None):
+        land = index if land is None else land
+
         def start():
             pltpu.make_async_remote_copy(
-                src_ref=src, dst_ref=dst, send_sem=ss.at[it, index], recv_sem=rr.at[it, index],
+                src_ref=src, dst_ref=dst, send_sem=ss.at[it, index], recv_sem=rr.at[it, land],
                 device_id=device, device_id_type=pl.DeviceIdType.MESH,
             ).start()
 
@@ -240,10 +253,13 @@
         tiles(body)
 
     def gram(it):
-        def body(t, cols):
-            gp[it, cols, :] = dot3(chi[it, 0:512, cols], clo[it, :, cols], yhi[...], ylo[...], ((0,), (0,)))
-
-        tiles(body)
+        for a in range(4):
+            cols = slice(a * TILE, a * TILE + TILE)
+            rest = slice(a * TILE, ORBS)
+            g = dot3(chi[it, 0:512, cols], clo[it, :, cols], yhi[:, rest], ylo[:, rest], ((0,), (0,)))
+            for e in range(a, 4):
+                k = KEPT.index((a, e))
+                gp[it, k * TILE : k * TILE + TILE, :] = g[:, (e - a) * TILE : (e - a) * TILE + TILE]
 
     def cross(it):
         def body(t, cols):
@@ -253,23 +269,25 @@
 
     own_half = pl.ds(pl.multiple_of(core * HALF, HALF), HALF)
     other_half = pl.ds(pl.multiple_of((1 - core) * HALF, HALF), HALF)
-
-    def pair_and_pack(it, part, from_pair, packed, scale, size):
-        count = HALF // size
+    own_part = pl.ds(pl.multiple_of(core * PHALF, PHALF), PHALF)
+    other_part = pl.ds(pl.multiple_of((1 - core) * PHALF, PHALF), PHALF)
+
+    def pair_and_pack(it, part, from_pair, packed, scale, size, count):
+        half, wide = size * count, part.shape[2]
 
         def add(i, top_value):
-            rows = pl.ds(pl.multiple_of(core * HALF + i * size, size), size)
+            rows = pl.ds(pl.multiple_of(core * half + i * size, size), size)
             x = part[it, rows, :] + from_pair[it, pl.ds(pl.multiple_of(i * size, size), size), :]
             part[it, rows, :] = x
             return jnp.maximum(top_value, jnp.abs(x))
 
-        peak = jnp.max(lax.fori_loop(0, count, add, jnp.zeros((size, ORBS), F32)), axis=(0, 1), keepdims=True)
+        peak = jnp.max(lax.fori_loop(0, count, add, jnp.zeros((size, wide), F32)), axis=(0, 1), keepdims=True)
         peak = jnp.maximum(peak, 1e-30)
         scale[it] = jnp.broadcast_to(peak * (1.0 / QMAX), (8, 128))
         inv = QMAX / peak
 
         def pack(i, carry):
-            rows = pl.ds(pl.multiple_of(core * HALF + i * size, size), size)
+            rows = pl.ds(pl.multiple_of(core * half + i * size, size), size)
             packed[it, i] = jnp.round(part[it, rows, :] * inv).astype(I16)
             return carry
 
@@ -281,7 +299,7 @@
 
     def scatter_gram(it):
         arrived(gsib.at[it], it, GSIB)
-        pair_and_pack(it, gp, gsib, qs, qsc, GP)
+        pair_and_pack(it, gp, gsib, qs, qsc, GP, 8)
         for k in range(1, 8):
             to = (z + k) % 8
             send(qs.at[it, to], rs.at[it, k], it, RS + k, zdev(to, o))
@@ -289,7 +307,7 @@
 
     def scatter_cross(it):
         arrived(hsib.at[it], it, HSIB)
-        pair_and_pack(it, hp, hsib, hqs, hqsc, HP)
+        pair_and_pack(it, hp, hsib, hqs, hqsc, HP, 4)
 
     def high_peer(m):
         pz = zl if m % 2 == 0 else 5 - zl
@@ -303,16 +321,20 @@
             send(hqs.at[it, pr * 2 + pz - 2], hrs.at[it, m], it, HRS + m, device, high)
             send(hqsc.at[it], hrsc.at[it, m], it, HRSC + m, device, high)
 
-    def own_gram(it, with_side):
-        rows = pl.ds(pl.multiple_of(core * HALF + z * GP, GP), GP)
+    def own_gram(it):
+        rows = pl.ds(pl.multiple_of(core * PHALF + z * GP, GP), GP)
         total = gp[it, rows, :]
         for k in range(1, 8):
             arrived(rs.at[it, k], it, RS + k)
             arrived(rsc.at[it, k], it, RSC + k)
             total = total + rs[it, k].astype(jnp.int32).astype(F32) * rsc[it, k, 0:1, 0:1]
-        here = lax.broadcasted_iota(jnp.int32, (GP, ORBS), 0) + (core * HALF + z * GP)
-        same = here == lax.broadcasted_iota(jnp.int32, (GP, ORBS), 1)
-        value, scale = quantized(total * (1.0 / (SUPPORT * BLK)) - same.astype(F32))
+        here = lax.broadcasted_iota(jnp.int32, (GP, TILE), 0) + (core * PHALF + z * GP)
+        tile = lax.shift_right_logical(here, 7)
+        within = jnp.bitwise_and(here, 127) == lax.broadcasted_iota(jnp.int32, (GP, TILE), 1)
+        on = jnp.zeros((GP, TILE), F32)
+        for a in range(4):
+            on = jnp.where(jnp.logical_and(tile == KEPT.index((a, a)), within), 1.0, on)
+        value, scale = quantized(total * (1.0 / (SUPPORT * BLK)) - on)
         ea[it, rows, :] = value
         at = core * 8 + z
         es[it, at] = scale
@@ -320,13 +342,6 @@
             device = zdev((z + k) % 8, o)
             send(ea.at[it, rows], ea.at[it, rows], it, EA + k, device)
             send(es.at[it, at], es.at[it, at], it, EAS + k, device)
-        if with_side:
-            for k in range(8):
-                to = (z + k) % 8
-                column = jnp.where(to % 4 < 2, o + 1, o - 1)
-                there = jnp.logical_and(column >= 0, column < groups)
-                send(ea.at[it, rows], na.at[rows], it, NA + k, zdev(to, column), there)
-                send(es.at[it, at], ns.at[at], it, NAS + k, zdev(to, column), there)
 
     def own_cross(it):
         rows = pl.ds(pl.multiple_of(core * HALF + j * HP, HP), HP)
@@ -344,127 +359,148 @@
             ha[it, rows, :] = value
             hs[it, at] = scale
 
-        for m in range(4):
+        for m in range(1, 4):
             pz, pr = high_peer(m)
-            low_z = zl - 2 if m % 2 == 0 else 3 - zl
-            send(ha.at[it, rows], ha.at[it, rows], it, HL + m, dev(low_z * 2 + core, o + 1, pr), low_there)
-            send(hs.at[it, at], hs.at[it, at], it, HLS + m, dev(low_z * 2 + core, o + 1, pr), low_there)
-            if m > 0:
-                send(ha.at[it, rows], ha.at[it, rows], it, HA + m, dev(pz * 2 + core, o, pr), high)
-                send(hs.at[it, at], hs.at[it, at], it, HAS + m, dev(pz * 2 + core, o, pr), high)
-
-    def from_peer(full, scales, it, k, size, count, data, tag):
-        return full, scales
+            send(ha.at[it, rows], ha.at[it, rows], it, HA + m, dev(pz * 2 + core, o, pr), high)
+            send(hs.at[it, at], hs.at[it, at], it, HAS + m, dev(pz * 2 + core, o, pr), high)
+        for m in range(2):
+            device = dev(2 + core, o + 1, r) if m == 0 else dev(core, o + 1, 1 - r)
+            send(ha.at[it, rows], ha.at[it, rows], it, HL + m, device, low_there, HL + jnp.maximum(zl - 2, 0))
+            send(hs.at[it, at], hs.at[it, at], it, HLS + m, device, low_there, HLS + jnp.maximum(zl - 2, 0))
 
     own_eight = pl.ds(pl.multiple_of(core * 8, 8), 8)
     other_eight = pl.ds(pl.multiple_of((1 - core) * 8, 8), 8)
-    own_four = pl.ds(pl.multiple_of(core * 4, 4), 4)
-    other_four = pl.ds(pl.multiple_of((1 - core) * 4, 4), 4)
+    near = jnp.where(jnp.logical_and(low, zl == 0), 1 - r, r)
+    near_rows = pl.ds(pl.multiple_of(core * HALF + near * 128, 128), 128)
+    far_rows = pl.ds(pl.multiple_of(core * HALF + (1 - near) * 128, 128), 128)
+    near_two = pl.ds(core * 4 + near * 2, 2)
+    far_two = pl.ds(core * 4 + (1 - near) * 2, 2)
+    pair_near_rows = pl.ds(pl.multiple_of((1 - core) * HALF + near * 128, 128), 128)
+    pair_far_rows = pl.ds(pl.multiple_of((1 - core) * HALF + (1 - near) * 128, 128), 128)
+    pair_near_two = pl.ds((1 - core) * 4 + near * 2, 2)
+    pair_far_two = pl.ds((1 - core) * 4 + (1 - near) * 2, 2)
 
     def piece(at, size):
         return pl.ds(pl.multiple_of(at * size, size), size)
 
-    def pass_gram(it):
+    def pass_gram(it, with_side):
         for k in range(1, 8):
             at = core * 8 + (z + 8 - k) % 8
             arrived(ea.at[it, piece(at, GP)], it, EA + k)
             arrived(es.at[it, at], it, EAS + k)
-        send(ea.at[it, own_half], ea.at[it, own_half], it, FE, sibling)
+        send(ea.at[it, own_part], ea.at[it, own_part], it, FE, sibling)
         send(es.at[it, own_eight], es.at[it, own_eight], it, FES, sibling)
+        if with_side:
+            send(ea.at[it, own_part], na.at[own_part], it, NA, dev(b, away, r), has_away)
+            send(es.at[it, own_eight], ns.at[own_eight], it, NAS, dev(b, away, r), has_away)
 
     def pass_side(it):
         @pl.when(has_side)
         def _():
-            for k in range(8):
-                at = core * 8 + (z + 8 - k) % 8
-                arrived(na.at[piece(at, GP)], it, NA + k)
-                arrived(ns.at[at], it, NAS + k)
-
-        send(na.at[own_half], na.at[own_half], it, FN, sibling, has_side)
+            arrived(na.at[own_part], it, NA)
+            arrived(ns.at[own_eight], it, NAS)
+
+        send(na.at[own_part], na.at[own_part], it, FN, sibling, has_side)
         send(ns.at[own_eight], ns.at[own_eight], it, FNS, sibling, has_side)
 
     def pass_cross(it):
-        @pl.when(high)
-        def _():
-            for m in range(1, 4):
-                pz, pr = high_peer(m)
-                at = core * 4 + pr * 2 + pz - 2
-                arrived(ha.at[it, piece(at, HP)], it, HA + m)
-                arrived(hs.at[it, at], it, HAS + m)
-
-        @pl.when(jnp.logical_and(low, has_side))
-        def _():
-            for m in range(4):
-                pz = zl if m % 2 == 0 else 1 - zl
-                pr = r if m // 2 == 0 else 1 - r
-                at = core * 4 + pr * 2 + pz
+        cond = jnp.logical_or(high, has_side)
+        low_side = jnp.logical_and(low, has_side)
+
+        def high_arrived(m):
+            pz, pr = high_peer(m)
+            at = core * 4 + pr * 2 + pz - 2
+            arrived(ha.at[it, piece(at, HP)], it, HA + m)
+            arrived(hs.at[it, at], it, HAS + m)
+
+        pl.when(high)(lambda: high_arrived(1))
+
+        @pl.when(low_side)
+        def _():
+            for m in range(2):
+                at = core * 4 + near * 2 + m
                 arrived(ha.at[it, piece(at, HP)], it, HL + m)
                 arrived(hs.at[it, at], it, HLS + m)
 
-        cond = jnp.logical_or(high, has_side)
-        send(ha.at[it, own_half], ha.at[it, own_half], it, FH, sibling, cond)
-        send(hs.at[it, own_four], hs.at[it, own_four], it, FHS, sibling, cond)
+        beside_low = dev((1 - zl) * 2 + core, o, r)
+        send(ha.at[it, near_rows], ha.at[it, near_rows], it, HN, beside_low, low_side)
+        send(hs.at[it, near_two], hs.at[it, near_two], it, HNS, beside_low, low_side)
+        send(ha.at[it, near_rows], ha.at[it, near_rows], it, FH, sibling, cond)
+        send(hs.at[it, near_two], hs.at[it, near_two], it, FHS, sibling, cond)
+
+        @pl.when(high)
+        def _():
+            high_arrived(2)
+            high_arrived(3)
+
+        @pl.when(low_side)
+        def _():
+            arrived(ha.at[it, far_rows], it, HN)
+            arrived(hs.at[it, far_two], it, HNS)
+
+        send(ha.at[it, far_rows], ha.at[it, far_rows], it, FH + 1, sibling, cond)
+        send(hs.at[it, far_two], hs.at[it, far_two], it, FHS + 1, sibling, cond)
 
     def unpack(value, scale):
         return value.astype(jnp.int32).astype(F32) * scale[0:1, 0:1]
 
-    def take_gram(it):
-        arrived(ea.at[it, other_half], it, FE)
-        arrived(es.at[it, other_eight], it, FES)
-
+    def spread(packed, scales, to_hi, to_lo):
         def body(i, carry):
             rows = piece(i, GP)
-            ehi[rows, :], elo[rows, :] = split(unpack(ea[it, rows, :], es[it, i]))
+            ef[rows, :] = unpack(packed[rows, :], scales[i])
             return carry
 
         lax.fori_loop(0, 16, body, 0)
+        for k, (a, e) in enumerate(KEPT):
+            x = ef[k * TILE : k * TILE + TILE, :]
+            at, to = slice(a * TILE, a * TILE + TILE), slice(e * TILE, e * TILE + TILE)
+            to_hi[at, to], to_lo[at, to] = split(x)
+            if a != e:
+                to_hi[to, at], to_lo[to, at] = split(x.T)
+
+    def take_gram(it):
+        arrived(ea.at[it, other_part], it, FE)
+        arrived(es.at[it, other_eight], it, FES)
+        spread(ea.at[it], es.at[it], ehi, elo)
 
     def take_side(it):
         @pl.when(has_side)
         def _():
-            arrived(na.at[other_half], it, FN)
+            arrived(na.at[other_part], it, FN)
             arrived(ns.at[other_eight], it, FNS)
-
-            def body(i, carry):
-                rows = piece(i, GP)
-                mhi[rows, :], mlo[rows, :] = split(unpack(na[rows, :], ns[i]))
-                return carry
-
-            lax.fori_loop(0, 16, body, 0)
-
-        @pl.when(jnp.logical_not(has_side))
-        def _():
-            mhi[...] = jnp.zeros((ORBS, ORBS), BF)
-            mlo[...] = jnp.zeros((ORBS, ORBS), BF)
+            spread(na, ns, mhi, mlo)
+
+    def cross_value(it, i):
+        return jnp.concatenate(
+            [unpack(ha[it, piece(2 * i, HP), :], hs[it, 2 * i]), unpack(ha[it, piece(2 * i + 1, HP), :], hs[it, 2 * i + 1])], axis=0
+        )
+
+    def cross_plain(it, to_hi, to_lo):
+        def body(i, carry):
+            rows = piece(i, TILE)
+            to_hi[rows, :], to_lo[rows, :] = split(cross_value(it, i))
+            return carry
+
+        lax.fori_loop(0, 4, body, 0)
+
+    def cross_turned(it, to_hi, to_lo):
+        def body(i, carry):
+            cols = piece(i, TILE)
+            to_hi[:, cols], to_lo[:, cols] = split(cross_value(it, i).T)
+            return carry
+
+        lax.fori_loop(0, 4, body, 0)
 
     def take_cross(it):
         @pl.when(jnp.logical_or(high, has_side))
         def _():
-            arrived(ha.at[it, other_half], it, FH)
-            arrived(hs.at[it, other_four], it, FHS)
-
-        def value(i):
-            return jnp.concatenate(
-                [unpack(ha[it, piece(2 * i, HP), :], hs[it, 2 * i]), unpack(ha[it, piece(2 * i + 1, HP), :], hs[it, 2 * i + 1])], axis=0
-            )
-
-        @pl.when(jnp.logical_and(low, has_side))
-        def _():
-            def body(i, carry):
-                rows = piece(i, TILE)
-                xhi[rows, :], xlo[rows, :] = split(value(i))
-                return carry
-
-            lax.fori_loop(0, 4, body, 0)
-
-        @pl.when(jnp.logical_and(high, has_side))
-        def _():
-            def body(i, carry):
-                cols = piece(i, TILE)
-                xhi[:, cols], xlo[:, cols] = split(value(i).T)
-                return carry
-
-            lax.fori_loop(0, 4, body, 0)
+            arrived(ha.at[it, pair_near_rows], it, FH)
+            arrived(hs.at[it, pair_near_two], it, FHS)
+            arrived(ha.at[it, pair_far_rows], it, FH + 1)
+            arrived(hs.at[it, pair_far_two], it, FHS + 1)
+
+        pl.when(jnp.logical_and(low, has_side))(lambda: cross_plain(it, xhi, xlo))
+        pl.when(jnp.logical_and(high, has_side))(lambda: cross_turned(it, xhi, xlo))
 
         @pl.when(jnp.logical_not(has_side))
         def _():
@@ -476,45 +512,27 @@
         change = change + dot3(nhi[rows, :], nlo[rows, :], xhi[...], xlo[...])
         return jnp.where(live(t, cs_own), c[rows, :] - 0.5 * change, 0.0)
 
-    wait_halo(0)
-    images(0)
-    gram(0)
-    send(gp.at[0, other_half], gsib.at[0], 0, GSIB, sibling)
-    scatter_gram(0)
-    own_gram(0, True)
-
-    @pl.when(has_side)
-    def _():
-        arrived(nq_in, 0, NX)
-        arrived(cs_in, 0, NXC)
-
-        def body(t, rows):
-            x = nq_in[rows, :].astype(jnp.int32).astype(F32) * (CMAX / QMAX)
-            nf[rows, :] = x
-            nhi[rows, :], nlo[rows, :] = split(x)
-
-        tiles(body)
-
-    @pl.when(jnp.logical_not(has_side))
-    def _():
-        nf[...] = jnp.zeros((ROWS, ORBS), F32)
-        nhi[...] = jnp.zeros((ROWS, ORBS), BF)
-        nlo[...] = jnp.zeros((ROWS, ORBS), BF)
-        cs_in[...] = jnp.zeros((8, ORBS), F32)
+    def take_rows():
+        @pl.when(has_side)
+        def _():
+            arrived(nq_in, 0, NX)
+            arrived(cs_in, 0, NXC)
+
+            def body(t, rows):
+                x = nq_in[rows, :].astype(jnp.int32).astype(F32) * (CMAX / QMAX)
+                nf[rows, :] = x
+                nhi[rows, :], nlo[rows, :] = split(x)
+
+            tiles(body)
+
+        @pl.when(jnp.logical_not(has_side))
+        def _():
+            nhi[...] = jnp.zeros((ROWS, ORBS), BF)
+            nlo[...] = jnp.zeros((ROWS, ORBS), BF)
 
     def cross_round(it):
         pl.when(high)(lambda: cross(it))
         send(hp.at[it, other_half], hsib.at[it], it, HSIB, sibling, high)
-
-    cross_round(0)
-    pass_gram(0)
-    pass_side(0)
-    pl.when(high)(lambda: scatter_cross(0))
-    send_cross(0)
-    own_cross(0)
-    take_gram(0)
-    pass_cross(0)
-    take_cross(0)
 
     def first(t, rows):
         x = updated(0, t, rows)
@@ -523,36 +541,61 @@
         chi[1, rows, :] = hi
         clo[1, rows, :] = lo
 
-    tiles(first)
-    send_halo(1)
-    take_side(0)
+    def some(body, start, step):
+        def run(i, carry):
+            t = start + i * step
+            body(t, pl.ds(pl.multiple_of(t * TILE, TILE), TILE))
+            return carry
+
+        lax.fori_loop(0, 2, run, 0)
 
     def beside(t, rows):
         change = dot3(nhi[rows, :], nlo[rows, :], mhi[...], mlo[...])
-        change = change + dot3(chi[0, rows, :], clo[0, rows, :], xhi[...], xlo[...], ((1,), (1,)))
+        change = change + dot3(chi[0, rows, :], clo[0, rows, :], thi[...], tlo[...])
         x = jnp.where(live(t, cs_in), nf[rows, :] - 0.5 * change, 0.0)
         nhi[rows, :], nlo[rows, :] = split(x)
 
+    def last(t, rows):
+        out[rows, :] = updated(1, t, rows)
+
+    wait_halo(0)
+    images(0)
+    gram(0)
+    send(gp.at[0, other_part], gsib.at[0], 0, GSIB, sibling)
+    scatter_gram(0)
+    take_rows()
+    cross_round(0)
+    own_gram(0)
+    pl.when(high)(lambda: scatter_cross(0))
+    send_cross(0)
+    own_cross(0)
+    pass_gram(0, True)
+    pass_cross(0)
+    take_gram(0)
+    take_cross(0)
+    some(first, 0, 3)
+    send_halo(1)
+    some(first, 1, 1)
+    pass_side(0)
+    pl.when(jnp.logical_and(low, has_side))(lambda: cross_turned(0, thi, tlo))
+    pl.when(jnp.logical_and(high, has_side))(lambda: cross_plain(0, thi, tlo))
+    take_side(0)
     pl.when(has_side)(lambda: tiles(beside))
 
     wait_halo(1)
     images(1)
     gram(1)
-    send(gp.at[1, other_half], gsib.at[1], 1, GSIB, sibling)
+    send(gp.at[1, other_part], gsib.at[1], 1, GSIB, sibling)
     cross_round(1)
     scatter_gram(1)
     pl.when(high)(lambda: scatter_cross(1))
     send_cross(1)
-    own_gram(1, False)
+    own_gram(1)
     own_cross(1)
-    pass_gram(1)
+    pass_gram(1, False)
     pass_cross(1)
     take_gram(1)
     take_cross(1)
-
-    def last(t, rows):
-        out[rows, :] = updated(1, t, rows)
-
     tiles(last)
 
     for src, it, index, cond in sent:
@@ -573,23 +616,24 @@
         vm((ROWS, ORBS), F32), vm((2, 640, ORBS), BF), vm((2, ROWS, ORBS), BF),
         vm((ROWS, ORBS), F32), vm((ROWS, ORBS), BF), vm((ROWS, ORBS), BF),
         vm((ROWS, ORBS), BF), vm((ROWS, ORBS), BF), vm((ROWS, 640), BF),
-        vm((2, ORBS, ORBS), F32), vm((2, ORBS, ORBS), F32),
+        vm((2, PACKED, TILE), F32), vm((2, ORBS, ORBS), F32),
         vm((ROWS, ORBS), I16), vm((ROWS, ORBS), I16), vm((8, ORBS), F32), vm((8, ORBS), F32),
         vm((576, 128), BF), vm((576, 128), BF), vm((576, 128), BF),
-        vm((2, HALF, ORBS), F32), vm((2, HALF, ORBS), F32),
-        vm((2, 8, GP, ORBS), I16), vm((2, 8, GP, ORBS), I16), vm((2, 8, 128), F32), vm((2, 8, 8, 128), F32),
+        vm((2, PHALF, TILE), F32), vm((2, HALF, ORBS), F32),
+        vm((2, 8, GP, TILE), I16), vm((2, 8, GP, TILE), I16), vm((2, 8, 128), F32), vm((2, 8, 8, 128), F32),
         vm((2, 4, HP, ORBS), I16), vm((2, 4, HP, ORBS), I16), vm((2, 8, 128), F32), vm((2, 4, 8, 128), F32),
-        vm((2, ORBS, ORBS), I16), vm((2, 16, 8, 128), F32), vm(square, I16), vm((16, 8, 128), F32),
+        vm((2, PACKED, TILE), I16), vm((2, 16, 8, 128), F32), vm((PACKED, TILE), I16), vm((16, 8, 128), F32),
         vm((2, ORBS, ORBS), I16), vm((2, 8, 8, 128), F32),
         vm(square, BF), vm(square, BF), vm(square, BF), vm(square, BF), vm(square, BF), vm(square, BF),
-        pltpu.SemaphoreType.DMA((2, COUNT)), pltpu.SemaphoreType.DMA((2, COUNT)), pltpu.SemaphoreType.DMA((2,)),
+        vm(square, BF), vm(square, BF), vm((PACKED, TILE), F32),
+        pltpu.SemaphoreType.DMA((2, COUNT)), pltpu.SemaphoreType.DMA((2, COUNT)), pltpu.SemaphoreType.DMA((6,)),
     ]
     result = pl.pallas_call(
         kernel,
         out_shape=jax.ShapeDtypeStruct((ROWS, ORBS), F32),
         in_specs=[
-            pl.BlockSpec(memory_space=pltpu.VMEM),
-            pl.BlockSpec(memory_space=pl.ANY),
+            pl.BlockSpec(memory_space=pltpu.HBM),
+            pl.BlockSpec(memory_space=pltpu.HBM),
             pl.BlockSpec(memory_space=pltpu.SMEM),
             pl.BlockSpec(memory_space=pltpu.SMEM),
         ],

time: 136 us -> 123 us (0.904)
  the two profiles are of different devices: /device:TPU:25 before, /device:TPU:59 now
where the time goes in v2:
time: 123 us; the launch traced here: 122 us
  Pallas kernels  118 us (96%)
  local copies, waits for them, and re-layouts  4.09 us (3%)
    pallas_call x1, Pallas kernels, per_device(): pl.pallas_call(kernel, out_shape=jax.ShapeDtypeStruct((ROWS, ORBS), F32),...  118 us
    unnamed x9, local copies, waits for them, and re-layouts  4.09 us

profile of v2, /device:TPU:59, one launch (start us, length us, event | category | flops | bytes accessed | tf_op | source)
XLA Modules:
  0.0 122.5 jit_solution(436814917416784691)
XLA Ops:
  0.0 0.0 copy-start.3
  0.0 0.0 copy-start.2
  0.0 0.7 copy-done.3
  0.7 0.0 copy-done.2
  0.7 0.0 copy-start
  0.7 1.2 copy-done
  1.9 0.0 copy-start.1
  1.9 1.2 copy-done.1
  3.1 118.4 %shard_map.46 = f32[512,512]{1,0:T(8,128)S(1)} custom-call(f32[512,512]{1,0:T(8,128)S(1)} %bitcast.3, bf16[4096,128]{1,0:T(8,128)(2,1)S(1)} %copy-done.1, s32[64]{0:T(128)S(1)} %copy-done.2, s32[8]{0:T(128)S(1)} %copy-done.3), custom_call_target="tpu_custom_call" | custom-call | tf_op jit(solution)/shard_map/pallas_call | solution.py:631
  121.5 1.0 copy.6
Async XLA Ops:
  0.0 0.7 copy-start.3
  0.0 0.7 copy-start.2
  0.7 1.2 copy-start
  1.9 1.2 copy-start.1

commit v3 on v2

--- a/solution.py
+++ b/solution.py
@@ -25,13 +25,18 @@
 F32 = jnp.float32
 I16 = jnp.int16
 
-HALO_NEXT, HALO_PREV, GSIB, HSIB = 0, 1, 2, 3
-RS, RSC, HRS, HRSC = 4, 12, 20, 24
-EA, EAS, NA, NAS = 28, 36, 44, 52
-HA, HAS, HL, HLS = 60, 64, 68, 72
-FE, FES, FN, FNS, FH, FHS = 76, 77, 78, 79, 80, 82
-NX, NXC, MET, HN, HNS = 84, 85, 86, 87, 88
-COUNT = 89
+HALO_NEXT, HALO_PREV, GSIB, RS, RSC, EA, EAS, NA, NAS = 0, 1, 2, 3, 11, 19, 27, 35, 36
+FE, FES, FN, FNS, NXC, MET = 37, 38, 39, 40, 41, 42
+CHUNKS = 2
+WIDE = ORBS // CHUNKS
+HSIB, HRS, HRSC, HA, HAS, HL, HLS, HN, HNS, FH, FHS, NX = 0, 1, 5, 9, 13, 17, 19, 21, 23, 25, 27, 29
+CHUNK_COUNT = 30
+COUNT = 43 + CHUNKS * CHUNK_COUNT
+
+
+def of(ch, index):
+    return 43 + ch * CHUNK_COUNT + index
+
 
 KEPT = [(a, b) for a in range(4) for b in range(a, 4)]
 
@@ -142,7 +147,9 @@
         hi, lo = split(x)
         chi[0, rows, :] = hi
         clo[0, rows, :] = lo
-        nq_out[rows, :] = jnp.round(jnp.clip(x, -CMAX, CMAX) * (QMAX / CMAX)).astype(I16)
+        coded = jnp.round(jnp.clip(x, -CMAX, CMAX) * (QMAX / CMAX)).astype(I16)
+        for ch in range(CHUNKS):
+            nq_out[ch, rows, :] = coded[:, ch * WIDE : ch * WIDE + WIDE]
 
     for t in range(4):
         loads[t].wait()
@@ -204,8 +211,12 @@
     send(meff, mrecv, 0, MET, dev(b, o - 1, r), gives_metric)
     send_halo(0)
     partner = dev(jnp.where(low, b + 4, b - 4), side, r)
-    send(nq_out, nq_in, 0, NX, partner, has_side)
     send(cs_own, cs_in, 0, NXC, partner, has_side)
+
+    def send_rows(ch):
+        send(nq_out.at[ch], nq_in.at[ch], 0, of(ch, NX), partner, has_side)
+
+    send_rows(0)
 
     @pl.when(low)
     def _():
@@ -247,10 +258,15 @@
 
     def images(it):
         def body(t, rows):
-            y = dot(band[rows, :], chi[it]) + dot(band[rows, 0:512], clo[it])
-            yhi[rows, :], ylo[rows, :] = split(y)
+            yhi[rows, :], ylo[rows, :] = split(dot(band[rows, 0:512], chi[it, 0:512]) + dot(band[rows, 0:512], clo[it]))
 
         tiles(body)
+
+    def edges(it):
+        wait_halo(it)
+        for rows in (slice(0, 64), slice(448, 512)):
+            y = yhi[rows, :].astype(F32) + ylo[rows, :].astype(F32)
+            yhi[rows, :], ylo[rows, :] = split(y + dot(band[rows, 512:640], chi[it, 512:640]))
 
     def gram(it):
         for a in range(4):
@@ -261,9 +277,11 @@
                 k = KEPT.index((a, e))
                 gp[it, k * TILE : k * TILE + TILE, :] = g[:, (e - a) * TILE : (e - a) * TILE + TILE]
 
-    def cross(it):
+    def cross(it, ch):
+        wide = slice(ch * WIDE, ch * WIDE + WIDE)
+
         def body(t, cols):
-            hp[it, cols, :] = dot3(yhi[:, cols], ylo[:, cols], nhi[...], nlo[...], ((0,), (0,)))
+            hp[it, ch, cols, :] = dot3(yhi[:, cols], ylo[:, cols], nhi[:, wide], nlo[:, wide], ((0,), (0,)))
 
         tiles(body)
 
@@ -272,23 +290,23 @@
     own_part = pl.ds(pl.multiple_of(core * PHALF, PHALF), PHALF)
     other_part = pl.ds(pl.multiple_of((1 - core) * PHALF, PHALF), PHALF)
 
-    def pair_and_pack(it, part, from_pair, packed, scale, size, count):
-        half, wide = size * count, part.shape[2]
+    def pair_and_pack(part, from_pair, packed, scale, size, count):
+        half, wide = size * count, part.shape[1]
 
         def add(i, top_value):
             rows = pl.ds(pl.multiple_of(core * half + i * size, size), size)
-            x = part[it, rows, :] + from_pair[it, pl.ds(pl.multiple_of(i * size, size), size), :]
-            part[it, rows, :] = x
+            x = part[rows, :] + from_pair[pl.ds(pl.multiple_of(i * size, size), size), :]
+            part[rows, :] = x
             return jnp.maximum(top_value, jnp.abs(x))
 
         peak = jnp.max(lax.fori_loop(0, count, add, jnp.zeros((size, wide), F32)), axis=(0, 1), keepdims=True)
         peak = jnp.maximum(peak, 1e-30)
-        scale[it] = jnp.broadcast_to(peak * (1.0 / QMAX), (8, 128))
+        scale[...] = jnp.broadcast_to(peak * (1.0 / QMAX), (8, 128))
         inv = QMAX / peak
 
         def pack(i, carry):
             rows = pl.ds(pl.multiple_of(core * half + i * size, size), size)
-            packed[it, i] = jnp.round(part[it, rows, :] * inv).astype(I16)
+            packed[i] = jnp.round(part[rows, :] * inv).astype(I16)
             return carry
 
         lax.fori_loop(0, count, pack, 0)
@@ -299,27 +317,28 @@
 
     def scatter_gram(it):
         arrived(gsib.at[it], it, GSIB)
-        pair_and_pack(it, gp, gsib, qs, qsc, GP, 8)
+        pair_and_pack(gp.at[it], gsib.at[it], qs.at[it], qsc.at[it], GP, 8)
         for k in range(1, 8):
             to = (z + k) % 8
             send(qs.at[it, to], rs.at[it, k], it, RS + k, zdev(to, o))
             send(qsc.at[it], rsc.at[it, k], it, RSC + k, zdev(to, o))
 
-    def scatter_cross(it):
-        arrived(hsib.at[it], it, HSIB)
-        pair_and_pack(it, hp, hsib, hqs, hqsc, HP, 4)
+    def scatter_cross(it, ch):
+        arrived(hsib.at[it, ch], it, of(ch, HSIB))
+        pair_and_pack(hp.at[it, ch], hsib.at[it, ch], hqs.at[it, ch], hqsc.at[it, ch], HP, 4)
 
     def high_peer(m):
         pz = zl if m % 2 == 0 else 5 - zl
         pr = r if m // 2 == 0 else 1 - r
         return pz, pr
 
-    def send_cross(it):
+    def send_cross(it, ch):
+        pl.when(high)(lambda: scatter_cross(it, ch))
         for m in range(1, 4):
             pz, pr = high_peer(m)
             device = dev(pz * 2 + core, o, pr)
-            send(hqs.at[it, pr * 2 + pz - 2], hrs.at[it, m], it, HRS + m, device, high)
-            send(hqsc.at[it], hrsc.at[it, m], it, HRSC + m, device, high)
+            send(hqs.at[it, ch, jnp.maximum(pr * 2 + pz - 2, 0)], hrs.at[it, ch, m], it, of(ch, HRS + m), device, high)
+            send(hqsc.at[it, ch], hrsc.at[it, ch, m], it, of(ch, HRSC + m), device, high)
 
     def own_gram(it):
         rows = pl.ds(pl.multiple_of(core * PHALF + z * GP, GP), GP)
@@ -343,30 +362,32 @@
             send(ea.at[it, rows], ea.at[it, rows], it, EA + k, device)
             send(es.at[it, at], es.at[it, at], it, EAS + k, device)
 
-    def own_cross(it):
-        rows = pl.ds(pl.multiple_of(core * HALF + j * HP, HP), HP)
-        at = core * 4 + j
+    def own_cross(it, ch):
+        rows = pl.ds(pl.multiple_of(core * HALF + jnp.maximum(j, 0) * HP, HP), HP)
+        at = core * 4 + jnp.maximum(j, 0)
         low_there = jnp.logical_and(high, o < groups - 1)
+        data, tags = ha.at[it, ch], hs.at[it, ch]
 
         @pl.when(high)
         def _():
-            total = hp[it, rows, :]
+            total = hp[it, ch, rows, :]
             for m in range(1, 4):
-                arrived(hrs.at[it, m], it, HRS + m)
-                arrived(hrsc.at[it, m], it, HRSC + m)
-                total = total + hrs[it, m].astype(jnp.int32).astype(F32) * hrsc[it, m, 0:1, 0:1]
+                arrived(hrs.at[it, ch, m], it, of(ch, HRS + m))
+                arrived(hrsc.at[it, ch, m], it, of(ch, HRSC + m))
+                total = total + hrs[it, ch, m].astype(jnp.int32).astype(F32) * hrsc[it, ch, m, 0:1, 0:1]
             value, scale = quantized(total * (1.0 / (SUPPORT * BLK)))
-            ha[it, rows, :] = value
-            hs[it, at] = scale
-
-        for m in range(1, 4):
+            ha[it, ch, rows, :] = value
+            hs[it, ch, at] = scale
+
+        for m in (3, 1):
             pz, pr = high_peer(m)
-            send(ha.at[it, rows], ha.at[it, rows], it, HA + m, dev(pz * 2 + core, o, pr), high)
-            send(hs.at[it, at], hs.at[it, at], it, HAS + m, dev(pz * 2 + core, o, pr), high)
+            send(data.at[rows], data.at[rows], it, of(ch, HA + m), dev(pz * 2 + core, o, pr), high)
+            send(tags.at[at], tags.at[at], it, of(ch, HAS + m), dev(pz * 2 + core, o, pr), high)
         for m in range(2):
             device = dev(2 + core, o + 1, r) if m == 0 else dev(core, o + 1, 1 - r)
-            send(ha.at[it, rows], ha.at[it, rows], it, HL + m, device, low_there, HL + jnp.maximum(zl - 2, 0))
-            send(hs.at[it, at], hs.at[it, at], it, HLS + m, device, low_there, HLS + jnp.maximum(zl - 2, 0))
+            mine = jnp.maximum(zl - 2, 0)
+            send(data.at[rows], data.at[rows], it, of(ch, HL + m), device, low_there, of(ch, HL + mine))
+            send(tags.at[at], tags.at[at], it, of(ch, HLS + m), device, low_there, of(ch, HLS + mine))
 
     own_eight = pl.ds(pl.multiple_of(core * 8, 8), 8)
     other_eight = pl.ds(pl.multiple_of((1 - core) * 8, 8), 8)
@@ -403,43 +424,39 @@
         send(na.at[own_part], na.at[own_part], it, FN, sibling, has_side)
         send(ns.at[own_eight], ns.at[own_eight], it, FNS, sibling, has_side)
 
-    def pass_cross(it):
+    def pass_cross(it, ch):
         cond = jnp.logical_or(high, has_side)
         low_side = jnp.logical_and(low, has_side)
-
-        def high_arrived(m):
-            pz, pr = high_peer(m)
-            at = core * 4 + pr * 2 + pz - 2
-            arrived(ha.at[it, piece(at, HP)], it, HA + m)
-            arrived(hs.at[it, at], it, HAS + m)
-
-        pl.when(high)(lambda: high_arrived(1))
-
-        @pl.when(low_side)
-        def _():
-            for m in range(2):
-                at = core * 4 + near * 2 + m
-                arrived(ha.at[it, piece(at, HP)], it, HL + m)
-                arrived(hs.at[it, at], it, HLS + m)
-
-        beside_low = dev((1 - zl) * 2 + core, o, r)
-        send(ha.at[it, near_rows], ha.at[it, near_rows], it, HN, beside_low, low_side)
-        send(hs.at[it, near_two], hs.at[it, near_two], it, HNS, beside_low, low_side)
-        send(ha.at[it, near_rows], ha.at[it, near_rows], it, FH, sibling, cond)
-        send(hs.at[it, near_two], hs.at[it, near_two], it, FHS, sibling, cond)
-
-        @pl.when(high)
-        def _():
-            high_arrived(2)
-            high_arrived(3)
-
-        @pl.when(low_side)
-        def _():
-            arrived(ha.at[it, far_rows], it, HN)
-            arrived(hs.at[it, far_two], it, HNS)
-
-        send(ha.at[it, far_rows], ha.at[it, far_rows], it, FH + 1, sibling, cond)
-        send(hs.at[it, far_two], hs.at[it, far_two], it, FHS + 1, sibling, cond)
+        data, tags = ha.at[it, ch], hs.at[it, ch]
+
+        def pass_on(at, index, device, ok):
+            rows = piece(at, HP)
+            send(data.at[rows], data.at[rows], it, of(ch, HN + index), device, ok)
+            send(tags.at[at], tags.at[at], it, of(ch, HNS + index), device, ok)
+
+        def taken(at, index, tag):
+            arrived(data.at[piece(at, HP)], it, of(ch, index))
+            arrived(tags.at[at], it, of(ch, tag))
+
+        def to_sibling(rows, two, index):
+            send(data.at[rows], data.at[rows], it, of(ch, FH + index), sibling, cond)
+            send(tags.at[two], tags.at[two], it, of(ch, FHS + index), sibling, cond)
+
+        base = core * 4
+        beside_low = dev(jnp.maximum(1 - zl, 0) * 2 + core, o, r)
+        for m in range(2):
+            at = base + near * 2 + m
+            pl.when(low_side)(functools.partial(taken, at, HL + m, HLS + m))
+            pass_on(at, m, beside_low, low_side)
+        pl.when(high)(lambda: taken(base + r * 2 + jnp.maximum(3 - zl, 0), HA + 1, HAS + 1))
+        to_sibling(near_rows, near_two, 0)
+        far_own = base + (1 - r) * 2 + jnp.maximum(3 - zl, 0)
+        pl.when(high)(lambda: taken(far_own, HA + 3, HAS + 3))
+        pass_on(far_own, 0, dev(jnp.minimum(5 - zl, 3) * 2 + core, o, r), high)
+        pl.when(high)(lambda: taken(base + (1 - r) * 2 + jnp.maximum(zl - 2, 0), HN, HNS))
+        for m in range(2):
+            pl.when(low_side)(functools.partial(taken, base + (1 - near) * 2 + m, HN + m, HNS + m))
+        to_sibling(far_rows, far_two, 1)
 
     def unpack(value, scale):
         return value.astype(jnp.int32).astype(F32) * scale[0:1, 0:1]
@@ -470,69 +487,81 @@
             arrived(ns.at[other_eight], it, FNS)
             spread(na, ns, mhi, mlo)
 
-    def cross_value(it, i):
-        return jnp.concatenate(
-            [unpack(ha[it, piece(2 * i, HP), :], hs[it, 2 * i]), unpack(ha[it, piece(2 * i + 1, HP), :], hs[it, 2 * i + 1])], axis=0
-        )
-
-    def cross_plain(it, to_hi, to_lo):
+    def cross_value(it, ch, i):
+        two = [unpack(ha[it, ch, piece(2 * i + e, HP), :], hs[it, ch, 2 * i + e]) for e in range(2)]
+        return jnp.concatenate(two, axis=0)
+
+    def cross_plain(it, ch, to_hi, to_lo):
+        wide = slice(ch * WIDE, ch * WIDE + WIDE)
+
         def body(i, carry):
             rows = piece(i, TILE)
-            to_hi[rows, :], to_lo[rows, :] = split(cross_value(it, i))
+            to_hi[rows, wide], to_lo[rows, wide] = split(cross_value(it, ch, i))
             return carry
 
         lax.fori_loop(0, 4, body, 0)
 
-    def cross_turned(it, to_hi, to_lo):
+    def cross_turned(it, ch, to_hi, to_lo):
+        wide = slice(ch * WIDE, ch * WIDE + WIDE)
+
         def body(i, carry):
             cols = piece(i, TILE)
-            to_hi[:, cols], to_lo[:, cols] = split(cross_value(it, i).T)
+            to_hi[wide, cols], to_lo[wide, cols] = split(cross_value(it, ch, i).T)
             return carry
 
         lax.fori_loop(0, 4, body, 0)
 
-    def take_cross(it):
+    def take_cross(it, ch):
+        data, tags = ha.at[it, ch], hs.at[it, ch]
+
         @pl.when(jnp.logical_or(high, has_side))
         def _():
-            arrived(ha.at[it, pair_near_rows], it, FH)
-            arrived(hs.at[it, pair_near_two], it, FHS)
-            arrived(ha.at[it, pair_far_rows], it, FH + 1)
-            arrived(hs.at[it, pair_far_two], it, FHS + 1)
-
-        pl.when(jnp.logical_and(low, has_side))(lambda: cross_plain(it, xhi, xlo))
-        pl.when(jnp.logical_and(high, has_side))(lambda: cross_turned(it, xhi, xlo))
-
-        @pl.when(jnp.logical_not(has_side))
-        def _():
-            xhi[...] = jnp.zeros((ORBS, ORBS), BF)
-            xlo[...] = jnp.zeros((ORBS, ORBS), BF)
+            arrived(data.at[pair_near_rows], it, of(ch, FH))
+            arrived(tags.at[pair_near_two], it, of(ch, FHS))
+            arrived(data.at[pair_far_rows], it, of(ch, FH + 1))
+            arrived(tags.at[pair_far_two], it, of(ch, FHS + 1))
+
+        pl.when(jnp.logical_and(low, has_side))(lambda: cross_plain(it, ch, xhi, xlo))
+        pl.when(jnp.logical_and(high, has_side))(lambda: cross_turned(it, ch, xhi, xlo))
+
+        if ch == 0:
+
+            @pl.when(jnp.logical_not(has_side))
+            def _():
+                xhi[...] = jnp.zeros((ORBS, ORBS), BF)
+                xlo[...] = jnp.zeros((ORBS, ORBS), BF)
 
     def updated(it, t, rows):
         change = dot3(chi[it, rows, :], clo[it, rows, :], ehi[...], elo[...])
         change = change + dot3(nhi[rows, :], nlo[rows, :], xhi[...], xlo[...])
         return jnp.where(live(t, cs_own), c[rows, :] - 0.5 * change, 0.0)
 
-    def take_rows():
+    def take_rows(ch):
+        wide = slice(ch * WIDE, ch * WIDE + WIDE)
+
         @pl.when(has_side)
         def _():
-            arrived(nq_in, 0, NX)
-            arrived(cs_in, 0, NXC)
+            arrived(nq_in.at[ch], 0, of(ch, NX))
 
             def body(t, rows):
-                x = nq_in[rows, :].astype(jnp.int32).astype(F32) * (CMAX / QMAX)
-                nf[rows, :] = x
-                nhi[rows, :], nlo[rows, :] = split(x)
+                x = nq_in[ch, rows, :].astype(jnp.int32).astype(F32) * (CMAX / QMAX)
+                nf[rows, wide] = x
+                nhi[rows, wide], nlo[rows, wide] = split(x)
 
             tiles(body)
 
         @pl.when(jnp.logical_not(has_side))
         def _():
-            nhi[...] = jnp.zeros((ROWS, ORBS), BF)
-            nlo[...] = jnp.zeros((ROWS, ORBS), BF)
-
-    def cross_round(it):
-        pl.when(high)(lambda: cross(it))
-        send(hp.at[it, other_half], hsib.at[it], it, HSIB, sibling, high)
+            nhi[:, wide] = jnp.zeros((ROWS, WIDE), BF)
+            nlo[:, wide] = jnp.zeros((ROWS, WIDE), BF)
+
+    def cross_round(it, ch):
+        pl.when(high)(lambda: cross(it, ch))
+        send(hp.at[it, ch, other_half], hsib.at[it, ch], it, of(ch, HSIB), sibling, high)
+
+    def turned_side(ch):
+        pl.when(jnp.logical_and(low, has_side))(lambda: cross_turned(0, ch, thi, tlo))
+        pl.when(jnp.logical_and(high, has_side))(lambda: cross_plain(0, ch, thi, tlo))
 
     def first(t, rows):
         x = updated(0, t, rows)
@@ -558,44 +587,55 @@
     def last(t, rows):
         out[rows, :] = updated(1, t, rows)
 
-    wait_halo(0)
     images(0)
+    edges(0)
     gram(0)
     send(gp.at[0, other_part], gsib.at[0], 0, GSIB, sibling)
     scatter_gram(0)
-    take_rows()
-    cross_round(0)
+    send_rows(1)
+    take_rows(0)
+    cross_round(0, 0)
     own_gram(0)
-    pl.when(high)(lambda: scatter_cross(0))
-    send_cross(0)
-    own_cross(0)
+    send_cross(0, 0)
     pass_gram(0, True)
-    pass_cross(0)
+    own_cross(0, 0)
     take_gram(0)
-    take_cross(0)
+    pass_cross(0, 0)
+    take_rows(1)
+    cross_round(0, 1)
+    take_cross(0, 0)
+    send_cross(0, 1)
+    pass_side(0)
+    own_cross(0, 1)
+    turned_side(0)
+    pass_cross(0, 1)
+    take_cross(0, 1)
     some(first, 0, 3)
     send_halo(1)
     some(first, 1, 1)
-    pass_side(0)
-    pl.when(jnp.logical_and(low, has_side))(lambda: cross_turned(0, thi, tlo))
-    pl.when(jnp.logical_and(high, has_side))(lambda: cross_plain(0, thi, tlo))
+    pl.when(has_side)(lambda: arrived(cs_in, 0, NXC))
+    turned_side(1)
     take_side(0)
     pl.when(has_side)(lambda: tiles(beside))
 
-    wait_halo(1)
     images(1)
+    edges(1)
     gram(1)
     send(gp.at[1, other_part], gsib.at[1], 1, GSIB, sibling)
-    cross_round(1)
+    cross_round(1, 0)
     scatter_gram(1)
-    pl.when(high)(lambda: scatter_cross(1))
-    send_cross(1)
+    cross_round(1, 1)
+    send_cross(1, 0)
     own_gram(1)
-    own_cross(1)
+    send_cross(1, 1)
+    own_cross(1, 0)
     pass_gram(1, False)
-    pass_cross(1)
+    own_cross(1, 1)
+    pass_cross(1, 0)
     take_gram(1)
-    take_cross(1)
+    pass_cross(1, 1)
+    take_cross(1, 0)
+    take_cross(1, 1)
     tiles(last)
 
     for src, it, index, cond in sent:
@@ -616,14 +656,14 @@
         vm((ROWS, ORBS), F32), vm((2, 640, ORBS), BF), vm((2, ROWS, ORBS), BF),
         vm((ROWS, ORBS), F32), vm((ROWS, ORBS), BF), vm((ROWS, ORBS), BF),
         vm((ROWS, ORBS), BF), vm((ROWS, ORBS), BF), vm((ROWS, 640), BF),
-        vm((2, PACKED, TILE), F32), vm((2, ORBS, ORBS), F32),
-        vm((ROWS, ORBS), I16), vm((ROWS, ORBS), I16), vm((8, ORBS), F32), vm((8, ORBS), F32),
+        vm((2, PACKED, TILE), F32), vm((2, CHUNKS, ORBS, WIDE), F32),
+        vm((CHUNKS, ROWS, WIDE), I16), vm((CHUNKS, ROWS, WIDE), I16), vm((8, ORBS), F32), vm((8, ORBS), F32),
         vm((576, 128), BF), vm((576, 128), BF), vm((576, 128), BF),
-        vm((2, PHALF, TILE), F32), vm((2, HALF, ORBS), F32),
+        vm((2, PHALF, TILE), F32), vm((2, CHUNKS, HALF, WIDE), F32),
         vm((2, 8, GP, TILE), I16), vm((2, 8, GP, TILE), I16), vm((2, 8, 128), F32), vm((2, 8, 8, 128), F32),
-        vm((2, 4, HP, ORBS), I16), vm((2, 4, HP, ORBS), I16), vm((2, 8, 128), F32), vm((2, 4, 8, 128), F32),
+        vm((2, CHUNKS, 4, HP, WIDE), I16), vm((2, CHUNKS, 4, HP, WIDE), I16), vm((2, CHUNKS, 8, 128), F32), vm((2, CHUNKS, 4, 8, 128), F32),
         vm((2, PACKED, TILE), I16), vm((2, 16, 8, 128), F32), vm((PACKED, TILE), I16), vm((16, 8, 128), F32),
-        vm((2, ORBS, ORBS), I16), vm((2, 8, 8, 128), F32),
+        vm((2, CHUNKS, ORBS, WIDE), I16), vm((2, CHUNKS, 8, 8, 128), F32),
         vm(square, BF), vm(square, BF), vm(square, BF), vm(square, BF), vm(square, BF), vm(square, BF),
         vm(square, BF), vm(square, BF), vm((PACKED, TILE), F32),
         pltpu.SemaphoreType.DMA((2, COUNT)), pltpu.SemaphoreType.DMA((2, COUNT)), pltpu.SemaphoreType.DMA((6,)),

time: 123 us -> 128 us (1.041)
  the two profiles are of different devices: /device:TPU:59 before, /device:TPU:25 now
where the time goes in v3:
time: 128 us
  Pallas kernels  124 us (97%)
  local copies, waits for them, and re-layouts  4.09 us (3%)
    pallas_call x1, Pallas kernels, per_device(): pl.pallas_call(kernel, out_shape=jax.ShapeDtypeStruct((ROWS, ORBS), F32),...  124 us
    unnamed x9, local copies, waits for them, and re-layouts  4.09 us

profile of v3, /device:TPU:25, one launch (start us, length us, event | category | flops | bytes accessed | tf_op | source)
XLA Modules:
  0.0 127.7 jit_solution(9242297611210043060)
XLA Ops:
  0.0 0.0 copy-start.3
  0.0 0.0 copy-start.2
  0.0 0.7 copy-done.3
  0.7 0.0 copy-done.2
  0.7 0.0 copy-start
  0.7 1.2 copy-done
  1.9 0.0 copy-start.1
  1.9 1.2 copy-done.1
  3.1 123.6 %shard_map.46 = f32[512,512]{1,0:T(8,128)S(1)} custom-call(f32[512,512]{1,0:T(8,128)S(1)} %bitcast.3, bf16[4096,128]{1,0:T(8,128)(2,1)S(1)} %copy-done.1, s32[64]{0:T(128)S(1)} %copy-done.2, s32[8]{0:T(128)S(1)} %copy-done.3), custom_call_target="tpu_custom_call" | custom-call | tf_op jit(solution)/shard_map/pallas_call | solution.py:671
  126.7 1.0 copy.6
Async XLA Ops:
  0.0 0.7 copy-start.3
  0.0 0.7 copy-start.2
  0.7 1.2 copy-start
  1.9 1.2 copy-start.1

commit v4 on v2

--- a/solution.py
+++ b/solution.py
@@ -30,8 +30,8 @@
 EA, EAS, NA, NAS = 28, 36, 44, 52
 HA, HAS, HL, HLS = 60, 64, 68, 72
 FE, FES, FN, FNS, FH, FHS = 76, 77, 78, 79, 80, 82
-NX, NXC, MET, HN, HNS = 84, 85, 86, 87, 88
-COUNT = 89
+NX, NXC, MET = 84, 88, 89
+COUNT = 90
 
 KEPT = [(a, b) for a in range(4) for b in range(a, 4)]
 
@@ -108,8 +108,8 @@
     loads = [
         pltpu.make_async_copy(coef.at[pl.ds(t * TILE, TILE)], c.at[pl.ds(t * TILE, TILE)], local_sem.at[2 + t]) for t in range(4)
     ]
-    for load in loads:
-        load.start()
+    for t in (0, 3, 1, 2):
+        loads[t].start()
     load_main = pltpu.make_async_copy(metric.at[pl.ds(pl.multiple_of(q * 512, 64), 512)], meff.at[pl.ds(0, 512)], local_sem.at[0])
     load_prev = pltpu.make_async_copy(
         metric.at[pl.ds(pl.multiple_of((q * 512 + 4032) % 4096, 64), 64)], meff.at[pl.ds(512, 64)], local_sem.at[1]
@@ -144,10 +144,12 @@
         clo[0, rows, :] = lo
         nq_out[rows, :] = jnp.round(jnp.clip(x, -CMAX, CMAX) * (QMAX / CMAX)).astype(I16)
 
-    for t in range(4):
+    def prepare_tile(t):
         loads[t].wait()
         prepare(jnp.int32(t), pl.ds(t * TILE, TILE))
 
+    prepare_tile(0)
+    prepare_tile(3)
     for it in range(ITERS):
 
         @pl.when(p == 0)
@@ -204,7 +206,11 @@
     send(meff, mrecv, 0, MET, dev(b, o - 1, r), gives_metric)
     send_halo(0)
     partner = dev(jnp.where(low, b + 4, b - 4), side, r)
-    send(nq_out, nq_in, 0, NX, partner, has_side)
+    for t in (0, 3, 1, 2):
+        if t in (1, 2):
+            prepare_tile(t)
+        rows = pl.ds(t * TILE, TILE)
+        send(nq_out.at[rows], nq_in.at[rows], 0, NX + t, partner, has_side)
     send(cs_own, cs_in, 0, NXC, partner, has_side)
 
     @pl.when(low)
@@ -247,10 +253,15 @@
 
     def images(it):
         def body(t, rows):
-            y = dot(band[rows, :], chi[it]) + dot(band[rows, 0:512], clo[it])
-            yhi[rows, :], ylo[rows, :] = split(y)
+            yhi[rows, :], ylo[rows, :] = split(dot(band[rows, 0:512], chi[it, 0:512]) + dot(band[rows, 0:512], clo[it]))
 
         tiles(body)
+
+    def edges(it):
+        wait_halo(it)
+        for rows in (slice(0, 64), slice(448, 512)):
+            y = yhi[rows, :].astype(F32) + ylo[rows, :].astype(F32)
+            yhi[rows, :], ylo[rows, :] = split(y + dot(band[rows, 512:640], chi[it, 512:640]))
 
     def gram(it):
         for a in range(4):
@@ -264,6 +275,13 @@
     def cross(it):
         def body(t, cols):
             hp[it, cols, :] = dot3(yhi[:, cols], ylo[:, cols], nhi[...], nlo[...], ((0,), (0,)))
+
+        tiles(body)
+
+    def cross_rows(it, rows, begin):
+        def body(t, cols):
+            more = dot3(yhi[rows, cols], ylo[rows, cols], nhi[rows, :], nlo[rows, :], ((0,), (0,)))
+            hp[it, cols, :] = more if begin else hp[it, cols, :] + more
 
         tiles(body)
 
@@ -344,8 +362,8 @@
             send(es.at[it, at], es.at[it, at], it, EAS + k, device)
 
     def own_cross(it):
-        rows = pl.ds(pl.multiple_of(core * HALF + j * HP, HP), HP)
-        at = core * 4 + j
+        rows = pl.ds(pl.multiple_of(core * HALF + jnp.maximum(j, 0) * HP, HP), HP)
+        at = core * 4 + jnp.maximum(j, 0)
         low_there = jnp.logical_and(high, o < groups - 1)
 
         @pl.when(high)
@@ -363,10 +381,11 @@
             pz, pr = high_peer(m)
             send(ha.at[it, rows], ha.at[it, rows], it, HA + m, dev(pz * 2 + core, o, pr), high)
             send(hs.at[it, at], hs.at[it, at], it, HAS + m, dev(pz * 2 + core, o, pr), high)
-        for m in range(2):
-            device = dev(2 + core, o + 1, r) if m == 0 else dev(core, o + 1, 1 - r)
-            send(ha.at[it, rows], ha.at[it, rows], it, HL + m, device, low_there, HL + jnp.maximum(zl - 2, 0))
-            send(hs.at[it, at], hs.at[it, at], it, HLS + m, device, low_there, HLS + jnp.maximum(zl - 2, 0))
+        mine = jnp.maximum(j, 0)
+        for m in range(4):
+            device = dev((m // 2) * 2 + core, o + 1, m % 2)
+            send(ha.at[it, rows], ha.at[it, rows], it, HL + m, device, low_there, HL + mine)
+            send(hs.at[it, at], hs.at[it, at], it, HLS + m, device, low_there, HLS + mine)
 
     own_eight = pl.ds(pl.multiple_of(core * 8, 8), 8)
     other_eight = pl.ds(pl.multiple_of((1 - core) * 8, 8), 8)
@@ -406,40 +425,31 @@
     def pass_cross(it):
         cond = jnp.logical_or(high, has_side)
         low_side = jnp.logical_and(low, has_side)
+        data, tags = ha.at[it], hs.at[it]
 
         def high_arrived(m):
             pz, pr = high_peer(m)
             at = core * 4 + pr * 2 + pz - 2
-            arrived(ha.at[it, piece(at, HP)], it, HA + m)
-            arrived(hs.at[it, at], it, HAS + m)
+            arrived(data.at[piece(at, HP)], it, HA + m)
+            arrived(tags.at[at], it, HAS + m)
+
+        def low_arrived(e, m):
+            at = core * 4 + e * 2 + m
+            arrived(data.at[piece(at, HP)], it, HL + e * 2 + m)
+            arrived(tags.at[at], it, HLS + e * 2 + m)
+
+        def to_sibling(rows, two, index):
+            send(data.at[rows], data.at[rows], it, FH + index, sibling, cond)
+            send(tags.at[two], tags.at[two], it, FHS + index, sibling, cond)
 
         pl.when(high)(lambda: high_arrived(1))
-
-        @pl.when(low_side)
-        def _():
-            for m in range(2):
-                at = core * 4 + near * 2 + m
-                arrived(ha.at[it, piece(at, HP)], it, HL + m)
-                arrived(hs.at[it, at], it, HLS + m)
-
-        beside_low = dev((1 - zl) * 2 + core, o, r)
-        send(ha.at[it, near_rows], ha.at[it, near_rows], it, HN, beside_low, low_side)
-        send(hs.at[it, near_two], hs.at[it, near_two], it, HNS, beside_low, low_side)
-        send(ha.at[it, near_rows], ha.at[it, near_rows], it, FH, sibling, cond)
-        send(hs.at[it, near_two], hs.at[it, near_two], it, FHS, sibling, cond)
-
-        @pl.when(high)
-        def _():
-            high_arrived(2)
-            high_arrived(3)
-
-        @pl.when(low_side)
-        def _():
-            arrived(ha.at[it, far_rows], it, HN)
-            arrived(hs.at[it, far_two], it, HNS)
-
-        send(ha.at[it, far_rows], ha.at[it, far_rows], it, FH + 1, sibling, cond)
-        send(hs.at[it, far_two], hs.at[it, far_two], it, FHS + 1, sibling, cond)
+        for m in range(2):
+            pl.when(low_side)(functools.partial(low_arrived, near, m))
+        to_sibling(near_rows, near_two, 0)
+        for m in range(2):
+            pl.when(high)(functools.partial(high_arrived, m + 2))
+            pl.when(low_side)(functools.partial(low_arrived, 1 - near, m))
+        to_sibling(far_rows, far_two, 1)
 
     def unpack(value, scale):
         return value.astype(jnp.int32).astype(F32) * scale[0:1, 0:1]
@@ -507,31 +517,35 @@
             xhi[...] = jnp.zeros((ORBS, ORBS), BF)
             xlo[...] = jnp.zeros((ORBS, ORBS), BF)
 
+    def own_change(it):
+        def body(t, rows):
+            c[rows, :] = c[rows, :] - 0.5 * dot3(chi[it, rows, :], clo[it, rows, :], ehi[...], elo[...])
+
+        tiles(body)
+
     def updated(it, t, rows):
-        change = dot3(chi[it, rows, :], clo[it, rows, :], ehi[...], elo[...])
-        change = change + dot3(nhi[rows, :], nlo[rows, :], xhi[...], xlo[...])
+        change = dot3(nhi[rows, :], nlo[rows, :], xhi[...], xlo[...])
         return jnp.where(live(t, cs_own), c[rows, :] - 0.5 * change, 0.0)
 
     def take_rows():
-        @pl.when(has_side)
-        def _():
-            arrived(nq_in, 0, NX)
-            arrived(cs_in, 0, NXC)
-
-            def body(t, rows):
+        for t in (0, 3, 1, 2):
+            rows = slice(t * TILE, t * TILE + TILE)
+
+            @pl.when(has_side)
+            def _():
+                arrived(nq_in.at[rows], 0, NX + t)
                 x = nq_in[rows, :].astype(jnp.int32).astype(F32) * (CMAX / QMAX)
                 nf[rows, :] = x
                 nhi[rows, :], nlo[rows, :] = split(x)
 
-            tiles(body)
-
-        @pl.when(jnp.logical_not(has_side))
-        def _():
-            nhi[...] = jnp.zeros((ROWS, ORBS), BF)
-            nlo[...] = jnp.zeros((ROWS, ORBS), BF)
-
-    def cross_round(it):
-        pl.when(high)(lambda: cross(it))
+            @pl.when(jnp.logical_not(has_side))
+            def _():
+                nhi[rows, :] = jnp.zeros((TILE, ORBS), BF)
+                nlo[rows, :] = jnp.zeros((TILE, ORBS), BF)
+
+            pl.when(high)(functools.partial(cross_rows, 0, rows, t == 0))
+
+    def pair_cross(it):
         send(hp.at[it, other_half], hsib.at[it], it, HSIB, sibling, high)
 
     def first(t, rows):
@@ -558,43 +572,47 @@
     def last(t, rows):
         out[rows, :] = updated(1, t, rows)
 
-    wait_halo(0)
     images(0)
+    edges(0)
     gram(0)
     send(gp.at[0, other_part], gsib.at[0], 0, GSIB, sibling)
     scatter_gram(0)
+    own_gram(0)
     take_rows()
-    cross_round(0)
-    own_gram(0)
+    pair_cross(0)
     pl.when(high)(lambda: scatter_cross(0))
     send_cross(0)
+    pass_gram(0, True)
+    take_gram(0)
+    own_change(0)
     own_cross(0)
-    pass_gram(0, True)
+    pass_side(0)
     pass_cross(0)
-    take_gram(0)
     take_cross(0)
     some(first, 0, 3)
     send_halo(1)
     some(first, 1, 1)
-    pass_side(0)
+    pl.when(has_side)(lambda: arrived(cs_in, 0, NXC))
     pl.when(jnp.logical_and(low, has_side))(lambda: cross_turned(0, thi, tlo))
     pl.when(jnp.logical_and(high, has_side))(lambda: cross_plain(0, thi, tlo))
     take_side(0)
     pl.when(has_side)(lambda: tiles(beside))
 
-    wait_halo(1)
     images(1)
+    edges(1)
     gram(1)
     send(gp.at[1, other_part], gsib.at[1], 1, GSIB, sibling)
-    cross_round(1)
+    pl.when(high)(lambda: cross(1))
+    pair_cross(1)
     scatter_gram(1)
     pl.when(high)(lambda: scatter_cross(1))
     send_cross(1)
     own_gram(1)
     own_cross(1)
     pass_gram(1, False)
+    take_gram(1)
+    own_change(1)
     pass_cross(1)
-    take_gram(1)
     take_cross(1)
     tiles(last)
 

time: 123 us -> 117 us (0.951)
  the two profiles are of different devices: /device:TPU:59 before, /device:TPU:25 now
where the time goes in v4:
time: 117 us; the launch traced here: 115 us
  Pallas kernels  111 us (95%)
  local copies, waits for them, and re-layouts  4.09 us (3%)
    pallas_call x1, Pallas kernels, per_device(): pl.pallas_call(kernel, out_shape=jax.ShapeDtypeStruct((ROWS, ORBS), F32),...  111 us
    unnamed x9, local copies, waits for them, and re-layouts  4.09 us

profile of v4, /device:TPU:25, one launch (start us, length us, event | category | flops | bytes accessed | tf_op | source)
XLA Modules:
  0.0 115.5 jit_solution(8679542194967312568)
XLA Ops:
  0.0 0.0 copy-start.3
  0.0 0.0 copy-start.2
  0.0 0.7 copy-done.3
  0.7 0.0 copy-done.2
  0.7 0.0 copy-start
  0.7 1.2 %copy-done = f32[1,512,512]{2,1,0:T(8,128)S(1)} copy-done((f32[1,512,512]{2,1,0:T(8,128)S(1)}, f32[1,512,512]{2,1,0:T(8,128)}, u32[]{:S(2)}) %copy-start) | copy-done | bytes 1048600
  1.9 0.0 copy-start.1
  1.9 1.2 %copy-done.1 = bf16[4096,128]{1,0:T(8,128)(2,1)S(1)} copy-done((bf16[4096,128]{1,0:T(8,128)(2,1)S(1)}, bf16[4096,128]{1,0:T(8,128)(2,1)}, u32[]{:S(2)}) %copy-start.1) | copy-done | bytes 1048600
  3.1 111.4 %shard_map.46 = f32[512,512]{1,0:T(8,128)S(1)} custom-call(f32[512,512]{1,0:T(8,128)S(1)} %bitcast.3, bf16[4096,128]{1,0:T(8,128)(2,1)S(1)} %copy-done.1, s32[64]{0:T(128)S(1)} %copy-done.2, s32[8]{0:T(128)S(1)} %copy-done.3), custom_call_target="tpu_custom_call" | custom-call | tf_op jit(solution)/shard_map/pallas_call | solution.py:649
  114.5 1.0 copy.6
Async XLA Ops:
  0.0 0.7 copy-start.3
  0.0 0.7 copy-start.2
  0.7 1.2 %copy-start = (f32[1,512,512]{2,1,0:T(8,128)S(1)}, f32[1,512,512]{2,1,0:T(8,128)}, u32[]{:S(2)}) copy-start(f32[1,512,512]{2,1,0:T(8,128)} %param.4) | copy-start | bytes 3145732
  1.9 1.2 %copy-start.1 = (bf16[4096,128]{1,0:T(8,128)(2,1)S(1)}, bf16[4096,128]{1,0:T(8,128)(2,1)}, u32[]{:S(2)}) copy-start(bf16[4096,128]{1,0:T(8,128)(2,1)} %metric.1) | copy-start | bytes 3145732

commit v5 on v4

--- a/solution.py
+++ b/solution.py
@@ -17,7 +17,7 @@
 GP = 80
 PACKED = 1280
 PHALF = 640
-HP = 64
+HP = 32
 TILE = 128
 CMAX = 6.0
 QMAX = 32767.0
@@ -25,13 +25,10 @@
 F32 = jnp.float32
 I16 = jnp.int16
 
-HALO_NEXT, HALO_PREV, GSIB, HSIB = 0, 1, 2, 3
-RS, RSC, HRS, HRSC = 4, 12, 20, 24
-EA, EAS, NA, NAS = 28, 36, 44, 52
-HA, HAS, HL, HLS = 60, 64, 68, 72
-FE, FES, FN, FNS, FH, FHS = 76, 77, 78, 79, 80, 82
-NX, NXC, MET = 84, 88, 89
-COUNT = 90
+HALO_NEXT, HALO_PREV, GSIB, HSIB, NA, NAS, FES, FN, FNS, FHS, NXC, MET = range(12)
+NX = 12
+RS, RSC, HRS, HRSC, EA, EAS, HA, HAS, FE, FH = range(16, 96, 8)
+COUNT = 96
 
 KEPT = [(a, b) for a in range(4) for b in range(a, 4)]
 
@@ -50,11 +47,11 @@
 
 
 def kernel(
-    coef, metric, pattern, starts, out,
+    coef, metric, pattern_in, starts_in, out,
     c, chi, clo, nf, nhi, nlo, yhi, ylo, band, gp, hp,
     nq_out, nq_in, cs_own, cs_in, meff, mrecv, msel,
     gsib, hsib, qs, rs, qsc, rsc, hqs, hrs, hqsc, hrsc,
-    ea, es, na, ns, ha, hs, ehi, elo, xhi, xlo, thi, tlo, mhi, mlo, ef,
+    ea, es, na, ns, ha, hs, ehi, elo, xhi, xlo, thi, tlo, mhi, mlo, ef, ho, hos, sums, dhi, dlo, pattern, starts,
     ss, rr, local_sem,
 ):
     b, o, r = lax.axis_index("basis"), lax.axis_index("orb"), lax.axis_index("rep")
@@ -69,7 +66,6 @@
     away = jnp.where(low, o + 1, o - 1)
     has_side = jnp.logical_and(side >= 0, side < groups)
     has_away = jnp.logical_and(away >= 0, away < groups)
-    j = r * 2 + zl - 2
 
     def dev(bb, oo, rep):
         return {"basis": bb, "orb": oo, "rep": rep}
@@ -94,20 +90,40 @@
     def _():
         greet(dev(step_b, o, 1 - r))
 
-    @pl.when(has_side)
-    def _():
-        base = jnp.where(low, 4, 0)
+    below = jnp.logical_and(low, o > 0)
+    above = o < groups - 1
+
+    @pl.when(below)
+    def _():
+        for k in range(8):
+            greet(zdev((z + k) % 8, o - 1))
+
+    @pl.when(above)
+    def _():
         for m in range(4):
-            greet(dev(base + (m % 2) * 2 + core, side, m // 2))
-        greet(dev(b, side, r))
-
-    @pl.when(has_away)
-    def _():
-        greet(dev(b, away, r))
+            greet(dev((m // 2) * 2 + core, o + 1, m % 2))
+
+    straight = jnp.logical_and(high, above)
+
+    @pl.when(straight)
+    def _():
+        greet(dev(b, o + 1, r))
+
+    straight_down = jnp.logical_and(high, o > 0)
+
+    @pl.when(straight_down)
+    def _():
+        greet(dev(b, o - 1, r))
 
     loads = [
         pltpu.make_async_copy(coef.at[pl.ds(t * TILE, TILE)], c.at[pl.ds(t * TILE, TILE)], local_sem.at[2 + t]) for t in range(4)
     ]
+    small = [
+        pltpu.make_async_copy(starts_in, starts, local_sem.at[6]),
+        pltpu.make_async_copy(pattern_in, pattern, local_sem.at[7]),
+    ]
+    for load in small:
+        load.start()
     for t in (0, 3, 1, 2):
         loads[t].start()
     load_main = pltpu.make_async_copy(metric.at[pl.ds(pl.multiple_of(q * 512, 64), 512)], meff.at[pl.ds(0, 512)], local_sem.at[0])
@@ -116,6 +132,8 @@
     )
     load_main.start()
     load_prev.start()
+    small[0].wait()
+    small[1].wait()
     lane = lax.broadcasted_iota(jnp.int32, (8, ORBS), 1) // BLK
     cs = jnp.zeros((8, ORBS), F32)
     for i in range(8):
@@ -152,7 +170,7 @@
     prepare_tile(3)
     for it in range(ITERS):
 
-        @pl.when(p == 0)
+        @pl.when(low)
         def _():
             chi[it, 512:576, :] = jnp.zeros((64, ORBS), BF)
 
@@ -169,8 +187,10 @@
         block = meff[i * 64 : i * 64 + 64, :].astype(F32)
         meff[i * 64 : i * 64 + 64, :] = jnp.where(right, block * keep, block).astype(BF)
 
-    waits = [jnp.int32(8), has_step.astype(jnp.int32), 5 * has_side.astype(jnp.int32), has_away.astype(jnp.int32)]
-    pl.semaphore_wait(barrier, waits[0] + waits[1] + waits[2] + waits[3])
+    def ones(flag):
+        return flag.astype(jnp.int32)
+
+    pl.semaphore_wait(barrier, 8 + ones(has_step) + 8 * ones(below) + 4 * ones(above) + ones(straight) + ones(straight_down))
 
     sent = []
 
@@ -196,11 +216,11 @@
         up_b = jnp.where(r == 0, b, b + 1)
         down_b = jnp.where(r == 1, b, b - 1)
         send(chi.at[it, pl.ds(0, 64)], chi.at[it, pl.ds(576, 64)], it, HALO_NEXT, dev(down_b, o, 1 - r), p > 0)
-        send(chi.at[it, pl.ds(448, 64)], chi.at[it, pl.ds(512, 64)], it, HALO_PREV, dev(up_b, o, 1 - r), p < 15)
+        send(chi.at[it, pl.ds(448, 64)], chi.at[it, pl.ds(512, 64)], it, HALO_PREV, dev(up_b, o, 1 - r), jnp.logical_and(p > 6, p < 15))
 
     def wait_halo(it):
         pl.when(p < 15)(lambda: arrived(chi.at[it, pl.ds(576, 64)], it, HALO_NEXT))
-        pl.when(p > 0)(lambda: arrived(chi.at[it, pl.ds(512, 64)], it, HALO_PREV))
+        pl.when(high)(lambda: arrived(chi.at[it, pl.ds(512, 64)], it, HALO_PREV))
 
     gives_metric = jnp.logical_and(high, o > 0)
     send(meff, mrecv, 0, MET, dev(b, o - 1, r), gives_metric)
@@ -261,7 +281,9 @@
         wait_halo(it)
         for rows in (slice(0, 64), slice(448, 512)):
             y = yhi[rows, :].astype(F32) + ylo[rows, :].astype(F32)
-            yhi[rows, :], ylo[rows, :] = split(y + dot(band[rows, 512:640], chi[it, 512:640]))
+            more = dot(band[rows, 512:640], chi[it, 512:640])
+            yhi[rows, :], ylo[rows, :] = split(y + more)
+        dhi[...], dlo[...] = split(more)
 
     def gram(it):
         for a in range(4):
@@ -272,6 +294,16 @@
                 k = KEPT.index((a, e))
                 gp[it, k * TILE : k * TILE + TILE, :] = g[:, (e - a) * TILE : (e - a) * TILE + TILE]
 
+        @pl.when(p < 7)
+        def _():
+            for a in range(4):
+                cols = slice(a * TILE, a * TILE + TILE)
+                rest = slice(a * TILE, ORBS)
+                g = dot3(dhi[:, cols], dlo[:, cols], chi[it, 448:512, rest], clo[it, 448:512, rest], ((0,), (0,)))
+                for e in range(a, 4):
+                    rows = slice(KEPT.index((a, e)) * TILE, KEPT.index((a, e)) * TILE + TILE)
+                    gp[it, rows, :] = gp[it, rows, :] + g[:, (e - a) * TILE : (e - a) * TILE + TILE]
+
     def cross(it):
         def body(t, cols):
             hp[it, cols, :] = dot3(yhi[:, cols], ylo[:, cols], nhi[...], nlo[...], ((0,), (0,)))
@@ -325,19 +357,16 @@
 
     def scatter_cross(it):
         arrived(hsib.at[it], it, HSIB)
-        pair_and_pack(it, hp, hsib, hqs, hqsc, HP, 4)
-
-    def high_peer(m):
-        pz = zl if m % 2 == 0 else 5 - zl
-        pr = r if m // 2 == 0 else 1 - r
-        return pz, pr
+        pair_and_pack(it, hp, hsib, hqs, hqsc, HP, 8)
+
+    def from_high(k):
+        return (z + 8 - k) % 4 >= 2
 
     def send_cross(it):
-        for m in range(1, 4):
-            pz, pr = high_peer(m)
-            device = dev(pz * 2 + core, o, pr)
-            send(hqs.at[it, pr * 2 + pz - 2], hrs.at[it, m], it, HRS + m, device, high)
-            send(hqsc.at[it], hrsc.at[it, m], it, HRSC + m, device, high)
+        for k in range(1, 8):
+            to = (z + k) % 8
+            send(hqs.at[it, to], hrs.at[it, k], it, HRS + k, zdev(to, o), high)
+            send(hqsc.at[it], hrsc.at[it, k], it, HRSC + k, zdev(to, o), high)
 
     def own_gram(it):
         rows = pl.ds(pl.multiple_of(core * PHALF + z * GP, GP), GP)
@@ -362,43 +391,46 @@
             send(es.at[it, at], es.at[it, at], it, EAS + k, device)
 
     def own_cross(it):
-        rows = pl.ds(pl.multiple_of(core * HALF + jnp.maximum(j, 0) * HP, HP), HP)
-        at = core * 4 + jnp.maximum(j, 0)
-        low_there = jnp.logical_and(high, o < groups - 1)
+        rows = pl.ds(pl.multiple_of(core * HALF + z * HP, HP), HP)
+        at = core * 8 + z
 
         @pl.when(high)
         def _():
-            total = hp[it, rows, :]
-            for m in range(1, 4):
-                arrived(hrs.at[it, m], it, HRS + m)
-                arrived(hrsc.at[it, m], it, HRSC + m)
-                total = total + hrs[it, m].astype(jnp.int32).astype(F32) * hrsc[it, m, 0:1, 0:1]
-            value, scale = quantized(total * (1.0 / (SUPPORT * BLK)))
+            sums[...] = hp[it, rows, :]
+
+        @pl.when(low)
+        def _():
+            sums[...] = jnp.zeros((HP, ORBS), F32)
+
+        for k in range(1, 8):
+
+            @pl.when(from_high(k))
+            def _():
+                arrived(hrs.at[it, k], it, HRS + k)
+                arrived(hrsc.at[it, k], it, HRSC + k)
+                sums[...] = sums[...] + hrs[it, k].astype(jnp.int32).astype(F32) * hrsc[it, k, 0:1, 0:1]
+
+        value, scale = quantized(sums[...] * (1.0 / (SUPPORT * BLK)))
+        ho[it] = value
+        hos[it] = scale
+
+        @pl.when(high)
+        def _():
             ha[it, rows, :] = value
             hs[it, at] = scale
 
-        for m in range(1, 4):
-            pz, pr = high_peer(m)
-            send(ha.at[it, rows], ha.at[it, rows], it, HA + m, dev(pz * 2 + core, o, pr), high)
-            send(hs.at[it, at], hs.at[it, at], it, HAS + m, dev(pz * 2 + core, o, pr), high)
-        mine = jnp.maximum(j, 0)
-        for m in range(4):
-            device = dev((m // 2) * 2 + core, o + 1, m % 2)
-            send(ha.at[it, rows], ha.at[it, rows], it, HL + m, device, low_there, HL + mine)
-            send(hs.at[it, at], hs.at[it, at], it, HLS + m, device, low_there, HLS + mine)
+        for k in range(8):
+            to = (z + k) % 8
+            to_low = to % 4 < 2
+            cond = jnp.logical_and(to_low, above)
+            if k > 0:
+                cond = jnp.logical_or(cond, to % 4 >= 2)
+            device = zdev(to, jnp.where(to_low, o + 1, o))
+            send(ho.at[it], ha.at[it, rows], it, HA + k, device, cond)
+            send(hos.at[it], hs.at[it, at], it, HAS + k, device, cond)
 
     own_eight = pl.ds(pl.multiple_of(core * 8, 8), 8)
     other_eight = pl.ds(pl.multiple_of((1 - core) * 8, 8), 8)
-    near = jnp.where(jnp.logical_and(low, zl == 0), 1 - r, r)
-    near_rows = pl.ds(pl.multiple_of(core * HALF + near * 128, 128), 128)
-    far_rows = pl.ds(pl.multiple_of(core * HALF + (1 - near) * 128, 128), 128)
-    near_two = pl.ds(core * 4 + near * 2, 2)
-    far_two = pl.ds(core * 4 + (1 - near) * 2, 2)
-    pair_near_rows = pl.ds(pl.multiple_of((1 - core) * HALF + near * 128, 128), 128)
-    pair_far_rows = pl.ds(pl.multiple_of((1 - core) * HALF + (1 - near) * 128, 128), 128)
-    pair_near_two = pl.ds((1 - core) * 4 + near * 2, 2)
-    pair_far_two = pl.ds((1 - core) * 4 + (1 - near) * 2, 2)
-
     def piece(at, size):
         return pl.ds(pl.multiple_of(at * size, size), size)
 
@@ -407,7 +439,9 @@
             at = core * 8 + (z + 8 - k) % 8
             arrived(ea.at[it, piece(at, GP)], it, EA + k)
             arrived(es.at[it, at], it, EAS + k)
-        send(ea.at[it, own_part], ea.at[it, own_part], it, FE, sibling)
+            send(ea.at[it, piece(at, GP)], ea.at[it, piece(at, GP)], it, FE + k, sibling)
+        mine = piece(core * 8 + z, GP)
+        send(ea.at[it, mine], ea.at[it, mine], it, FE, sibling)
         send(es.at[it, own_eight], es.at[it, own_eight], it, FES, sibling)
         if with_side:
             send(ea.at[it, own_part], na.at[own_part], it, NA, dev(b, away, r), has_away)
@@ -423,33 +457,18 @@
         send(ns.at[own_eight], ns.at[own_eight], it, FNS, sibling, has_side)
 
     def pass_cross(it):
-        cond = jnp.logical_or(high, has_side)
-        low_side = jnp.logical_and(low, has_side)
         data, tags = ha.at[it], hs.at[it]
-
-        def high_arrived(m):
-            pz, pr = high_peer(m)
-            at = core * 4 + pr * 2 + pz - 2
-            arrived(data.at[piece(at, HP)], it, HA + m)
-            arrived(tags.at[at], it, HAS + m)
-
-        def low_arrived(e, m):
-            at = core * 4 + e * 2 + m
-            arrived(data.at[piece(at, HP)], it, HL + e * 2 + m)
-            arrived(tags.at[at], it, HLS + e * 2 + m)
-
-        def to_sibling(rows, two, index):
-            send(data.at[rows], data.at[rows], it, FH + index, sibling, cond)
-            send(tags.at[two], tags.at[two], it, FHS + index, sibling, cond)
-
-        pl.when(high)(lambda: high_arrived(1))
-        for m in range(2):
-            pl.when(low_side)(functools.partial(low_arrived, near, m))
-        to_sibling(near_rows, near_two, 0)
-        for m in range(2):
-            pl.when(high)(functools.partial(high_arrived, m + 2))
-            pl.when(low_side)(functools.partial(low_arrived, 1 - near, m))
-        to_sibling(far_rows, far_two, 1)
+        takes = jnp.logical_or(high, has_side)
+        for k in range(8):
+            at = core * 8 + (z + 8 - k) % 8
+
+            def taken(at=at, k=k):
+                arrived(data.at[piece(at, HP)], it, HA + k)
+                arrived(tags.at[at], it, HAS + k)
+
+            pl.when(below if k == 0 else takes)(taken)
+            send(data.at[piece(at, HP)], data.at[piece(at, HP)], it, FH + k, sibling, takes)
+        send(tags.at[own_eight], tags.at[own_eight], it, FHS, sibling, takes)
 
     def unpack(value, scale):
         return value.astype(jnp.int32).astype(F32) * scale[0:1, 0:1]
@@ -469,7 +488,8 @@
                 to_hi[to, at], to_lo[to, at] = split(x.T)
 
     def take_gram(it):
-        arrived(ea.at[it, other_part], it, FE)
+        for k in range(8):
+            arrived(ea.at[it, piece((1 - core) * 8 + (z + 8 - k) % 8, GP)], it, FE + k)
         arrived(es.at[it, other_eight], it, FES)
         spread(ea.at[it], es.at[it], ehi, elo)
 
@@ -481,9 +501,7 @@
             spread(na, ns, mhi, mlo)
 
     def cross_value(it, i):
-        return jnp.concatenate(
-            [unpack(ha[it, piece(2 * i, HP), :], hs[it, 2 * i]), unpack(ha[it, piece(2 * i + 1, HP), :], hs[it, 2 * i + 1])], axis=0
-        )
+        return jnp.concatenate([unpack(ha[it, piece(4 * i + e, HP), :], hs[it, 4 * i + e]) for e in range(4)], axis=0)
 
     def cross_plain(it, to_hi, to_lo):
         def body(i, carry):
@@ -504,10 +522,9 @@
     def take_cross(it):
         @pl.when(jnp.logical_or(high, has_side))
         def _():
-            arrived(ha.at[it, pair_near_rows], it, FH)
-            arrived(hs.at[it, pair_near_two], it, FHS)
-            arrived(ha.at[it, pair_far_rows], it, FH + 1)
-            arrived(hs.at[it, pair_far_two], it, FHS + 1)
+            for k in range(8):
+                arrived(ha.at[it, piece((1 - core) * 8 + (z + 8 - k) % 8, HP)], it, FH + k)
+            arrived(hs.at[it, other_eight], it, FHS)
 
         pl.when(jnp.logical_and(low, has_side))(lambda: cross_plain(it, xhi, xlo))
         pl.when(jnp.logical_and(high, has_side))(lambda: cross_turned(it, xhi, xlo))
@@ -570,7 +587,8 @@
         nhi[rows, :], nlo[rows, :] = split(x)
 
     def last(t, rows):
-        out[rows, :] = updated(1, t, rows)
+        c[rows, :] = updated(1, t, rows)
+        pltpu.make_async_copy(c.at[rows], out.at[rows], local_sem.at[t]).start()
 
     images(0)
     edges(0)
@@ -615,6 +633,9 @@
     pass_cross(1)
     take_cross(1)
     tiles(last)
+    for t in range(4):
+        rows = pl.ds(t * TILE, TILE)
+        pltpu.make_async_copy(c.at[rows], out.at[rows], local_sem.at[t]).wait()
 
     for src, it, index, cond in sent:
 
@@ -639,12 +660,14 @@
         vm((576, 128), BF), vm((576, 128), BF), vm((576, 128), BF),
         vm((2, PHALF, TILE), F32), vm((2, HALF, ORBS), F32),
         vm((2, 8, GP, TILE), I16), vm((2, 8, GP, TILE), I16), vm((2, 8, 128), F32), vm((2, 8, 8, 128), F32),
-        vm((2, 4, HP, ORBS), I16), vm((2, 4, HP, ORBS), I16), vm((2, 8, 128), F32), vm((2, 4, 8, 128), F32),
+        vm((2, 8, HP, ORBS), I16), vm((2, 8, HP, ORBS), I16), vm((2, 8, 128), F32), vm((2, 8, 8, 128), F32),
         vm((2, PACKED, TILE), I16), vm((2, 16, 8, 128), F32), vm((PACKED, TILE), I16), vm((16, 8, 128), F32),
-        vm((2, ORBS, ORBS), I16), vm((2, 8, 8, 128), F32),
+        vm((2, ORBS, ORBS), I16), vm((2, 16, 8, 128), F32),
         vm(square, BF), vm(square, BF), vm(square, BF), vm(square, BF), vm(square, BF), vm(square, BF),
         vm(square, BF), vm(square, BF), vm((PACKED, TILE), F32),
-        pltpu.SemaphoreType.DMA((2, COUNT)), pltpu.SemaphoreType.DMA((2, COUNT)), pltpu.SemaphoreType.DMA((6,)),
+        vm((2, HP, ORBS), I16), vm((2, 8, 128), F32), vm((HP, ORBS), F32), vm((BLK, ORBS), BF), vm((BLK, ORBS), BF),
+        pltpu.SMEM((64,), jnp.int32), pltpu.SMEM((8,), jnp.int32),
+        pltpu.SemaphoreType.DMA((2, COUNT)), pltpu.SemaphoreType.DMA((2, COUNT)), pltpu.SemaphoreType.DMA((8,)),
     ]
     result = pl.pallas_call(
         kernel,
@@ -652,13 +675,13 @@
         in_specs=[
             pl.BlockSpec(memory_space=pltpu.HBM),
             pl.BlockSpec(memory_space=pltpu.HBM),
-            pl.BlockSpec(memory_space=pltpu.SMEM),
-            pl.BlockSpec(memory_space=pltpu.SMEM),
+            pl.BlockSpec(memory_space=pltpu.HBM),
+            pl.BlockSpec(memory_space=pltpu.HBM),
         ],
-        out_specs=pl.BlockSpec(memory_space=pltpu.VMEM),
+        out_specs=pl.BlockSpec(memory_space=pltpu.HBM),
         scratch_shapes=scratch,
         compiler_params=pltpu.CompilerParams(
-            collective_id=0, has_side_effects=True, vmem_limit_bytes=50 * 1024 * 1024
+            collective_id=0, has_side_effects=True, vmem_limit_bytes=62 * 1024 * 1024
         ),
     )(coefficients[0], basis_metric, pattern, starts)
     return result[None]

time: 117 us -> 113 us (0.966)
  local copies, waits for them, and re-layouts: 4.09 us -> 2.26 us
    unnamed x9 -> x1, local copies, waits for them, and re-layouts: 4.09 us -> 2.26 us
where the time goes in v5:
time: 113 us
  Pallas kernels  110 us (97%)
  local copies, waits for them, and re-layouts  2.26 us (2%)
    pallas_call x1, Pallas kernels, per_device(): pl.pallas_call(kernel, out_shape=jax.ShapeDtypeStruct((ROWS, ORBS), F32),...  110 us
    unnamed x1, local copies, waits for them, and re-layouts  2.26 us

profile of v5, /device:TPU:25, one launch (start us, length us, event | category | flops | bytes accessed | tf_op | source)
XLA Modules:
  0.0 112.6 jit_solution(5653960222805386209)
XLA Ops:
  0.0 110.3 %shard_map.46 = f32[512,512]{1,0:T(8,128)} custom-call(f32[512,512]{1,0:T(8,128)} %bitcast.3, bf16[4096,128]{1,0:T(8,128)(2,1)} %metric.1, s32[64]{0:T(128)} %pattern_in.1, s32[8]{0:T(128)} %starts_in.1), custom_call_target="tpu_custom_call" | custom-call | tf_op jit(solution)/shard_map/pallas_call | solution.py:672
  110.3 2.3 %copy.6 = f32[1,512,512]{2,1,0:T(8,128)} copy(f32[1,512,512]{2,1,0:T(8,128)} %bitcast.2) | data formatting | bytes 2097152

commit v6 on v5

--- a/solution.py
+++ b/solution.py
@@ -51,7 +51,7 @@
     c, chi, clo, nf, nhi, nlo, yhi, ylo, band, gp, hp,
     nq_out, nq_in, cs_own, cs_in, meff, mrecv, msel,
     gsib, hsib, qs, rs, qsc, rsc, hqs, hrs, hqsc, hrsc,
-    ea, es, na, ns, ha, hs, ehi, elo, xhi, xlo, thi, tlo, mhi, mlo, ef, ho, hos, sums, dhi, dlo, pattern, starts,
+    ea, es, na, ns, ha, hs, ehi, elo, xhi, xlo, thi, tlo, mhi, mlo, ef, ho, hos, sums, lhs, rhs, ends, pattern, starts,
     ss, rr, local_sem,
 ):
     b, o, r = lax.axis_index("basis"), lax.axis_index("orb"), lax.axis_index("rep")
@@ -141,11 +141,12 @@
     cs_own[...] = cs
     first_block = (o * GROUP_BLOCKS + p * 8).astype(F32)
 
-    def live(t, cs_ref):
-        rows = lax.broadcasted_iota(jnp.int32, (TILE, ORBS), 0) // BLK
-        block = rows.astype(F32) + (first_block + (t * (TILE // BLK)).astype(F32))
-        at = cs_ref[0:1, :]
-        return jnp.logical_and(block >= at, block < at + SUPPORT)
+    def live(rows, cs_ref):
+        start, count = rows.start, rows.size
+        at = lax.broadcasted_iota(jnp.int32, (count, ORBS), 0) + start
+        block = first_block + (at // BLK).astype(F32)
+        begin = cs_ref[0:1, :]
+        return jnp.logical_and(block >= begin, block < begin + SUPPORT)
 
     def tiles(body):
         def step(t, carry):
@@ -155,7 +156,7 @@
         lax.fori_loop(0, ROWS // TILE, step, 0)
 
     def prepare(t, rows):
-        x = jnp.where(live(t, cs_own), c[rows, :], 0.0)
+        x = jnp.where(live(rows, cs_own), c[rows, :], 0.0)
         c[rows, :] = x
         hi, lo = split(x)
         chi[0, rows, :] = hi
@@ -279,11 +280,34 @@
 
     def edges(it):
         wait_halo(it)
-        for rows in (slice(0, 64), slice(448, 512)):
-            y = yhi[rows, :].astype(F32) + ylo[rows, :].astype(F32)
-            more = dot(band[rows, 512:640], chi[it, 512:640])
-            yhi[rows, :], ylo[rows, :] = split(y + more)
-        dhi[...], dlo[...] = split(more)
+        top = dot(band[0:64, 512:640], chi[it, 512:640])
+        bottom = dot(band[448:512, 512:640], chi[it, 512:640])
+        last_block = chi[it, 448:512, :]
+        lhs[0:64, :] = chi[it, 0:64, :]
+        rhs[0:64, :] = top.astype(BF)
+        lhs[64:128, :] = last_block
+        rhs[64:128, :] = bottom.astype(BF)
+        lhs[128:192, :] = bottom.astype(BF)
+        rhs[128:192, :] = (last_block.astype(F32) * (p < 7).astype(F32)).astype(BF)
+        for a in range(4):
+            cols = slice(a * TILE, a * TILE + TILE)
+            g = dot(lhs[:, cols], rhs[:, a * TILE : ORBS], ((0,), (0,)))
+            for e in range(a, 4):
+                rows = slice(KEPT.index((a, e)) * TILE, KEPT.index((a, e)) * TILE + TILE)
+                gp[it, rows, :] = gp[it, rows, :] + g[:, (e - a) * TILE : (e - a) * TILE + TILE]
+        if it == 0:
+            for rows, more in ((slice(0, 64), top), (slice(448, 512), bottom)):
+                y = yhi[rows, :].astype(F32) + ylo[rows, :].astype(F32)
+                yhi[rows, :], ylo[rows, :] = split(y + more)
+
+    def cross_edges(it):
+        ends[0:64, :] = nhi[0:64, :]
+        ends[64:128, :] = nhi[448:512, :]
+
+        def body(t, cols):
+            hp[it, cols, :] = hp[it, cols, :] + dot(rhs[0:128, cols], ends[...], ((0,), (0,)))
+
+        tiles(body)
 
     def gram(it):
         for a in range(4):
@@ -293,16 +317,6 @@
             for e in range(a, 4):
                 k = KEPT.index((a, e))
                 gp[it, k * TILE : k * TILE + TILE, :] = g[:, (e - a) * TILE : (e - a) * TILE + TILE]
-
-        @pl.when(p < 7)
-        def _():
-            for a in range(4):
-                cols = slice(a * TILE, a * TILE + TILE)
-                rest = slice(a * TILE, ORBS)
-                g = dot3(dhi[:, cols], dlo[:, cols], chi[it, 448:512, rest], clo[it, 448:512, rest], ((0,), (0,)))
-                for e in range(a, 4):
-                    rows = slice(KEPT.index((a, e)) * TILE, KEPT.index((a, e)) * TILE + TILE)
-                    gp[it, rows, :] = gp[it, rows, :] + g[:, (e - a) * TILE : (e - a) * TILE + TILE]
 
     def cross(it):
         def body(t, cols):
@@ -542,7 +556,7 @@
 
     def updated(it, t, rows):
         change = dot3(nhi[rows, :], nlo[rows, :], xhi[...], xlo[...])
-        return jnp.where(live(t, cs_own), c[rows, :] - 0.5 * change, 0.0)
+        return jnp.where(live(rows, cs_own), c[rows, :] - 0.5 * change, 0.0)
 
     def take_rows():
         for t in (0, 3, 1, 2):
@@ -572,32 +586,30 @@
         chi[1, rows, :] = hi
         clo[1, rows, :] = lo
 
-    def some(body, start, step):
+    def some(body):
         def run(i, carry):
-            t = start + i * step
-            body(t, pl.ds(pl.multiple_of(t * TILE, TILE), TILE))
+            body(i, pl.ds(pl.multiple_of(64 + i * TILE, 64), TILE))
             return carry
 
-        lax.fori_loop(0, 2, run, 0)
+        lax.fori_loop(0, 3, run, 0)
 
     def beside(t, rows):
         change = dot3(nhi[rows, :], nlo[rows, :], mhi[...], mlo[...])
         change = change + dot3(chi[0, rows, :], clo[0, rows, :], thi[...], tlo[...])
-        x = jnp.where(live(t, cs_in), nf[rows, :] - 0.5 * change, 0.0)
+        x = jnp.where(live(rows, cs_in), nf[rows, :] - 0.5 * change, 0.0)
         nhi[rows, :], nlo[rows, :] = split(x)
 
     def last(t, rows):
-        c[rows, :] = updated(1, t, rows)
-        pltpu.make_async_copy(c.at[rows], out.at[rows], local_sem.at[t]).start()
+        out[rows, :] = updated(1, t, rows)
 
     images(0)
+    gram(0)
     edges(0)
-    gram(0)
     send(gp.at[0, other_part], gsib.at[0], 0, GSIB, sibling)
     scatter_gram(0)
-    own_gram(0)
     take_rows()
     pair_cross(0)
+    own_gram(0)
     pl.when(high)(lambda: scatter_cross(0))
     send_cross(0)
     pass_gram(0, True)
@@ -607,9 +619,10 @@
     pass_side(0)
     pass_cross(0)
     take_cross(0)
-    some(first, 0, 3)
+    first(0, pl.ds(0, BLK))
+    first(0, pl.ds(448, BLK))
     send_halo(1)
-    some(first, 1, 1)
+    some(first)
     pl.when(has_side)(lambda: arrived(cs_in, 0, NXC))
     pl.when(jnp.logical_and(low, has_side))(lambda: cross_turned(0, thi, tlo))
     pl.when(jnp.logical_and(high, has_side))(lambda: cross_plain(0, thi, tlo))
@@ -617,10 +630,11 @@
     pl.when(has_side)(lambda: tiles(beside))
 
     images(1)
+    gram(1)
+    pl.when(high)(lambda: cross(1))
     edges(1)
-    gram(1)
     send(gp.at[1, other_part], gsib.at[1], 1, GSIB, sibling)
-    pl.when(high)(lambda: cross(1))
+    pl.when(high)(lambda: cross_edges(1))
     pair_cross(1)
     scatter_gram(1)
     pl.when(high)(lambda: scatter_cross(1))
@@ -633,9 +647,6 @@
     pass_cross(1)
     take_cross(1)
     tiles(last)
-    for t in range(4):
-        rows = pl.ds(t * TILE, TILE)
-        pltpu.make_async_copy(c.at[rows], out.at[rows], local_sem.at[t]).wait()
 
     for src, it, index, cond in sent:
 
@@ -665,7 +676,7 @@
         vm((2, ORBS, ORBS), I16), vm((2, 16, 8, 128), F32),
         vm(square, BF), vm(square, BF), vm(square, BF), vm(square, BF), vm(square, BF), vm(square, BF),
         vm(square, BF), vm(square, BF), vm((PACKED, TILE), F32),
-        vm((2, HP, ORBS), I16), vm((2, 8, 128), F32), vm((HP, ORBS), F32), vm((BLK, ORBS), BF), vm((BLK, ORBS), BF),
+        vm((2, HP, ORBS), I16), vm((2, 8, 128), F32), vm((HP, ORBS), F32), vm((192, ORBS), BF), vm((192, ORBS), BF), vm((128, ORBS), BF),
         pltpu.SMEM((64,), jnp.int32), pltpu.SMEM((8,), jnp.int32),
         pltpu.SemaphoreType.DMA((2, COUNT)), pltpu.SemaphoreType.DMA((2, COUNT)), pltpu.SemaphoreType.DMA((8,)),
     ]
@@ -678,10 +689,10 @@
             pl.BlockSpec(memory_space=pltpu.HBM),
             pl.BlockSpec(memory_space=pltpu.HBM),
         ],
-        out_specs=pl.BlockSpec(memory_space=pltpu.HBM),
+        out_specs=pl.BlockSpec(memory_space=pltpu.VMEM),
         scratch_shapes=scratch,
         compiler_params=pltpu.CompilerParams(
-            collective_id=0, has_side_effects=True, vmem_limit_bytes=62 * 1024 * 1024
+            collective_id=0, has_side_effects=True, vmem_limit_bytes=52 * 1024 * 1024
         ),
     )(coefficients[0], basis_metric, pattern, starts)
     return result[None]

time: 113 us -> 110 us (0.973)
  Pallas kernels: 110 us -> 108 us
    pallas_call x1, Pallas kernels: 110 us -> 108 us  [per_device(): pl.pallas_call(kernel, out_shape=jax.ShapeDtypeStruct((ROWS, ORBS), F32),...]
    unnamed x1 -> x5, local copies, waits for them, and re-layouts: 2.26 us -> 1.64 us
where the time goes in v6:
time: 110 us; the launch traced here: 109 us
  Pallas kernels  108 us (98%)
  local copies, waits for them, and re-layouts  1.64 us (1%)
    pallas_call x1, Pallas kernels, per_device(): pl.pallas_call(kernel, out_shape=jax.ShapeDtypeStruct((ROWS, ORBS), F32),...  108 us

profile of v6, /device:TPU:25, one launch (start us, length us, event | category | flops | bytes accessed | tf_op | source)
XLA Modules:
  0.0 109.5 jit_solution(10854294502579430673)
XLA Ops:
  0.0 0.0 copy-start.1
  0.0 0.0 copy-start
  0.0 0.7 copy-done.1
  0.7 0.0 copy-done
  0.7 107.8 %shard_map.46 = f32[512,512]{1,0:T(8,128)S(1)} custom-call(f32[512,512]{1,0:T(8,128)} %bitcast.3, bf16[4096,128]{1,0:T(8,128)(2,1)} %metric.1, s32[64]{0:T(128)S(1)} %copy-done, s32[8]{0:T(128)S(1)} %copy-done.1), custom_call_target="tpu_custom_call" | custom-call | tf_op jit(solution)/shard_map/pallas_call | solution.py:683
  108.5 1.0 copy.6
Async XLA Ops:
  0.0 0.7 copy-start.1
  0.0 0.7 copy-start

commit v7 on v6

--- a/solution.py
+++ b/solution.py
@@ -134,8 +134,8 @@
     load_prev.start()
     small[0].wait()
     small[1].wait()
-    lane = lax.broadcasted_iota(jnp.int32, (8, ORBS), 1) // BLK
-    cs = jnp.zeros((8, ORBS), F32)
+    lane = lax.broadcasted_iota(jnp.int32, (1, ORBS), 1) // BLK
+    cs = jnp.zeros((1, ORBS), F32)
     for i in range(8):
         cs = jnp.where(lane == i, starts[i].astype(F32), cs)
     cs_own[...] = cs
@@ -273,10 +273,7 @@
     band[0:128, 512:640] = jnp.where(jnp.logical_and(top, left), shifted, 0.0).astype(BF)
 
     def images(it):
-        def body(t, rows):
-            yhi[rows, :], ylo[rows, :] = split(dot(band[rows, 0:512], chi[it, 0:512]) + dot(band[rows, 0:512], clo[it]))
-
-        tiles(body)
+        yhi[...], ylo[...] = split(dot(band[:, 0:512], chi[it, 0:512]) + dot(band[:, 0:512], clo[it]))
 
     def edges(it):
         wait_halo(it)
@@ -304,10 +301,7 @@
         ends[0:64, :] = nhi[0:64, :]
         ends[64:128, :] = nhi[448:512, :]
 
-        def body(t, cols):
-            hp[it, cols, :] = hp[it, cols, :] + dot(rhs[0:128, cols], ends[...], ((0,), (0,)))
-
-        tiles(body)
+        hp[it] = hp[it] + dot(rhs[0:128, :], ends[...], ((0,), (0,)))
 
     def gram(it):
         for a in range(4):
@@ -319,17 +313,11 @@
                 gp[it, k * TILE : k * TILE + TILE, :] = g[:, (e - a) * TILE : (e - a) * TILE + TILE]
 
     def cross(it):
-        def body(t, cols):
-            hp[it, cols, :] = dot3(yhi[:, cols], ylo[:, cols], nhi[...], nlo[...], ((0,), (0,)))
-
-        tiles(body)
+        hp[it] = dot3(yhi[...], ylo[...], nhi[...], nlo[...], ((0,), (0,)))
 
     def cross_rows(it, rows, begin):
-        def body(t, cols):
-            more = dot3(yhi[rows, cols], ylo[rows, cols], nhi[rows, :], nlo[rows, :], ((0,), (0,)))
-            hp[it, cols, :] = more if begin else hp[it, cols, :] + more
-
-        tiles(body)
+        more = dot3(yhi[rows, :], ylo[rows, :], nhi[rows, :], nlo[rows, :], ((0,), (0,)))
+        hp[it] = more if begin else hp[it] + more
 
     own_half = pl.ds(pl.multiple_of(core * HALF, HALF), HALF)
     other_half = pl.ds(pl.multiple_of((1 - core) * HALF, HALF), HALF)
@@ -347,7 +335,7 @@
 
         peak = jnp.max(lax.fori_loop(0, count, add, jnp.zeros((size, wide), F32)), axis=(0, 1), keepdims=True)
         peak = jnp.maximum(peak, 1e-30)
-        scale[it] = jnp.broadcast_to(peak * (1.0 / QMAX), (8, 128))
+        scale[it] = jnp.broadcast_to(peak * (1.0 / QMAX), (1, 128))
         inv = QMAX / peak
 
         def pack(i, carry):
@@ -359,7 +347,7 @@
 
     def quantized(x):
         peak = jnp.maximum(jnp.max(jnp.abs(x), axis=(0, 1), keepdims=True), 1e-30)
-        return jnp.round(x * (QMAX / peak)).astype(I16), jnp.broadcast_to(peak * (1.0 / QMAX), (8, 128))
+        return jnp.round(x * (QMAX / peak)).astype(I16), jnp.broadcast_to(peak * (1.0 / QMAX), (1, 128))
 
     def scatter_gram(it):
         arrived(gsib.at[it], it, GSIB)
@@ -549,10 +537,7 @@
             xlo[...] = jnp.zeros((ORBS, ORBS), BF)
 
     def own_change(it):
-        def body(t, rows):
-            c[rows, :] = c[rows, :] - 0.5 * dot3(chi[it, rows, :], clo[it, rows, :], ehi[...], elo[...])
-
-        tiles(body)
+        c[...] = c[...] - 0.5 * dot3(chi[it, 0:512], clo[it], ehi[...], elo[...])
 
     def updated(it, t, rows):
         change = dot3(nhi[rows, :], nlo[rows, :], xhi[...], xlo[...])
@@ -579,19 +564,22 @@
     def pair_cross(it):
         send(hp.at[it, other_half], hsib.at[it], it, HSIB, sibling, high)
 
-    def first(t, rows):
-        x = updated(0, t, rows)
+    def keep(rows, x):
         c[rows, :] = x
         hi, lo = split(x)
         chi[1, rows, :] = hi
         clo[1, rows, :] = lo
 
-    def some(body):
-        def run(i, carry):
-            body(i, pl.ds(pl.multiple_of(64 + i * TILE, 64), TILE))
-            return carry
-
-        lax.fori_loop(0, 3, run, 0)
+    def first(rows):
+        keep(rows, updated(0, 0, rows))
+
+    def first_ends():
+        two = (pl.ds(0, BLK), pl.ds(448, BLK))
+        change = dot3(
+            jnp.concatenate([nhi[rows, :] for rows in two], axis=0), jnp.concatenate([nlo[rows, :] for rows in two], axis=0), xhi[...], xlo[...]
+        )
+        for i, rows in enumerate(two):
+            keep(rows, jnp.where(live(rows, cs_own), c[rows, :] - 0.5 * change[i * BLK : i * BLK + BLK], 0.0))
 
     def beside(t, rows):
         change = dot3(nhi[rows, :], nlo[rows, :], mhi[...], mlo[...])
@@ -609,9 +597,9 @@
     scatter_gram(0)
     take_rows()
     pair_cross(0)
-    own_gram(0)
     pl.when(high)(lambda: scatter_cross(0))
     send_cross(0)
+    own_gram(0)
     pass_gram(0, True)
     take_gram(0)
     own_change(0)
@@ -619,15 +607,14 @@
     pass_side(0)
     pass_cross(0)
     take_cross(0)
-    first(0, pl.ds(0, BLK))
-    first(0, pl.ds(448, BLK))
+    first_ends()
     send_halo(1)
-    some(first)
+    first(pl.ds(64, 384))
     pl.when(has_side)(lambda: arrived(cs_in, 0, NXC))
     pl.when(jnp.logical_and(low, has_side))(lambda: cross_turned(0, thi, tlo))
     pl.when(jnp.logical_and(high, has_side))(lambda: cross_plain(0, thi, tlo))
     take_side(0)
-    pl.when(has_side)(lambda: tiles(beside))
+    pl.when(has_side)(lambda: beside(0, pl.ds(0, ROWS)))
 
     images(1)
     gram(1)
@@ -646,7 +633,7 @@
     own_change(1)
     pass_cross(1)
     take_cross(1)
-    tiles(last)
+    last(0, pl.ds(0, ROWS))
 
     for src, it, index, cond in sent:
 
@@ -667,16 +654,16 @@
         vm((ROWS, ORBS), F32), vm((ROWS, ORBS), BF), vm((ROWS, ORBS), BF),
         vm((ROWS, ORBS), BF), vm((ROWS, ORBS), BF), vm((ROWS, 640), BF),
         vm((2, PACKED, TILE), F32), vm((2, ORBS, ORBS), F32),
-        vm((ROWS, ORBS), I16), vm((ROWS, ORBS), I16), vm((8, ORBS), F32), vm((8, ORBS), F32),
+        vm((ROWS, ORBS), I16), vm((ROWS, ORBS), I16), vm((1, ORBS), F32), vm((1, ORBS), F32),
         vm((576, 128), BF), vm((576, 128), BF), vm((576, 128), BF),
         vm((2, PHALF, TILE), F32), vm((2, HALF, ORBS), F32),
-        vm((2, 8, GP, TILE), I16), vm((2, 8, GP, TILE), I16), vm((2, 8, 128), F32), vm((2, 8, 8, 128), F32),
-        vm((2, 8, HP, ORBS), I16), vm((2, 8, HP, ORBS), I16), vm((2, 8, 128), F32), vm((2, 8, 8, 128), F32),
-        vm((2, PACKED, TILE), I16), vm((2, 16, 8, 128), F32), vm((PACKED, TILE), I16), vm((16, 8, 128), F32),
-        vm((2, ORBS, ORBS), I16), vm((2, 16, 8, 128), F32),
+        vm((2, 8, GP, TILE), I16), vm((2, 8, GP, TILE), I16), vm((2, 1, 128), F32), vm((2, 8, 1, 128), F32),
+        vm((2, 8, HP, ORBS), I16), vm((2, 8, HP, ORBS), I16), vm((2, 1, 128), F32), vm((2, 8, 1, 128), F32),
+        vm((2, PACKED, TILE), I16), vm((2, 16, 1, 128), F32), vm((PACKED, TILE), I16), vm((16, 1, 128), F32),
+        vm((2, ORBS, ORBS), I16), vm((2, 16, 1, 128), F32),
         vm(square, BF), vm(square, BF), vm(square, BF), vm(square, BF), vm(square, BF), vm(square, BF),
         vm(square, BF), vm(square, BF), vm((PACKED, TILE), F32),
-        vm((2, HP, ORBS), I16), vm((2, 8, 128), F32), vm((HP, ORBS), F32), vm((192, ORBS), BF), vm((192, ORBS), BF), vm((128, ORBS), BF),
+        vm((2, HP, ORBS), I16), vm((2, 1, 128), F32), vm((HP, ORBS), F32), vm((192, ORBS), BF), vm((192, ORBS), BF), vm((128, ORBS), BF),
         pltpu.SMEM((64,), jnp.int32), pltpu.SMEM((8,), jnp.int32),
         pltpu.SemaphoreType.DMA((2, COUNT)), pltpu.SemaphoreType.DMA((2, COUNT)), pltpu.SemaphoreType.DMA((8,)),
     ]

time: 110 us -> 106 us (0.964)
  Pallas kernels: 108 us -> 104 us
    pallas_call x1, Pallas kernels: 108 us -> 104 us  [per_device(): pl.pallas_call(kernel, out_shape=jax.ShapeDtypeStruct((ROWS, ORBS), F32),...]
where the time goes in v7:
time: 106 us; the launch traced here: 105 us
  Pallas kernels  104 us (98%)
  local copies, waits for them, and re-layouts  1.64 us (2%)
    pallas_call x1, Pallas kernels, per_device(): pl.pallas_call(kernel, out_shape=jax.ShapeDtypeStruct((ROWS, ORBS), F32),...  104 us

profile of v7, /device:TPU:25, one launch (start us, length us, event | category | flops | bytes accessed | tf_op | source)
XLA Modules:
  0.0 105.4 jit_solution(1721811279785806700)
XLA Ops:
  0.0 0.0 copy-start.1
  0.0 0.0 copy-start
  0.0 0.7 copy-done.1
  0.7 0.0 copy-done
  0.7 103.8 %shard_map.46 = f32[512,512]{1,0:T(8,128)S(1)} custom-call(f32[512,512]{1,0:T(8,128)} %bitcast.3, bf16[4096,128]{1,0:T(8,128)(2,1)} %metric.1, s32[64]{0:T(128)S(1)} %copy-done, s32[8]{0:T(128)S(1)} %copy-done.1), custom_call_target="tpu_custom_call" | custom-call | tf_op jit(solution)/shard_map/pallas_call | solution.py:670
  104.5 1.0 copy.6
Async XLA Ops:
  0.0 0.7 copy-start.1
  0.0 0.7 copy-start

commit v8 on v7

--- a/solution.py
+++ b/solution.py
@@ -29,6 +29,8 @@
 NX = 12
 RS, RSC, HRS, HRSC, EA, EAS, HA, HAS, FE, FH = range(16, 96, 8)
 COUNT = 96
+
+FAR = (4, 3, 5, 2, 6, 1, 7)
 
 KEPT = [(a, b) for a in range(4) for b in range(a, 4)]
 
@@ -333,7 +335,7 @@
             part[it, rows, :] = x
             return jnp.maximum(top_value, jnp.abs(x))
 
-        peak = jnp.max(lax.fori_loop(0, count, add, jnp.zeros((size, wide), F32)), axis=(0, 1), keepdims=True)
+        peak = jnp.max(lax.fori_loop(0, count, add, jnp.zeros((size, wide), F32), unroll=True), axis=(0, 1), keepdims=True)
         peak = jnp.maximum(peak, 1e-30)
         scale[it] = jnp.broadcast_to(peak * (1.0 / QMAX), (1, 128))
         inv = QMAX / peak
@@ -343,7 +345,7 @@
             packed[it, i] = jnp.round(part[it, rows, :] * inv).astype(I16)
             return carry
 
-        lax.fori_loop(0, count, pack, 0)
+        lax.fori_loop(0, count, pack, 0, unroll=True)
 
     def quantized(x):
         peak = jnp.maximum(jnp.max(jnp.abs(x), axis=(0, 1), keepdims=True), 1e-30)
@@ -352,7 +354,7 @@
     def scatter_gram(it):
         arrived(gsib.at[it], it, GSIB)
         pair_and_pack(it, gp, gsib, qs, qsc, GP, 8)
-        for k in range(1, 8):
+        for k in FAR:
             to = (z + k) % 8
             send(qs.at[it, to], rs.at[it, k], it, RS + k, zdev(to, o))
             send(qsc.at[it], rsc.at[it, k], it, RSC + k, zdev(to, o))
@@ -365,7 +367,7 @@
         return (z + 8 - k) % 4 >= 2
 
     def send_cross(it):
-        for k in range(1, 8):
+        for k in FAR:
             to = (z + k) % 8
             send(hqs.at[it, to], hrs.at[it, k], it, HRS + k, zdev(to, o), high)
             send(hqsc.at[it], hrsc.at[it, k], it, HRSC + k, zdev(to, o), high)
@@ -387,7 +389,7 @@
         ea[it, rows, :] = value
         at = core * 8 + z
         es[it, at] = scale
-        for k in range(1, 8):
+        for k in FAR:
             device = zdev((z + k) % 8, o)
             send(ea.at[it, rows], ea.at[it, rows], it, EA + k, device)
             send(es.at[it, at], es.at[it, at], it, EAS + k, device)
@@ -421,7 +423,7 @@
             ha[it, rows, :] = value
             hs[it, at] = scale
 
-        for k in range(8):
+        for k in FAR + (0,):
             to = (z + k) % 8
             to_low = to % 4 < 2
             cond = jnp.logical_and(to_low, above)
@@ -437,7 +439,7 @@
         return pl.ds(pl.multiple_of(at * size, size), size)
 
     def pass_gram(it, with_side):
-        for k in range(1, 8):
+        for k in FAR[::-1]:
             at = core * 8 + (z + 8 - k) % 8
             arrived(ea.at[it, piece(at, GP)], it, EA + k)
             arrived(es.at[it, at], it, EAS + k)
@@ -461,7 +463,7 @@
     def pass_cross(it):
         data, tags = ha.at[it], hs.at[it]
         takes = jnp.logical_or(high, has_side)
-        for k in range(8):
+        for k in (0,) + FAR[::-1]:
             at = core * 8 + (z + 8 - k) % 8
 
             def taken(at=at, k=k):
@@ -481,7 +483,7 @@
             ef[rows, :] = unpack(packed[rows, :], scales[i])
             return carry
 
-        lax.fori_loop(0, 16, body, 0)
+        lax.fori_loop(0, 16, body, 0, unroll=True)
         for k, (a, e) in enumerate(KEPT):
             x = ef[k * TILE : k * TILE + TILE, :]
             at, to = slice(a * TILE, a * TILE + TILE), slice(e * TILE, e * TILE + TILE)
@@ -511,7 +513,7 @@
             to_hi[rows, :], to_lo[rows, :] = split(cross_value(it, i))
             return carry
 
-        lax.fori_loop(0, 4, body, 0)
+        lax.fori_loop(0, 4, body, 0, unroll=True)
 
     def cross_turned(it, to_hi, to_lo):
         def body(i, carry):
@@ -519,7 +521,7 @@
             to_hi[:, cols], to_lo[:, cols] = split(cross_value(it, i).T)
             return carry
 
-        lax.fori_loop(0, 4, body, 0)
+        lax.fori_loop(0, 4, body, 0, unroll=True)
 
     def take_cross(it):
         @pl.when(jnp.logical_or(high, has_side))

time: 106 us -> 102 us (0.962)
  Pallas kernels: 104 us -> 100 us
    pallas_call x1, Pallas kernels: 104 us -> 100 us  [per_device(): pl.pallas_call(kernel, out_shape=jax.ShapeDtypeStruct((ROWS, ORBS), F32),...]
where the time goes in v8:
time: 102 us
  Pallas kernels  100 us (98%)
  local copies, waits for them, and re-layouts  1.64 us (2%)
    pallas_call x1, Pallas kernels, per_device(): pl.pallas_call(kernel, out_shape=jax.ShapeDtypeStruct((ROWS, ORBS), F32),...  100 us

profile of v8, /device:TPU:25, one launch (start us, length us, event | category | flops | bytes accessed | tf_op | source)
XLA Modules:
  0.0 102.1 jit_solution(6453489318250408270)
XLA Ops:
  0.0 0.0 copy-start.1
  0.0 0.0 copy-start
  0.0 0.7 copy-done.1
  0.7 0.0 copy-done
  0.7 100.5 %shard_map.46 = f32[512,512]{1,0:T(8,128)S(1)} custom-call(f32[512,512]{1,0:T(8,128)} %bitcast.3, bf16[4096,128]{1,0:T(8,128)(2,1)} %metric.1, s32[64]{0:T(128)S(1)} %copy-done, s32[8]{0:T(128)S(1)} %copy-done.1), custom_call_target="tpu_custom_call" | custom-call | tf_op jit(solution)/shard_map/pallas_call | solution.py:672
  101.1 1.0 copy.6
Async XLA Ops:
  0.0 0.7 copy-start.1
  0.0 0.7 copy-start

commit v9 on v8

--- a/solution.py
+++ b/solution.py
@@ -181,6 +181,62 @@
         def _():
             chi[it, 576:640, :] = jnp.zeros((64, ORBS), BF)
 
+    def ones(flag):
+        return flag.astype(jnp.int32)
+
+    pl.semaphore_wait(barrier, 8 + ones(has_step) + 8 * ones(below) + 4 * ones(above) + ones(straight) + ones(straight_down))
+
+    sent = []
+
+    def send(src, dst, it, index, device, cond=None, land=None):
+        land = index if land is None else land
+
+        def start():
+            pltpu.make_async_remote_copy(
+                src_ref=src, dst_ref=dst, send_sem=ss.at[it, index], recv_sem=rr.at[it, land],
+                device_id=device, device_id_type=pl.DeviceIdType.MESH,
+            ).start()
+
+        if cond is None:
+            start()
+        else:
+            pl.when(cond)(start)
+        sent.append((src, it, index, cond))
+
+    def drain():
+        for src, it, index, cond in sent:
+
+            def wait(src=src, it=it, index=index):
+                pltpu.make_async_copy(src, src, ss.at[it, index]).wait()
+
+            if cond is None:
+                wait()
+            else:
+                pl.when(cond)(wait)
+        sent.clear()
+
+    def arrived(dst, it, index):
+        pltpu.make_async_copy(dst, dst, rr.at[it, index]).wait()
+
+    def send_halo(it):
+        up_b = jnp.where(r == 0, b, b + 1)
+        down_b = jnp.where(r == 1, b, b - 1)
+        send(chi.at[it, pl.ds(0, 64)], chi.at[it, pl.ds(576, 64)], it, HALO_NEXT, dev(down_b, o, 1 - r), p > 0)
+        send(chi.at[it, pl.ds(448, 64)], chi.at[it, pl.ds(512, 64)], it, HALO_PREV, dev(up_b, o, 1 - r), jnp.logical_and(p > 6, p < 15))
+
+    def wait_halo(it):
+        pl.when(p < 15)(lambda: arrived(chi.at[it, pl.ds(576, 64)], it, HALO_NEXT))
+        pl.when(high)(lambda: arrived(chi.at[it, pl.ds(512, 64)], it, HALO_PREV))
+
+    send_halo(0)
+    partner = dev(jnp.where(low, b + 4, b - 4), side, r)
+    for t in (0, 3, 1, 2):
+        if t in (1, 2):
+            prepare_tile(t)
+        rows = pl.ds(t * TILE, TILE)
+        send(nq_out.at[rows], nq_in.at[rows], 0, NX + t, partner, has_side)
+    send(cs_own, cs_in, 0, NXC, partner, has_side)
+
     load_main.wait()
     load_prev.wait()
     right = lax.broadcasted_iota(jnp.int32, (BLK, 2 * BLK), 1) >= BLK
@@ -190,51 +246,8 @@
         block = meff[i * 64 : i * 64 + 64, :].astype(F32)
         meff[i * 64 : i * 64 + 64, :] = jnp.where(right, block * keep, block).astype(BF)
 
-    def ones(flag):
-        return flag.astype(jnp.int32)
-
-    pl.semaphore_wait(barrier, 8 + ones(has_step) + 8 * ones(below) + 4 * ones(above) + ones(straight) + ones(straight_down))
-
-    sent = []
-
-    def send(src, dst, it, index, device, cond=None, land=None):
-        land = index if land is None else land
-
-        def start():
-            pltpu.make_async_remote_copy(
-                src_ref=src, dst_ref=dst, send_sem=ss.at[it, index], recv_sem=rr.at[it, land],
-                device_id=device, device_id_type=pl.DeviceIdType.MESH,
-            ).start()
-
-        if cond is None:
-            start()
-        else:
-            pl.when(cond)(start)
-        sent.append((src, it, index, cond))
-
-    def arrived(dst, it, index):
-        pltpu.make_async_copy(dst, dst, rr.at[it, index]).wait()
-
-    def send_halo(it):
-        up_b = jnp.where(r == 0, b, b + 1)
-        down_b = jnp.where(r == 1, b, b - 1)
-        send(chi.at[it, pl.ds(0, 64)], chi.at[it, pl.ds(576, 64)], it, HALO_NEXT, dev(down_b, o, 1 - r), p > 0)
-        send(chi.at[it, pl.ds(448, 64)], chi.at[it, pl.ds(512, 64)], it, HALO_PREV, dev(up_b, o, 1 - r), jnp.logical_and(p > 6, p < 15))
-
-    def wait_halo(it):
-        pl.when(p < 15)(lambda: arrived(chi.at[it, pl.ds(576, 64)], it, HALO_NEXT))
-        pl.when(high)(lambda: arrived(chi.at[it, pl.ds(512, 64)], it, HALO_PREV))
-
     gives_metric = jnp.logical_and(high, o > 0)
     send(meff, mrecv, 0, MET, dev(b, o - 1, r), gives_metric)
-    send_halo(0)
-    partner = dev(jnp.where(low, b + 4, b - 4), side, r)
-    for t in (0, 3, 1, 2):
-        if t in (1, 2):
-            prepare_tile(t)
-        rows = pl.ds(t * TILE, TILE)
-        send(nq_out.at[rows], nq_in.at[rows], 0, NX + t, partner, has_side)
-    send(cs_own, cs_in, 0, NXC, partner, has_side)
 
     @pl.when(low)
     def _():
@@ -507,36 +520,43 @@
     def cross_value(it, i):
         return jnp.concatenate([unpack(ha[it, piece(4 * i + e, HP), :], hs[it, 4 * i + e]) for e in range(4)], axis=0)
 
-    def cross_plain(it, to_hi, to_lo):
-        def body(i, carry):
-            rows = piece(i, TILE)
-            to_hi[rows, :], to_lo[rows, :] = split(cross_value(it, i))
-            return carry
-
-        lax.fori_loop(0, 4, body, 0, unroll=True)
-
-    def cross_turned(it, to_hi, to_lo):
-        def body(i, carry):
-            cols = piece(i, TILE)
-            to_hi[:, cols], to_lo[:, cols] = split(cross_value(it, i).T)
-            return carry
-
-        lax.fori_loop(0, 4, body, 0, unroll=True)
-
-    def take_cross(it):
+    def cross_plain(it, to_hi, to_lo, halves=(0, 1)):
+        for half in halves:
+            for e in range(2):
+                rows = piece(2 * half + e, TILE)
+                to_hi[rows, :], to_lo[rows, :] = split(cross_value(it, 2 * half + e))
+
+    def cross_turned(it, to_hi, to_lo, halves=(0, 1)):
+        for half in halves:
+            for e in range(2):
+                cols = piece(2 * half + e, TILE)
+                to_hi[:, cols], to_lo[:, cols] = split(cross_value(it, 2 * half + e).T)
+
+    low_side = jnp.logical_and(low, has_side)
+    high_side = jnp.logical_and(high, has_side)
+
+    def unpack_half(it, half):
+        pl.when(low_side)(lambda: cross_plain(it, xhi, xlo, (half,)))
+        pl.when(high_side)(lambda: cross_turned(it, xhi, xlo, (half,)))
+
+    def take_own_cross(it):
+        if it == 0:
+
+            @pl.when(jnp.logical_not(has_side))
+            def _():
+                xhi[...] = jnp.zeros((ORBS, ORBS), BF)
+                xlo[...] = jnp.zeros((ORBS, ORBS), BF)
+
+        unpack_half(it, core)
+
+    def take_pair_cross(it):
         @pl.when(jnp.logical_or(high, has_side))
         def _():
             for k in range(8):
                 arrived(ha.at[it, piece((1 - core) * 8 + (z + 8 - k) % 8, HP)], it, FH + k)
             arrived(hs.at[it, other_eight], it, FHS)
 
-        pl.when(jnp.logical_and(low, has_side))(lambda: cross_plain(it, xhi, xlo))
-        pl.when(jnp.logical_and(high, has_side))(lambda: cross_turned(it, xhi, xlo))
-
-        @pl.when(jnp.logical_not(has_side))
-        def _():
-            xhi[...] = jnp.zeros((ORBS, ORBS), BF)
-            xlo[...] = jnp.zeros((ORBS, ORBS), BF)
+        unpack_half(it, 1 - core)
 
     def own_change(it):
         c[...] = c[...] - 0.5 * dot3(chi[it, 0:512], clo[it], ehi[...], elo[...])
@@ -589,8 +609,25 @@
         x = jnp.where(live(rows, cs_in), nf[rows, :] - 0.5 * change, 0.0)
         nhi[rows, :], nlo[rows, :] = split(x)
 
-    def last(t, rows):
-        out[rows, :] = updated(1, t, rows)
+    def ended(cols, change):
+        at = lax.broadcasted_iota(jnp.int32, (ROWS, HALF), 0)
+        block = first_block + (at // BLK).astype(F32)
+        begin = cs_own[0:1, cols]
+        lives = jnp.logical_and(block >= begin, block < begin + SUPPORT)
+        out[:, cols] = jnp.where(lives, c[:, cols] - 0.5 * change, 0.0)
+
+    def last_half(half, final):
+        @pl.when(low)
+        def _():
+            part = dot3(nhi[:, half], nlo[:, half], xhi[half, :], xlo[half, :])
+            if final:
+                out[...] = jnp.where(live(pl.ds(0, ROWS), cs_own), nf[...] - 0.5 * part, 0.0)
+            else:
+                nf[...] = c[...] - 0.5 * part
+
+        @pl.when(high)
+        def _():
+            ended(half, dot3(nhi[...], nlo[...], xhi[:, half], xlo[:, half]))
 
     images(0)
     gram(0)
@@ -608,7 +645,8 @@
     own_cross(0)
     pass_side(0)
     pass_cross(0)
-    take_cross(0)
+    take_own_cross(0)
+    take_pair_cross(0)
     first_ends()
     send_halo(1)
     first(pl.ds(64, 384))
@@ -621,6 +659,7 @@
     images(1)
     gram(1)
     pl.when(high)(lambda: cross(1))
+    drain()
     edges(1)
     send(gp.at[1, other_part], gsib.at[1], 1, GSIB, sibling)
     pl.when(high)(lambda: cross_edges(1))
@@ -634,18 +673,11 @@
     take_gram(1)
     own_change(1)
     pass_cross(1)
-    take_cross(1)
-    last(0, pl.ds(0, ROWS))
-
-    for src, it, index, cond in sent:
-
-        def wait(src=src, it=it, index=index):
-            pltpu.make_async_copy(src, src, ss.at[it, index]).wait()
-
-        if cond is None:
-            wait()
-        else:
-            pl.when(cond)(wait)
+    take_own_cross(1)
+    last_half(own_half, False)
+    drain()
+    take_pair_cross(1)
+    last_half(other_half, True)
 
 
 def per_device(coefficients, basis_metric, pattern, starts):

time: 102 us -> 101 us (level)
    pallas_call x1, Pallas kernels: 100 us -> 99.4 us  [per_device(): pl.pallas_call(kernel, out_shape=jax.ShapeDtypeStruct((ROWS, ORBS), F32),...]
where the time goes in v9:
time: 101 us
  Pallas kernels  99.4 us (98%)
  local copies, waits for them, and re-layouts  1.64 us (2%)
    pallas_call x1, Pallas kernels, per_device(): pl.pallas_call(kernel, out_shape=jax.ShapeDtypeStruct((ROWS, ORBS), F32),...  99.4 us

profile of v9, /device:TPU:25, one launch (start us, length us, event | category | flops | bytes accessed | tf_op | source)
XLA Modules:
  0.0 101.1 jit_solution(9337356313460309490)
XLA Ops:
  0.0 0.0 copy-start.1
  0.0 0.0 copy-start
  0.0 0.7 copy-done.1
  0.7 0.0 copy-done
  0.7 99.4 %shard_map.46 = f32[512,512]{1,0:T(8,128)S(1)} custom-call(f32[512,512]{1,0:T(8,128)} %bitcast.3, bf16[4096,128]{1,0:T(8,128)(2,1)} %metric.1, s32[64]{0:T(128)S(1)} %copy-done, s32[8]{0:T(128)S(1)} %copy-done.1), custom_call_target="tpu_custom_call" | custom-call | tf_op jit(solution)/shard_map/pallas_call | solution.py:704
  100.1 1.0 copy.6
Async XLA Ops:
  0.0 0.7 copy-start.1
  0.0 0.7 copy-start

commit v10 on v9

--- a/solution.py
+++ b/solution.py
@@ -330,10 +330,6 @@
     def cross(it):
         hp[it] = dot3(yhi[...], ylo[...], nhi[...], nlo[...], ((0,), (0,)))
 
-    def cross_rows(it, rows, begin):
-        more = dot3(yhi[rows, :], ylo[rows, :], nhi[rows, :], nlo[rows, :], ((0,), (0,)))
-        hp[it] = more if begin else hp[it] + more
-
     own_half = pl.ds(pl.multiple_of(core * HALF, HALF), HALF)
     other_half = pl.ds(pl.multiple_of((1 - core) * HALF, HALF), HALF)
     own_part = pl.ds(pl.multiple_of(core * PHALF, PHALF), PHALF)
@@ -367,6 +363,8 @@
     def scatter_gram(it):
         arrived(gsib.at[it], it, GSIB)
         pair_and_pack(it, gp, gsib, qs, qsc, GP, 8)
+
+    def send_gram(it):
         for k in FAR:
             to = (z + k) % 8
             send(qs.at[it, to], rs.at[it, k], it, RS + k, zdev(to, o))
@@ -565,23 +563,25 @@
         change = dot3(nhi[rows, :], nlo[rows, :], xhi[...], xlo[...])
         return jnp.where(live(rows, cs_own), c[rows, :] - 0.5 * change, 0.0)
 
+    def rows_arrived():
+        @pl.when(has_side)
+        def _():
+            for t in range(4):
+                arrived(nq_in.at[pl.ds(t * TILE, TILE)], 0, NX + t)
+
     def take_rows():
-        for t in (0, 3, 1, 2):
-            rows = slice(t * TILE, t * TILE + TILE)
-
-            @pl.when(has_side)
-            def _():
-                arrived(nq_in.at[rows], 0, NX + t)
+        @pl.when(has_side)
+        def _():
+            for t in range(4):
+                rows = pl.ds(t * TILE, TILE)
                 x = nq_in[rows, :].astype(jnp.int32).astype(F32) * (CMAX / QMAX)
                 nf[rows, :] = x
                 nhi[rows, :], nlo[rows, :] = split(x)
 
-            @pl.when(jnp.logical_not(has_side))
-            def _():
-                nhi[rows, :] = jnp.zeros((TILE, ORBS), BF)
-                nlo[rows, :] = jnp.zeros((TILE, ORBS), BF)
-
-            pl.when(high)(functools.partial(cross_rows, 0, rows, t == 0))
+        @pl.when(jnp.logical_not(has_side))
+        def _():
+            nhi[...] = jnp.zeros((ROWS, ORBS), BF)
+            nlo[...] = jnp.zeros((ROWS, ORBS), BF)
 
     def pair_cross(it):
         send(hp.at[it, other_half], hsib.at[it], it, HSIB, sibling, high)
@@ -634,7 +634,10 @@
     edges(0)
     send(gp.at[0, other_part], gsib.at[0], 0, GSIB, sibling)
     scatter_gram(0)
+    rows_arrived()
+    send_gram(0)
     take_rows()
+    pl.when(high)(lambda: cross(0))
     pair_cross(0)
     pl.when(high)(lambda: scatter_cross(0))
     send_cross(0)
@@ -665,6 +668,7 @@
     pl.when(high)(lambda: cross_edges(1))
     pair_cross(1)
     scatter_gram(1)
+    send_gram(1)
     pl.when(high)(lambda: scatter_cross(1))
     send_cross(1)
     own_gram(1)

time: 101 us -> 102 us (level)
  no operation moved by 1% of the time
where the time goes in v10:
time: 102 us
  Pallas kernels  100 us (98%)
  local copies, waits for them, and re-layouts  1.64 us (2%)
    pallas_call x1, Pallas kernels, per_device(): pl.pallas_call(kernel, out_shape=jax.ShapeDtypeStruct((ROWS, ORBS), F32),...  100 us

profile of v10, /device:TPU:25, one launch (start us, length us, event | category | flops | bytes accessed | tf_op | source)
XLA Modules:
  0.0 101.7 jit_solution(13157091570058921350)
XLA Ops:
  0.0 0.0 copy-start.1
  0.0 0.0 copy-start
  0.0 0.7 copy-done.1
  0.7 0.0 copy-done
  0.7 100.0 %shard_map.46 = f32[512,512]{1,0:T(8,128)S(1)} custom-call(f32[512,512]{1,0:T(8,128)} %bitcast.3, bf16[4096,128]{1,0:T(8,128)(2,1)} %metric.1, s32[64]{0:T(128)S(1)} %copy-done, s32[8]{0:T(128)S(1)} %copy-done.1), custom_call_target="tpu_custom_call" | custom-call | tf_op jit(solution)/shard_map/pallas_call | solution.py:708
  100.7 1.0 copy.6
Async XLA Ops:
  0.0 0.7 copy-start.1
  0.0 0.7 copy-start

commit v11 on v10

--- a/solution.py
+++ b/solution.py
@@ -642,10 +642,10 @@
     pl.when(high)(lambda: scatter_cross(0))
     send_cross(0)
     own_gram(0)
+    own_cross(0)
     pass_gram(0, True)
     take_gram(0)
     own_change(0)
-    own_cross(0)
     pass_side(0)
     pass_cross(0)
     take_own_cross(0)

time: 102 us -> 101 us (level)
  Pallas kernels: 100 us -> 98.9 us
    pallas_call x1, Pallas kernels: 100 us -> 98.9 us  [per_device(): pl.pallas_call(kernel, out_shape=jax.ShapeDtypeStruct((ROWS, ORBS), F32),...]
where the time goes in v11:
time: 101 us
  Pallas kernels  98.9 us (98%)
  local copies, waits for them, and re-layouts  1.64 us (2%)
    pallas_call x1, Pallas kernels, per_device(): pl.pallas_call(kernel, out_shape=jax.ShapeDtypeStruct((ROWS, ORBS), F32),...  98.9 us

profile of v11, /device:TPU:25, one launch (start us, length us, event | category | flops | bytes accessed | tf_op | source)
XLA Modules:
  0.0 100.6 jit_solution(8204005524819575419)
XLA Ops:
  0.0 0.0 copy-start.1
  0.0 0.0 copy-start
  0.0 0.7 copy-done.1
  0.7 0.0 copy-done
  0.7 98.9 %shard_map.46 = f32[512,512]{1,0:T(8,128)S(1)} custom-call(f32[512,512]{1,0:T(8,128)} %bitcast.3, bf16[4096,128]{1,0:T(8,128)(2,1)} %metric.1, s32[64]{0:T(128)S(1)} %copy-done, s32[8]{0:T(128)S(1)} %copy-done.1), custom_call_target="tpu_custom_call" | custom-call | tf_op jit(solution)/shard_map/pallas_call | solution.py:708
  99.6 1.0 copy.6
Async XLA Ops:
  0.0 0.7 copy-start.1
  0.0 0.7 copy-start

commit v12 on v11

--- a/solution.py
+++ b/solution.py
@@ -203,8 +203,8 @@
             pl.when(cond)(start)
         sent.append((src, it, index, cond))
 
-    def drain():
-        for src, it, index, cond in sent:
+    def drain(count=None):
+        for src, it, index, cond in sent[:count]:
 
             def wait(src=src, it=it, index=index):
                 pltpu.make_async_copy(src, src, ss.at[it, index]).wait()
@@ -213,7 +213,7 @@
                 wait()
             else:
                 pl.when(cond)(wait)
-        sent.clear()
+        del sent[:count]
 
     def arrived(dst, it, index):
         pltpu.make_async_copy(dst, dst, rr.at[it, index]).wait()
@@ -330,6 +330,9 @@
     def cross(it):
         hp[it] = dot3(yhi[...], ylo[...], nhi[...], nlo[...], ((0,), (0,)))
 
+    def cross_half(it, half):
+        hp[it, half, :] = dot3(yhi[:, half], ylo[:, half], nhi[...], nlo[...], ((0,), (0,)))
+
     own_half = pl.ds(pl.multiple_of(core * HALF, HALF), HALF)
     other_half = pl.ds(pl.multiple_of((1 - core) * HALF, HALF), HALF)
     own_part = pl.ds(pl.multiple_of(core * PHALF, PHALF), PHALF)
@@ -637,8 +640,9 @@
     rows_arrived()
     send_gram(0)
     take_rows()
-    pl.when(high)(lambda: cross(0))
+    pl.when(high)(lambda: cross_half(0, other_half))
     pair_cross(0)
+    pl.when(high)(lambda: cross_half(0, own_half))
     pl.when(high)(lambda: scatter_cross(0))
     send_cross(0)
     own_gram(0)
@@ -646,12 +650,12 @@
     pass_gram(0, True)
     take_gram(0)
     own_change(0)
-    pass_side(0)
     pass_cross(0)
     take_own_cross(0)
     take_pair_cross(0)
     first_ends()
     send_halo(1)
+    pass_side(0)
     first(pl.ds(64, 384))
     pl.when(has_side)(lambda: arrived(cs_in, 0, NXC))
     pl.when(jnp.logical_and(low, has_side))(lambda: cross_turned(0, thi, tlo))
@@ -662,15 +666,16 @@
     images(1)
     gram(1)
     pl.when(high)(lambda: cross(1))
-    drain()
     edges(1)
     send(gp.at[1, other_part], gsib.at[1], 1, GSIB, sibling)
     pl.when(high)(lambda: cross_edges(1))
     pair_cross(1)
     scatter_gram(1)
+    before = len(sent)
     send_gram(1)
     pl.when(high)(lambda: scatter_cross(1))
     send_cross(1)
+    drain(before)
     own_gram(1)
     own_cross(1)
     pass_gram(1, False)

time: 101 us -> 97.1 us (0.961)
  Pallas kernels: 98.9 us -> 95.3 us
    pallas_call x1, Pallas kernels: 98.9 us -> 95.3 us  [per_device(): pl.pallas_call(kernel, out_shape=jax.ShapeDtypeStruct((ROWS, ORBS), F32),...]
where the time goes in v12:
time: 97.1 us; the launch traced here: 96.9 us
  Pallas kernels  95.3 us (98%)
  local copies, waits for them, and re-layouts  1.64 us (2%)
    pallas_call x1, Pallas kernels, per_device(): pl.pallas_call(kernel, out_shape=jax.ShapeDtypeStruct((ROWS, ORBS), F32),...  95.3 us

profile of v12, /device:TPU:25, one launch (start us, length us, event | category | flops | bytes accessed | tf_op | source)
XLA Modules:
  0.0 96.9 jit_solution(5015028040692260164)
XLA Ops:
  0.0 0.0 copy-start.1
  0.0 0.0 copy-start
  0.0 0.7 copy-done.1
  0.7 0.0 copy-done
  0.7 95.3 %shard_map.46 = f32[512,512]{1,0:T(8,128)S(1)} custom-call(f32[512,512]{1,0:T(8,128)} %bitcast.3, bf16[4096,128]{1,0:T(8,128)(2,1)} %metric.1, s32[64]{0:T(128)S(1)} %copy-done, s32[8]{0:T(128)S(1)} %copy-done.1), custom_call_target="tpu_custom_call" | custom-call | tf_op jit(solution)/shard_map/pallas_call | solution.py:713
  95.9 1.0 %copy.6 = f32[1,512,512]{2,1,0:T(8,128)} copy(f32[1,512,512]{2,1,0:T(8,128)S(1)} %bitcast.2) | data formatting | bytes 2097152
Async XLA Ops:
  0.0 0.7 copy-start.1
  0.0 0.7 copy-start

commit v13 on v12

--- a/solution.py
+++ b/solution.py
@@ -312,11 +312,11 @@
                 y = yhi[rows, :].astype(F32) + ylo[rows, :].astype(F32)
                 yhi[rows, :], ylo[rows, :] = split(y + more)
 
-    def cross_edges(it):
+    def cross_edges(it, half):
         ends[0:64, :] = nhi[0:64, :]
         ends[64:128, :] = nhi[448:512, :]
 
-        hp[it] = hp[it] + dot(rhs[0:128, :], ends[...], ((0,), (0,)))
+        hp[it, half, :] = hp[it, half, :] + dot(rhs[0:128, half], ends[...], ((0,), (0,)))
 
     def gram(it):
         for a in range(4):
@@ -578,7 +578,6 @@
             for t in range(4):
                 rows = pl.ds(t * TILE, TILE)
                 x = nq_in[rows, :].astype(jnp.int32).astype(F32) * (CMAX / QMAX)
-                nf[rows, :] = x
                 nhi[rows, :], nlo[rows, :] = split(x)
 
         @pl.when(jnp.logical_not(has_side))
@@ -609,7 +608,7 @@
     def beside(t, rows):
         change = dot3(nhi[rows, :], nlo[rows, :], mhi[...], mlo[...])
         change = change + dot3(chi[0, rows, :], clo[0, rows, :], thi[...], tlo[...])
-        x = jnp.where(live(rows, cs_in), nf[rows, :] - 0.5 * change, 0.0)
+        x = jnp.where(live(rows, cs_in), nq_in[rows, :].astype(jnp.int32).astype(F32) * (CMAX / QMAX) - 0.5 * change, 0.0)
         nhi[rows, :], nlo[rows, :] = split(x)
 
     def ended(cols, change):
@@ -668,8 +667,9 @@
     pl.when(high)(lambda: cross(1))
     edges(1)
     send(gp.at[1, other_part], gsib.at[1], 1, GSIB, sibling)
-    pl.when(high)(lambda: cross_edges(1))
+    pl.when(high)(lambda: cross_edges(1, other_half))
     pair_cross(1)
+    pl.when(high)(lambda: cross_edges(1, own_half))
     scatter_gram(1)
     before = len(sent)
     send_gram(1)

time: 97.1 us -> 97.1 us (level)
  no operation moved by 1% of the time
where the time goes in v13:
time: 97.1 us; the launch traced here: 97 us
  Pallas kernels  95.3 us (98%)
  local copies, waits for them, and re-layouts  1.64 us (2%)
    pallas_call x1, Pallas kernels, per_device(): pl.pallas_call(kernel, out_shape=jax.ShapeDtypeStruct((ROWS, ORBS), F32),...  95.3 us

profile of v13, /device:TPU:25, one launch (start us, length us, event | category | flops | bytes accessed | tf_op | source)
XLA Modules:
  0.0 97.0 jit_solution(17856102031064836013)
XLA Ops:
  0.0 0.0 copy-start.1
  0.0 0.0 copy-start
  0.0 0.7 copy-done.1
  0.7 0.0 copy-done
  0.7 95.3 %shard_map.46 = f32[512,512]{1,0:T(8,128)S(1)} custom-call(f32[512,512]{1,0:T(8,128)} %bitcast.3, bf16[4096,128]{1,0:T(8,128)(2,1)} %metric.1, s32[64]{0:T(128)S(1)} %copy-done, s32[8]{0:T(128)S(1)} %copy-done.1), custom_call_target="tpu_custom_call" | custom-call | tf_op jit(solution)/shard_map/pallas_call | solution.py:713
  96.0 1.0 %copy.6 = f32[1,512,512]{2,1,0:T(8,128)} copy(f32[1,512,512]{2,1,0:T(8,128)S(1)} %bitcast.2) | data formatting | bytes 2097152
Async XLA Ops:
  0.0 0.7 copy-start.1
  0.0 0.7 copy-start
